TPU v7x, 32 devices: a whole 2x2x4 slice. The times are simulated.
32 devices in a mesh: dp: 16 (over z, x, core), ctx: 2 (over y).
Axes of the slice: x: 2, y: 2, z: 4, core: 2. Of those that a mesh axis runs over, the one named last changes fastest.
Arguments:
- tokens: bfloat16 [32768, 896], P(('dp', 'ctx')), may hold values from -6 to 6
- image_starts: int32 [16, 2], P('dp'), may hold values from 0 to 1792
- attn_gain: bfloat16 [896], P(('dp', 'ctx')), may hold values from 0.5 to 1.5
- query_weight: bfloat16 [896, 896], P(('dp', 'ctx')), may hold values from -0.1875 to 0.1875
- query_bias: bfloat16 [896], P(('dp', 'ctx')), may hold values from -3 to 3
- key_weight: bfloat16 [896, 128], P(('dp', 'ctx')), may hold values from -0.1875 to 0.1875
- key_bias: bfloat16 [128], P(('dp', 'ctx')), may hold values from -3 to 3
- value_weight: bfloat16 [896, 128], P(('dp', 'ctx')), may hold values from -0.1875 to 0.1875
- value_bias: bfloat16 [128], P(('dp', 'ctx')), may hold values from -2 to 2
- out_weight: bfloat16 [896, 896], P(('dp', 'ctx')), may hold values from -1.5 to 1.5
- mlp_gain: bfloat16 [896], P(('dp', 'ctx')), may hold values from 0.5 to 1.5
- gate_weight: bfloat16 [896, 4864], P(('dp', 'ctx')), may hold values from -0.1875 to 0.1875
- up_weight: bfloat16 [896, 4864], P(('dp', 'ctx')), may hold values from -0.1875 to 0.1875
- down_weight: bfloat16 [896, 4864], P(('dp', 'ctx')), may hold values from -0.078125 to 0.078125
- cotangent: bfloat16 [32768, 896], P(('dp', 'ctx')), may hold values from -6 to 6
Outputs:
- output: bfloat16 [32768, 896], P(('dp', 'ctx'))
- tokens_grad: bfloat16 [32768, 896], P(('dp', 'ctx'))
- attn_gain_grad: float32 [896], P(('dp', 'ctx'))
- query_weight_grad: float32 [896, 896], P(('dp', 'ctx'))
- query_bias_grad: float32 [896], P(('dp', 'ctx'))
- key_weight_grad: float32 [896, 128], P(('dp', 'ctx'))
- key_bias_grad: float32 [128], P(('dp', 'ctx'))
- value_weight_grad: float32 [896, 128], P(('dp', 'ctx'))
- value_bias_grad: float32 [128], P(('dp', 'ctx'))
- out_weight_grad: float32 [896, 896], P(('dp', 'ctx'))
- mlp_gain_grad: float32 [896], P(('dp', 'ctx'))
- gate_weight_grad: float32 [896, 4864], P(('dp', 'ctx'))
- up_weight_grad: float32 [896, 4864], P(('dp', 'ctx'))
- down_weight_grad: float32 [896, 4864], P(('dp', 'ctx'))
Inputs may be any that keep to these rules, and one draw needn't show every extreme that they name: `image_starts`: row s gives the first positions of the 2 picture pieces of sequence s, each 256 tokens long; pieces may intersect.
All inputs are finite; a program needn't handle non-finite values.
Results may differ from a plain program's by a relative error of at most 0.018.
Values may be sent and summed in bfloat16 or wider, within the bound.
No kernel may reach another device: no remote copies, remote signals or barrier semaphores. Data moves between devices by JAX's collectives and lax.ppermute only.
A program may use at most 320 MiB of HBM per device.

v0:
```python
import jax
import jax.numpy as jnp
from jax import lax
from jax.sharding import PartitionSpec as P

HD = 64
IMG = 256


eps = 1e-06
rope_base = 1000000.0
neg_fill = -1e30


def norm_scaled(values, gain):
    return values * lax.rsqrt(jnp.mean(values * values, axis=-1, keepdims=True) + eps) * gain


def rotate(values, positions):
    count = values.shape[0]
    heads = values.shape[1] // HD
    half_dim = HD // 2
    inverse = rope_base ** (-(jnp.arange(half_dim).astype(jnp.float32) * 2.0 / HD))
    angles = positions.astype(jnp.float32)[:, None] * inverse[None, :]
    cosine = jnp.cos(angles)[:, None, :]
    sine_vals = jnp.sin(angles)[:, None, :]
    shaped = values.reshape(count, heads, 2, half_dim)
    first = shaped[:, :, 0]
    second = shaped[:, :, 1]
    turned_a = first * cosine - second * sine_vals
    turned_b = second * cosine + first * sine_vals
    return jnp.stack([turned_a, turned_b], axis=2).reshape(count, heads * HD)


def visible(query_pos, key_pos, starts_row):
    causal = key_pos[None, :] <= query_pos[:, None]
    query_in = (query_pos[:, None] >= starts_row[None, :]) & (
        query_pos[:, None] < starts_row[None, :] + IMG
    )
    key_in = (key_pos[:, None] >= starts_row[None, :]) & (
        key_pos[:, None] < starts_row[None, :] + IMG
    )
    same_piece = jnp.any(query_in[:, None, :] & key_in[None, :, :], axis=-1)
    return causal | same_piece


def right_dot(left, right):
    return lax.dot_general(
        left, right, (((1,), (1,)), ((), ())), preferred_element_type=jnp.float32
    )


def rows_dot(left, right):
    return lax.dot_general(
        left, right, (((0,), (0,)), ((), ())), preferred_element_type=jnp.float32
    )


def shards(
    tokens,
    image_starts,
    attn_gain,
    query_weight,
    query_bias,
    key_weight,
    key_bias,
    value_weight,
    value_bias,
    out_weight,
    mlp_gain,
    gate_weight,
    up_weight,
    down_weight,
    cotangent,
):
    local_len = tokens.shape[0]
    groups = lax.axis_size("ctx")
    seq_len = local_len * groups
    kv_heads = key_weight.shape[1] // HD
    query_heads = query_weight.shape[1] // HD
    per_group = query_heads // kv_heads
    scale_factor = HD ** (-0.5)
    block_rows = min(local_len, 512)
    blocks = local_len // block_rows
    positions = lax.axis_index("ctx") * local_len + jnp.arange(local_len, dtype=jnp.int32)
    key_positions = jnp.arange(seq_len, dtype=jnp.int32)
    starts_row = image_starts[0]
    attn_full = (
        lax.all_gather(attn_gain, ("dp", "ctx"), axis=0, tiled=True),
        lax.all_gather(query_weight, ("dp", "ctx"), axis=0, tiled=True),
        lax.all_gather(query_bias, ("dp", "ctx"), axis=0, tiled=True),
        lax.all_gather(key_weight, ("dp", "ctx"), axis=0, tiled=True),
        lax.all_gather(key_bias, ("dp", "ctx"), axis=0, tiled=True),
        lax.all_gather(value_weight, ("dp", "ctx"), axis=0, tiled=True),
        lax.all_gather(value_bias, ("dp", "ctx"), axis=0, tiled=True),
        lax.all_gather(out_weight, ("dp", "ctx"), axis=0, tiled=True),
    )
    gain_attn, query_full, query_shift, key_full, key_shift, value_full, value_shift, out_full = (
        attn_full
    )
    residual = tokens.astype(jnp.float32)
    normed_one = norm_scaled(residual, gain_attn.astype(jnp.float32)).astype(jnp.bfloat16)
    query_pre = jnp.dot(
        normed_one, query_full, preferred_element_type=jnp.float32
    ) + query_shift.astype(jnp.float32)
    key_pre = jnp.dot(normed_one, key_full, preferred_element_type=jnp.float32) + key_shift.astype(
        jnp.float32
    )
    value_pre = jnp.dot(
        normed_one, value_full, preferred_element_type=jnp.float32
    ) + value_shift.astype(jnp.float32)
    queries = rotate(query_pre, positions).astype(jnp.bfloat16)
    keys_local = rotate(key_pre, positions).astype(jnp.bfloat16)
    values_local = value_pre.astype(jnp.bfloat16)
    keys_all, values_all = (
        lax.all_gather(keys_local, "ctx", axis=0, tiled=True),
        lax.all_gather(values_local, "ctx", axis=0, tiled=True),
    )
    key_heads = keys_all.reshape(seq_len, kv_heads, HD)
    value_heads = values_all.reshape(seq_len, kv_heads, HD)
    query_blocks = queries.reshape(blocks, block_rows, kv_heads, per_group, HD)
    position_blocks = positions.reshape(blocks, block_rows)

    def forward_block(packed):
        query_block, query_pos = packed
        allowed = visible(query_pos, key_positions, starts_row)
        scores = jnp.einsum(
            "skgd,tkd->kgst", query_block, key_heads, preferred_element_type=jnp.float32
        )
        masked = jnp.where(allowed[None, None], scores * scale_factor, neg_fill)
        top_score = jnp.max(masked, axis=-1, keepdims=True)
        weights = jnp.exp(masked - top_score)
        totals = jnp.sum(weights, axis=-1, keepdims=True)
        probs = (weights / totals).astype(jnp.bfloat16)
        mixed = jnp.einsum("kgst,tkd->skgd", probs, value_heads, preferred_element_type=jnp.float32)
        return (mixed, top_score[..., 0] + jnp.log(totals[..., 0]))

    mixed_blocks, logsum = lax.map(forward_block, (query_blocks, position_blocks))
    attended = mixed_blocks.reshape(local_len, query_heads * HD).astype(jnp.bfloat16)
    hidden_one = residual + right_dot(attended, out_full)
    mlp_full = (
        lax.all_gather(mlp_gain, ("dp", "ctx"), axis=0, tiled=True),
        lax.all_gather(gate_weight, ("dp", "ctx"), axis=0, tiled=True),
        lax.all_gather(up_weight, ("dp", "ctx"), axis=0, tiled=True),
        lax.all_gather(down_weight, ("dp", "ctx"), axis=0, tiled=True),
    )
    gain_mlp, gate_full, up_full, down_full = mlp_full
    normed_two = norm_scaled(hidden_one, gain_mlp.astype(jnp.float32)).astype(jnp.bfloat16)
    gate_vals = jnp.dot(normed_two, gate_full, preferred_element_type=jnp.float32)
    up_vals = jnp.dot(normed_two, up_full, preferred_element_type=jnp.float32)
    activated = (jax.nn.silu(gate_vals) * up_vals).astype(jnp.bfloat16)
    output = (hidden_one + right_dot(activated, down_full)).astype(jnp.bfloat16)
    attn_back = (
        lax.all_gather(attn_gain, ("dp", "ctx"), axis=0, tiled=True),
        lax.all_gather(query_weight, ("dp", "ctx"), axis=0, tiled=True),
        lax.all_gather(query_bias, ("dp", "ctx"), axis=0, tiled=True),
        lax.all_gather(key_weight, ("dp", "ctx"), axis=0, tiled=True),
        lax.all_gather(key_bias, ("dp", "ctx"), axis=0, tiled=True),
        lax.all_gather(value_weight, ("dp", "ctx"), axis=0, tiled=True),
        lax.all_gather(value_bias, ("dp", "ctx"), axis=0, tiled=True),
        lax.all_gather(out_weight, ("dp", "ctx"), axis=0, tiled=True),
    )
    mlp_back = (
        lax.all_gather(mlp_gain, ("dp", "ctx"), axis=0, tiled=True),
        lax.all_gather(gate_weight, ("dp", "ctx"), axis=0, tiled=True),
        lax.all_gather(up_weight, ("dp", "ctx"), axis=0, tiled=True),
        lax.all_gather(down_weight, ("dp", "ctx"), axis=0, tiled=True),
    )
    (
        gain_attn_back,
        query_back,
        query_shift_back,
        key_back,
        key_shift_back,
        value_back,
        value_shift_back,
        out_back,
    ) = attn_back
    gain_mlp_back, gate_back, up_back, down_back = mlp_back
    grad_out = cotangent.astype(jnp.float32)
    grad_act = jnp.dot(cotangent, down_back, preferred_element_type=jnp.float32)
    silu_unused, silu_pull = jax.vjp(
        lambda gate_in, up_in: jax.nn.silu(gate_in) * up_in, gate_vals, up_vals
    )
    grad_gate, grad_up = silu_pull(grad_act)
    gate_low = grad_gate.astype(jnp.bfloat16)
    up_low = grad_up.astype(jnp.bfloat16)
    grad_normed_two = right_dot(gate_low, gate_back) + right_dot(up_low, up_back)
    norm_unused, norm_pull = jax.vjp(norm_scaled, hidden_one, gain_mlp_back.astype(jnp.float32))
    grad_hidden_part, grad_gain_mlp = norm_pull(grad_normed_two)
    grad_hidden = grad_out + grad_hidden_part
    gate_term = rows_dot(normed_two, gate_low)
    up_term = rows_dot(normed_two, up_low)
    down_term = rows_dot(cotangent, activated)
    mlp_grads = (
        lax.psum_scatter(grad_gain_mlp, ("dp", "ctx"), scatter_dimension=0, tiled=True),
        lax.psum_scatter(gate_term, ("dp", "ctx"), scatter_dimension=0, tiled=True),
        lax.psum_scatter(up_term, ("dp", "ctx"), scatter_dimension=0, tiled=True),
        lax.psum_scatter(down_term, ("dp", "ctx"), scatter_dimension=0, tiled=True),
    )
    grad_attn_low = grad_hidden.astype(jnp.bfloat16)
    grad_attended = jnp.dot(grad_attn_low, out_back, preferred_element_type=jnp.float32)
    grad_blocks = grad_attended.astype(jnp.bfloat16).reshape(
        blocks, block_rows, kv_heads, per_group, HD
    )

    def backward_block(carry, packed):
        key_acc, value_acc = carry
        query_block, query_pos, grad_block, logsum_block = packed
        allowed = visible(query_pos, key_positions, starts_row)
        scores = jnp.einsum(
            "skgd,tkd->kgst", query_block, key_heads, preferred_element_type=jnp.float32
        )
        shifted = jnp.where(
            allowed[None, None], scores * scale_factor - logsum_block[..., None], neg_fill
        )
        probs = jnp.exp(shifted)
        grad_probs = jnp.einsum(
            "skgd,tkd->kgst", grad_block, value_heads, preferred_element_type=jnp.float32
        )
        inner_sum = jnp.sum(grad_probs * probs, axis=-1, keepdims=True)
        grad_scores = (probs * (grad_probs - inner_sum) * scale_factor).astype(jnp.bfloat16)
        grad_query = jnp.einsum(
            "kgst,tkd->skgd", grad_scores, key_heads, preferred_element_type=jnp.float32
        )
        key_acc = key_acc + jnp.einsum(
            "kgst,skgd->tkd", grad_scores, query_block, preferred_element_type=jnp.float32
        )
        value_acc = value_acc + jnp.einsum(
            "kgst,skgd->tkd",
            probs.astype(jnp.bfloat16),
            grad_block,
            preferred_element_type=jnp.float32,
        )
        return ((key_acc, value_acc), grad_query)

    zeros_kv = jnp.zeros((seq_len, kv_heads, HD), jnp.float32)
    (key_grad_all, value_grad_all), grad_query_blocks = lax.scan(
        backward_block, (zeros_kv, zeros_kv), (query_blocks, position_blocks, grad_blocks, logsum)
    )
    key_grad_sum, value_grad_sum = (
        lax.psum_scatter(
            key_grad_all.reshape(seq_len, kv_heads * HD), "ctx", scatter_dimension=0, tiled=True
        ),
        lax.psum_scatter(
            value_grad_all.reshape(seq_len, kv_heads * HD), "ctx", scatter_dimension=0, tiled=True
        ),
    )
    query_low = rotate(grad_query_blocks.reshape(local_len, query_heads * HD), -positions).astype(
        jnp.bfloat16
    )
    key_low = rotate(key_grad_sum, -positions).astype(jnp.bfloat16)
    value_low = value_grad_sum.astype(jnp.bfloat16)
    grad_normed_one = (
        right_dot(query_low, query_back)
        + right_dot(key_low, key_back)
        + right_dot(value_low, value_back)
    )
    norm_unused_one, norm_pull_one = jax.vjp(
        norm_scaled, residual, gain_attn_back.astype(jnp.float32)
    )
    grad_resid_part, grad_gain_attn = norm_pull_one(grad_normed_one)
    tokens_grad = (grad_hidden + grad_resid_part).astype(jnp.bfloat16)
    query_bias_term = jnp.sum(query_low.astype(jnp.float32), axis=0)
    key_bias_term = jnp.sum(key_low.astype(jnp.float32), axis=0)
    value_bias_term = jnp.sum(value_low.astype(jnp.float32), axis=0)
    query_term = rows_dot(normed_one, query_low)
    key_term = rows_dot(normed_one, key_low)
    value_term = rows_dot(normed_one, value_low)
    out_term = rows_dot(grad_attn_low, attended)
    attn_grads = (
        lax.psum_scatter(grad_gain_attn, ("dp", "ctx"), scatter_dimension=0, tiled=True),
        lax.psum_scatter(query_term, ("dp", "ctx"), scatter_dimension=0, tiled=True),
        lax.psum_scatter(query_bias_term, ("dp", "ctx"), scatter_dimension=0, tiled=True),
        lax.psum_scatter(key_term, ("dp", "ctx"), scatter_dimension=0, tiled=True),
        lax.psum_scatter(key_bias_term, ("dp", "ctx"), scatter_dimension=0, tiled=True),
        lax.psum_scatter(value_term, ("dp", "ctx"), scatter_dimension=0, tiled=True),
        lax.psum_scatter(value_bias_term, ("dp", "ctx"), scatter_dimension=0, tiled=True),
        lax.psum_scatter(out_term, ("dp", "ctx"), scatter_dimension=0, tiled=True),
    )
    return (
        output,
        tokens_grad,
        attn_grads[0],
        attn_grads[1],
        attn_grads[2],
        attn_grads[3],
        attn_grads[4],
        attn_grads[5],
        attn_grads[6],
        attn_grads[7],
        mlp_grads[0],
        mlp_grads[1],
        mlp_grads[2],
        mlp_grads[3],
    )


def solution(mesh):
    placed = (
        P(("dp", "ctx"), None),
        P("dp", None),
        P(("dp", "ctx")),
        P(("dp", "ctx"), None),
        P(("dp", "ctx")),
        P(("dp", "ctx"), None),
        P(("dp", "ctx")),
        P(("dp", "ctx"), None),
        P(("dp", "ctx")),
        P(("dp", "ctx"), None),
        P(("dp", "ctx")),
        P(("dp", "ctx"), None),
        P(("dp", "ctx"), None),
        P(("dp", "ctx"), None),
        P(("dp", "ctx"), None),
    )
    return jax.shard_map(
        shards,
        mesh=mesh,
        in_specs=placed,
        out_specs=(
            P(("dp", "ctx"), None),
            P(("dp", "ctx"), None),
            P(("dp", "ctx")),
            P(("dp", "ctx"), None),
            P(("dp", "ctx")),
            P(("dp", "ctx"), None),
            P(("dp", "ctx")),
            P(("dp", "ctx"), None),
            P(("dp", "ctx")),
            P(("dp", "ctx"), None),
            P(("dp", "ctx")),
            P(("dp", "ctx"), None),
            P(("dp", "ctx"), None),
            P(("dp", "ctx"), None),
        ),
        check_vma=False,
    )
```

profile of v0, /device:TPU:9, one launch (start us, length us, event | category | flops | bytes accessed | tf_op | source)
XLA Modules:
  0.0 2470.7 jit_solution(15662376206883601390)
XLA Ops:
  15.0 40.1 %all-reduce.24 = (bf16[896]{0:T(1024)(128)(2,1)S(1)}, bf16[896]{0:T(1024)(128)(2,1)S(1)}, bf16[128]{0:T(256)(128)(2,1)S(1)}, bf16[128]{0:T(256)(128)(2,1)S(1)}, bf16[896]{0:T(1024)(128)(2,1)S(1)}) all-reduce(bf16[896]{0:T(1024)(128)(2,1)S(1)} %dynamic-update-slice.1, ...), channel_id=1, replica_groups=mesh['dp'=16,'ctx'=2] {'dp','ctx'}, use_global_device_ids=true, to_apply=%add.1 | all-reduce | flops 2944 | bytes 11776
  58.5 52.5 %all-gather.1 = bf16[32,28,128]{2,1,0:T(8,128)(2,1)S(1)} all-gather(bf16[1,28,128]{2,1,0:T(8,128)(2,1)S(1)} %bitcast.284), channel_id=1, replica_groups=mesh['dp'=16,'ctx'=2] {'dp','ctx'}, dimensions={0}, use_global_device_ids=true | all-gather | bytes 236544 | tf_op jit(solution)/shard_map/all_gather | solution.py:92
  114.0 6.2 all_gather.56
  120.2 68.0 %all-gather.2 = bf16[32,28,128]{2,1,0:T(8,128)(2,1)S(1)} all-gather(bf16[1,28,128]{2,1,0:T(8,128)(2,1)S(1)} %bitcast.285), channel_id=1, replica_groups=mesh['dp'=16,'ctx'=2] {'dp','ctx'}, dimensions={0}, use_global_device_ids=true | all-gather | bytes 236544 | tf_op jit(solution)/shard_map/all_gather | solution.py:94
  191.2 12.0 all_gather.59
  221.6 138.1 %while.30 = (s32[]{:T(128)}, bf16[2,512,2,7,64]{1,4,3,2,0:T(8,128)(2,1)}, f32[2,2,7,512]{3,2,1,0:T(8,128)S(1)}, s32[2,512]{1,0:T(2,128)S(1)}, s32[1,2]{1,0:T(1,1...) while((s32[]{:T(128)}, ...), condition=%wide.region_5.6_spmd.clone.clone, body=%wide.region_1.5_spmd.clone.clone.sunk | while | flops 3939508224 | bytes 186513584 | solution.py:138
  223.8 22.4 bitcast_reduce_fusion.2
  246.2 19.9 fusion.155
  266.1 24.9 %bitcast_dynamic-update-slice_fusion.4 = bf16[2,512,2,7,64]{1,4,3,2,0:T(8,128)(2,1)} fusion(bf16[2,512,2,7,64]{1,4,3,2,0:T(8,128)(2,1)} %get-tuple-element.606, s32[]{:T(128)S(6)} %copy.140, f32[2,512,7,2048]{3,1,2,0:T(8,128)} %get-tuple-element.583, f32[2,7,512]{2,1,0:T(8,128)S(1)} %fusion.155, f32[2,7,512]{2,1,0:T(8,128)S(1)} %get-tuple-element.584, ...), kind=kOutput, calls=%fused_computation.12.clone.1 | convolution fusion | flops 1952448512 | bytes 62185476 | tf_op jit(solution)/shard_map/while/body/eval_jaxpr/kgst,tkd->skgd/dot_general | solution.py:135
  293.1 22.8 bitcast_reduce_fusion.2
  315.8 19.7 fusion.155
  335.5 23.7 bitcast_dynamic-update-slice_fusion.4
  367.6 4.2 multiply_reduce_fusion.2
  374.1 13.5 reshape.555
  387.6 12.9 reshape.557
  400.5 17.4 fusion.87
  417.9 13.9 fusion.88
  431.8 13.1 reshape.559
  444.9 30.3 %multiply_convert_fusion = (bf16[1024,4864]{1,0:T(8,128)(2,1)}, bf16[1024,4864]{1,0:T(8,128)(2,1)}, bf16[1024,4864]{1,0:T(8,128)(2,1)}) fusion(f32[1024,4864]{1,0:T(8,128)} %fusion.87, f32[1024,4864]{1,0:T(8,128)} %fusion.88, bf16[1024,896]{1,0:T(8,128)(2,1)S(1)} %copy-done.20, bf16[896,4864]{1,0:T(8,128)(2,1)} %reshape.559), kind=kOutput, calls=%fused_computation.77 | convolution fusion | flops 9005170688 | bytes 80281600 | tf_op jit(solution)/shard_map/dot_general | solution.py:181
  475.1 15.8 fusion.89
  490.9 15.8 fusion.92
  506.8 13.8 multiply_reduce_fusion
  529.9 5.4 copy.91
  535.4 499.7 %while.31 = (s32[]{:T(128)}, f32[2048,2,64]{0,2,1:T(8,128)}, f32[2048,2,64]{0,2,1:T(8,128)S(1)}, f32[2,512,2,7,64]{1,0,4,3,2:T(2,128)}, bf16[2,512,2,7,64]{1,4,3...) while((s32[]{:T(128)}, f32[2048,2,64]{0,2,1:T(8,128)}, ...), condition=%wide.region_11.12_spmd.clone.clone, body=%wide.region_8.11_spmd.clone.clone.sunk | while | flops 9607087104 | bytes 551393536 | solution.py:238
  537.8 23.2 fusion.165
  561.0 23.7 fusion.166
  584.7 72.3 %fusion.167 = f32[2048,2,64]{0,2,1:T(8,128)} fusion(f32[2,7,512,2048]{3,2,1,0:T(8,128)} %fusion.165, f32[2,512,7,2048]{3,1,2,0:T(8,128)} %fusion.166, f32[2048,2,64]{0,2,1:T(8,128)} %get-tuple-element.637, bf16[2,512,2,7,64]{1,4,3,2,0:T(8,128)(2,1)} %get-tuple-element.653, s32[]{:T(128)S(6)} %copy.150, pred[]{:T(512)S(6)} %compare.3), kind=kOutput, calls=%fused_computation.45.clone.2 | convolution fusion | flops 1952982016 | bytes 237895680 | tf_op jit(solution)/shard_map/while/body/eval_jaxpr/kgst,skgd->tkd/dot_general | solution.py:226
  657.0 19.7 fusion.168
  676.7 71.7 %fusion.169 = f32[1,512,2,7,64]{1,4,3,2,0:T(8,128)} fusion(f32[2,7,512,2048]{3,2,1,0:T(8,128)} %fusion.165, f32[2,512,7,2048]{3,1,2,0:T(8,128)} %fusion.166, bf16[2048,2,64]{0,2,1:T(8,128)(2,1)} %get-tuple-element.656), kind=kOutput, calls=%fused_computation.47.clone.1 | convolution fusion | flops 1952457728 | bytes 119799808 | tf_op jit(solution)/shard_map/while/body/eval_jaxpr/kgst,tkd->skgd/dot_general | solution.py:223
  751.8 33.4 %dynamic_update_slice.24 = f32[2,512,2,7,64]{1,0,4,3,2:T(2,128)} dynamic-update-slice(f32[2,512,2,7,64]{1,0,4,3,2:T(2,128)} %get-tuple-element.639, f32[1,512,2,7,64]{1,0,4,3,2:T(1,128)S(1)} %copy.128, s32[]{:T(128)S(6)} %copy.150, s32[]{:T(128)} %constant.72.clone.1..sunk, s32[]{:T(128)} %constant.72.clone.1..sunk, s32[]{:T(128)} %constant.72.clone.1..sunk, s32[]{:T(128)} %constant.72.clone.1..sunk) | dynamic-update-slice | bytes 3670020 | tf_op jit(solution)/shard_map/while/body/jit(dynamic_update_index_in_dim)/dynamic_update_slice | solution.py:138
  787.2 23.2 fusion.165
  810.4 23.7 fusion.166
  834.1 72.5 %fusion.167 = f32[2048,2,64]{0,2,1:T(8,128)} fusion(f32[2,7,512,2048]{3,2,1,0:T(8,128)} %fusion.165, f32[2,512,7,2048]{3,1,2,0:T(8,128)} %fusion.166, f32[2048,2,64]{0,2,1:T(8,128)} %get-tuple-element.637, bf16[2,512,2,7,64]{1,4,3,2,0:T(8,128)(2,1)} %get-tuple-element.653, s32[]{:T(128)S(6)} %copy.150, pred[]{:T(512)S(6)} %compare.3), kind=kOutput, calls=%fused_computation.45.clone.2 | convolution fusion | flops 1952982016 | bytes 237895680 | tf_op jit(solution)/shard_map/while/body/eval_jaxpr/kgst,skgd->tkd/dot_general | solution.py:226
  906.6 19.7 fusion.168
  926.3 71.7 %fusion.169 = f32[1,512,2,7,64]{1,4,3,2,0:T(8,128)} fusion(f32[2,7,512,2048]{3,2,1,0:T(8,128)} %fusion.165, f32[2,512,7,2048]{3,1,2,0:T(8,128)} %fusion.166, bf16[2048,2,64]{0,2,1:T(8,128)(2,1)} %get-tuple-element.656), kind=kOutput, calls=%fused_computation.47.clone.1 | convolution fusion | flops 1952457728 | bytes 119799808 | tf_op jit(solution)/shard_map/while/body/eval_jaxpr/kgst,tkd->skgd/dot_general | solution.py:223
  1001.5 33.4 %dynamic_update_slice.24 = f32[2,512,2,7,64]{1,0,4,3,2:T(2,128)} dynamic-update-slice(f32[2,512,2,7,64]{1,0,4,3,2:T(2,128)} %get-tuple-element.639, f32[1,512,2,7,64]{1,0,4,3,2:T(1,128)S(1)} %copy.128, s32[]{:T(128)S(6)} %copy.150, s32[]{:T(128)} %constant.72.clone.1..sunk, s32[]{:T(128)} %constant.72.clone.1..sunk, s32[]{:T(128)} %constant.72.clone.1..sunk, s32[]{:T(128)} %constant.72.clone.1..sunk) | dynamic-update-slice | bytes 3670020 | tf_op jit(solution)/shard_map/while/body/jit(dynamic_update_index_in_dim)/dynamic_update_slice | solution.py:138
  1035.0 6.4 reshape_reshape.3
  1041.5 15.6 fusion.93
  1061.5 16.6 convolution_bitcast_fusion
  1079.6 5.7 fusion.90
  1096.4 1114.5 %fusion.86 = (f32[32,896]{1,0:T(8,128)}, f32[32,128]{1,0:T(8,128)S(1)}, f32[32,128]{1,0:T(8,128)S(1)}, f32[32,896]{1,0:T(8,128)S(1)}, f32[32,4864]{1,0:T(8,128)S(1)}, /*index=5*/f32[32,4864]{1,0:T(8,128)S(1)}) fusion(f32[896,896]{1,0:T(8,128)} %fusion.90, f32[896,128]{1,0:T(8,128)} %fusion.91, f32[896,128]{1,0:T(8,128)} %fusion.83, f32[896,896]{1,0:T(8,128)} %fusion.77, ...), kind=kCustom, calls=%all-reduce-scatter.6 | all-reduce-scatter fusion | flops 12058625 | bytes 43712512
  2213.5 15.1 add_convert_fusion
  2239.0 10.7 collective-permute-start.10
  2293.9 9.8 collective-permute-done.13
  2303.7 8.9 collective-permute-start.16
  2333.4 65.8 %all-reduce.23 = (f32[896]{0:T(1024)S(1)}, f32[896]{0:T(1024)S(1)}, f32[128]{0:T(128)S(1)}, f32[128]{0:T(128)S(1)}, f32[896]{0:T(1024)S(1)}) all-reduce(f32[896]{0:T(1024)S(1)} %get-tuple-element.385, f32[896]{0:T(1024)S(1)} %reduce_sum.115, f32[128]{0:T(128)S(1)} %reduce_sum.120, ...), channel_id=4, replica_groups=mesh['dp'=16,'ctx'=2] {'dp','ctx'}, use_global_device_ids=true, to_apply=%region_16.17.clone | all-reduce | flops 2944 | bytes 23552
  2414.8 19.8 concatenate.4
  2434.6 20.2 concatenate.5
  (331 shorter events, 187.9 us)
Async XLA Ops:
  7.2 51.3 %copy-start.64 = (bf16[28,128]{1,0:T(8,128)(2,1)S(1)}, bf16[28,128]{1,0:T(8,128)(2,1)}, u32[]{:S(2)}) copy-start(bf16[28,128]{1,0:T(8,128)(2,1)} %param.24) | copy-start | bytes 21508
  7.2 200.8 %all-gather.13.cloned.1.call-start = ((), (), s32[]{:S(2)}) async-start(), calls=%async_computation.4 | async-start | bytes 1892352 | tf_op jit(solution)/shard_map/all_gather | solution.py:90
  7.9 357.2 %all-gather.15.cloned.1.call-start = ((), (), s32[]{:S(2)}) async-start(), calls=%async_computation.5 | async-start | bytes 1892352 | tf_op jit(solution)/shard_map/all_gather | solution.py:96
  8.7 365.4 %all-gather.17.cloned.1.call-start = ((), (), s32[]{:S(2)}) async-start(), calls=%async_computation.6 | async-start | bytes 10272768 | tf_op jit(solution)/shard_map/all_gather | solution.py:143
  9.4 378.2 %all-gather.19.cloned.1.call-start = ((), (), s32[]{:S(2)}) async-start(), calls=%async_computation.7 | async-start | bytes 10272768 | tf_op jit(solution)/shard_map/all_gather | solution.py:144
  10.0 421.8 %all-gather.21.cloned.1.call-start = ((), (), s32[]{:S(2)}) async-start(), calls=%async_computation.8 | async-start | bytes 10272768 | tf_op jit(solution)/shard_map/all_gather | solution.py:145
  10.6 1078.5 %reduce-scatter.16.cloned.1.call-start = ((), (), s32[]{:S(2)}) async-start(), calls=%async_computation.2 | async-start | bytes 1572864 | tf_op jit(solution)/shard_map/reduce_scatter | solution.py:242
  58.0 55.8 %copy-start.2 = (bf16[1024,896]{0,1:T(8,128)(2,1)}, bf16[1024,896]{0,1:T(8,128)(2,1)S(1)}, u32[]{:S(2)}) copy-start(bf16[1024,896]{0,1:T(8,128)(2,1)S(1)} %copy.81) | copy-start | bytes 5505028
  58.0 55.8 %copy-start.53 = (f32[896]{0:T(1024)}, f32[896]{0:T(1024)S(1)}, u32[]{:S(2)}) copy-start(f32[896]{0:T(1024)S(1)} %convert_element_type.134) | copy-start | bytes 10756
  58.5 55.4 %copy-start.58 = (f32[1024]{0:T(1024)}, f32[1024]{0:T(1024)S(1)}, u32[]{:S(2)}) copy-start(f32[1024]{0:T(1024)S(1)} %fusion.74) | copy-start | bytes 12292
  58.5 55.4 %copy-start.55 = (f32[1024]{0:T(1024)}, f32[1024]{0:T(1024)S(1)}, u32[]{:S(2)}) copy-start(f32[1024]{0:T(1024)S(1)} %fusion.81) | copy-start | bytes 12292
  374.0 43.8 %copy-start.24 = (bf16[1024,896]{0,1:T(8,128)(2,1)}, bf16[1024,896]{0,1:T(8,128)(2,1)S(1)}, u32[]{:S(2)}) copy-start(bf16[1024,896]{0,1:T(8,128)(2,1)S(1)} %multiply_convert_fusion.2) | copy-start | bytes 5505028
  1041.4 52.5 %reduce-scatter.18.cloned.1.call-start = ((), (), s32[]{:S(2)}) async-start(), calls=%async_computation.3 | async-start | bytes 1572864 | tf_op jit(solution)/shard_map/reduce_scatter | solution.py:245
  1057.1 1401.7 %all-reduce.28.cloned.1.call-start = ((), (), s32[]{:S(2)}) async-start(), calls=%async_computation.9 | async-start | bytes 34865152
  2210.9 40.9 %copy-start.23 = (bf16[1024,14,2,32]{0,3,2,1:T(8,128)(2,1)S(1)}, bf16[1024,14,2,32]{0,3,2,1:T(8,128)(2,1)}, u32[]{:S(2)}) copy-start(bf16[1024,14,2,32]{0,3,2,1:T(8,128)(2,1)} %get-tuple-element.450) | copy-start | bytes 5505028
  2210.9 40.9 %copy-start.27 = (bf16[896,896]{1,0:T(8,128)(2,1)S(1)}, bf16[896,896]{1,0:T(8,128)(2,1)}, u32[]{:S(2)}) copy-start(bf16[896,896]{1,0:T(8,128)(2,1)} %reshape.547) | copy-start | bytes 4816900
  2210.9 38.8 %collective-permute-start.7 = (f32[28,128]{1,0:T(8,128)S(1)}, f32[28,128]{1,0:T(8,128)S(1)}, u32[]{:S(2)}, u32[]{:S(2)}) collective-permute-start(f32[28,128]{1,0:T(8,128)S(1)} %slice.41), channel_id=1, source_target_pairs={{0,4},{1,5},{2,6},{3,7},{4,8},{5,9},{6,10},{7,11},{8,12},{9,13},{1... | collective-permute-start | bytes 43016
  2228.6 33.0 %collective-permute-start.6 = (f32[32,128]{1,0:T(8,128)S(1)}, f32[32,128]{1,0:T(8,128)S(1)}, u32[]{:S(2)}, u32[]{:S(2)}) collective-permute-start(f32[32,128]{1,0:T(8,128)S(1)} %get-tuple-element.442), channel_id=1, source_target_pairs={{0,3},{1,4},{2,5},{3,6},{4,7},{5,8},{6,9},{7,10},{8,11},{9,12},{10... | collective-permute-start | bytes 49160
  2232.3 31.2 %collective-permute-start.5 = (f32[32,128]{1,0:T(8,128)S(1)}, f32[32,128]{1,0:T(8,128)}, u32[]{:S(2)}, u32[]{:S(2)}) collective-permute-start(f32[32,128]{1,0:T(8,128)S(1)} %get-tuple-element.442), channel_id=1, source_target_pairs={{0,2},{1,3},{2,4},{3,5},{4,6},{5,7},{6,8},{7,9},{8,10},{9,11},{10,... | collective-permute-start | bytes 49160
  2236.4 30.4 %collective-permute-start.4 = (f32[32,128]{1,0:T(8,128)S(1)}, f32[32,128]{1,0:T(8,128)}, u32[]{:S(2)}, u32[]{:S(2)}) collective-permute-start(f32[32,128]{1,0:T(8,128)S(1)} %get-tuple-element.442), channel_id=1, source_target_pairs={{0,1},{1,2},{2,3},{3,4},{4,5},{5,6},{6,7},{7,8},{8,9},{9,10},{10,1... | collective-permute-start | bytes 49160
  2239.0 29.8 %collective-permute-start.10 = (f32[32,128]{1,0:T(8,128)S(1)}, f32[32,128]{1,0:T(8,128)}, u32[]{:S(2)}, u32[]{:S(2)}) collective-permute-start(f32[32,128]{1,0:T(8,128)S(1)} %get-tuple-element.443), channel_id=1, source_target_pairs={{0,3},{1,4},{2,5},{3,6},{4,7},{5,8},{6,9},{7,10},{8,11},{9,12},{10... | collective-permute-start | bytes 49160
  2249.6 9.6 collective-permute-start.11
  2259.3 22.7 collective-permute-start.2
  2261.6 10.8 collective-permute-start.9
  2263.5 11.3 collective-permute-start.8
  2266.8 10.0 collective-permute-start.3
  2268.8 11.1 collective-permute-start.15
  2272.3 51.9 %copy-start.12 = (f32[1024,896]{0,1:T(8,128)S(1)}, f32[1024,896]{0,1:T(8,128)}, u32[]{:S(2)}) copy-start(f32[1024,896]{0,1:T(8,128)} %copy-done.10) | copy-start | bytes 11010052
  2272.4 15.1 collective-permute-start.1
  2274.8 14.6 collective-permute-start
  2276.9 14.8 collective-permute-start.14
  2279.9 39.4 %collective-permute-start.18 = (f32[32,4864]{1,0:T(8,128)S(1)}, f32[32,4864]{1,0:T(8,128)S(1)}, u32[]{:S(2)}, u32[]{:S(2)}) collective-permute-start(f32[32,4864]{1,0:T(8,128)S(1)} %get-tuple-element.445), channel_id=1, source_target_pairs={{0,3},{1,4},{2,5},{3,6},{4,7},{5,8},{6,9},{7,10},{8,11},{9,12},{10... | collective-permute-start | bytes 1867784
  2282.0 34.8 %collective-permute-start.19 = (f32[28,4864]{1,0:T(8,128)S(1)}, f32[28,4864]{1,0:T(8,128)S(1)}, u32[]{:S(2)}, u32[]{:S(2)}) collective-permute-start(f32[28,4864]{1,0:T(8,128)S(1)} %slice.44), channel_id=1, source_target_pairs={{0,4},{1,5},{2,6},{3,7},{4,8},{5,9},{6,10},{7,11},{8,12},{9,13},{1... | collective-permute-start | bytes 1634312
  2287.5 36.7 %copy-start.47 = (f32[32,896]{1,0:T(8,128)}, f32[32,896]{1,0:T(8,128)S(1)}, u32[]{:S(2)}) copy-start(f32[32,896]{1,0:T(8,128)S(1)} %collective-permute-done.1) | copy-start | bytes 344068
  2287.5 16.2 collective-permute-start.13
  2289.4 112.2 %copy-start.49 = (f32[32,896]{1,0:T(8,128)}, f32[32,896]{1,0:T(8,128)S(1)}, u32[]{:S(2)}) copy-start(f32[32,896]{1,0:T(8,128)S(1)} %collective-permute-done) | copy-start | bytes 344068
  2289.4 23.2 collective-permute-start.12
  2291.7 39.7 %collective-permute-start.17 = (f32[32,4864]{1,0:T(8,128)S(1)}, f32[32,4864]{1,0:T(8,128)}, u32[]{:S(2)}, u32[]{:S(2)}) collective-permute-start(f32[32,4864]{1,0:T(8,128)S(1)} %get-tuple-element.445), channel_id=1, source_target_pairs={{0,2},{1,3},{2,4},{3,5},{4,6},{5,7},{6,8},{7,9},{8,10},{9,11},{10,... | collective-permute-start | bytes 1867784
  2303.7 111.1 %collective-permute-start.16 = (f32[32,4864]{1,0:T(8,128)S(1)}, f32[32,4864]{1,0:T(8,128)}, u32[]{:S(2)}, u32[]{:S(2)}) collective-permute-start(f32[32,4864]{1,0:T(8,128)S(1)} %get-tuple-element.445), channel_id=1, source_target_pairs={{0,1},{1,2},{2,3},{3,4},{4,5},{5,6},{6,7},{7,8},{8,9},{9,10},{10,1... | collective-permute-start | bytes 1867784
  2312.6 121.9 %collective-permute-start.22 = (f32[32,4864]{1,0:T(8,128)S(1)}, f32[32,4864]{1,0:T(8,128)}, u32[]{:S(2)}, u32[]{:S(2)}) collective-permute-start(f32[32,4864]{1,0:T(8,128)S(1)} %get-tuple-element.446), channel_id=1, source_target_pairs={{0,3},{1,4},{2,5},{3,6},{4,7},{5,8},{6,9},{7,10},{8,11},{9,12},{10... | collective-permute-start | bytes 1867784
  2316.8 117.8 %collective-permute-start.21 = (f32[32,4864]{1,0:T(8,128)S(1)}, f32[32,4864]{1,0:T(8,128)}, u32[]{:S(2)}, u32[]{:S(2)}) collective-permute-start(f32[32,4864]{1,0:T(8,128)S(1)} %get-tuple-element.446), channel_id=1, source_target_pairs={{0,2},{1,3},{2,4},{3,5},{4,6},{5,7},{6,8},{7,9},{8,10},{9,11},{10,... | collective-permute-start | bytes 1867784
  2320.1 114.5 %collective-permute-start.20 = (f32[32,4864]{1,0:T(8,128)S(1)}, f32[32,4864]{1,0:T(8,128)}, u32[]{:S(2)}, u32[]{:S(2)}) collective-permute-start(f32[32,4864]{1,0:T(8,128)S(1)} %get-tuple-element.446), channel_id=1, source_target_pairs={{0,1},{1,2},{2,3},{3,4},{4,5},{5,6},{6,7},{7,8},{8,9},{9,10},{10,1... | collective-permute-start | bytes 1867784
  2326.5 77.5 %copy-start.61 = (f32[32,128]{1,0:T(8,128)S(1)}, f32[32,128]{1,0:T(8,128)}, u32[]{:S(2)}) copy-start(f32[32,128]{1,0:T(8,128)} %copy-done.60) | copy-start | bytes 49156
  2326.5 80.6 %copy-start.33 = (f32[32,896]{1,0:T(8,128)S(1)}, f32[32,896]{1,0:T(8,128)}, u32[]{:S(2)}) copy-start(f32[32,896]{1,0:T(8,128)} %get-tuple-element.441) | copy-start | bytes 344068
  2326.5 80.6 %copy-start.46 = (f32[28,896]{1,0:T(8,128)S(1)}, f32[28,896]{1,0:T(8,128)}, u32[]{:S(2)}) copy-start(f32[28,896]{1,0:T(8,128)} %copy-done.45) | copy-start | bytes 301060
  2326.5 80.6 %copy-start.48 = (f32[32,896]{1,0:T(8,128)S(1)}, f32[32,896]{1,0:T(8,128)}, u32[]{:S(2)}) copy-start(f32[32,896]{1,0:T(8,128)} %copy-done.47) | copy-start | bytes 344068
  2327.4 87.4 %copy-start.37 = (f32[32,4864]{1,0:T(8,128)S(1)}, f32[32,4864]{1,0:T(8,128)}, u32[]{:S(2)}) copy-start(f32[32,4864]{1,0:T(8,128)} %copy-done.36) | copy-start | bytes 1867780
  2331.4 103.2 %collective-permute-start.23 = (f32[28,4864]{1,0:T(8,128)}, f32[28,4864]{1,0:T(8,128)}, u32[]{:S(2)}, u32[]{:S(2)}) collective-permute-start(f32[28,4864]{1,0:T(8,128)} %slice.45), channel_id=1, source_target_pairs={{0,4},{1,5},{2,6},{3,7},{4,8},{5,9},{6,10},{7,11},{8,12},{9,13},{1... | collective-permute-start | bytes 1634312
  (54 other events, 583.4 us)
Sparse Core Ops, SparseCore 0:
  10.9 56.4 all-gather.12
  70.4 54.9 all-gather.14
  128.3 85.6 all-gather.16
  216.7 87.5 all-gather.18
  306.9 82.8 all-gather.20
  1041.5 29.6 reduce-scatter.15
  1073.6 20.3 reduce-scatter.17
  1100.2 397.4 all-reduce.27
where the time goes:
time: 2490 us; the launch traced here: 2470 us
  blocking collectives  1360 us (55%)
  matrix products  704 us (28%)
  local copies, waits for them, and re-layouts  237 us (10%)
  starting transfers between devices  75.9 us (3%)
  other arithmetic  60.9 us (2%)
    unnamed x3, blocking collectives  1220 us
    unnamed x189, local copies, waits for them, and re-layouts  147 us
    dot_general x2, matrix products, backward_block(): jnp.einsum('kgst,skgd->tkd', grad_scores, query_block, preferred_element_...  145 us
    dot_general x2, matrix products, backward_block(): jnp.einsum('kgst,tkd->skgd', grad_scores, key_heads, preferred_element_ty...  143 us
    unnamed x25, starting transfers between devices  75.7 us
    dynamic_update_slice x4, local copies, waits for them, and re-layouts, shards(): lax.map(forward_block, (query_blocks, position_blocks))  73.5 us
    all_gather x1, blocking collectives, shards(): lax.all_gather(value_weight, ('dp', 'ctx'), axis=0, tiled=True)  68 us
    dot_general x7, matrix products, rows_dot(): lax.dot_general(left, right, (((0,), (0,)), ((), ())), preferred_element_...  61.3 us
  transfers between devices with their start and end apart: 32, of which 2 were waited for; matrix products, arithmetic and copies ran while one was open for 61% of the time, Pallas kernels for 0%

commit v1 on v0

v1 whole, which is shorter than its diff:
```python
import functools

import jax
import jax.numpy as jnp
from jax import lax
from jax.experimental import pallas as pl
from jax.experimental.pallas import tpu as pltpu
from jax.sharding import Mesh, PartitionSpec as P

HD = 64
IMG = 256
KV_HEADS = 2
LANES = 128
EXTRA = 128
TILE = 256

eps = 1e-06
rope_base = 1000000.0
neg_fill = -1e30

SWAP = ((0, 1), (1, 0))
F32 = jnp.float32
BF16 = jnp.bfloat16
VMEM_CAP = 60 * 1024 * 1024


def f32(v):
    return v.astype(F32)


def bf(v):
    return v.astype(BF16)


def nn(a, b):
    return jnp.dot(a, b, preferred_element_type=F32)


def nt(a, b):
    return lax.dot_general(a, b, (((1,), (1,)), ((), ())), preferred_element_type=F32)


def tn(a, b):
    return lax.dot_general(a, b, (((0,), (0,)), ((), ())), preferred_element_type=F32)


def swap(v, axis):
    return lax.ppermute(v, axis, SWAP)


def whole():
    return pl.BlockSpec(memory_space=pltpu.VMEM)


def after(values, *earlier):
    return lax.optimization_barrier((values, earlier))[0]


def along_z(own, direct):
    count = lax.axis_size("zz")
    if not direct:
        return lax.all_gather(own, "zz", axis=0, tiled=True)
    rows = own.shape[0]
    me = lax.axis_index("zz")
    zs = jnp.zeros((count * rows, own.shape[1]), own.dtype)
    zs = lax.dynamic_update_slice(zs, own, (me * rows, 0))
    for j in range(1, count):
        got = lax.ppermute(own, "zz", [(i, i ^ j) for i in range(count)])
        zs = lax.dynamic_update_slice(zs, got, ((me ^ j) * rows, 0))
    return zs


def beside(zs):
    return swap(zs, "xx"), swap(zs, "ctx")


def diagonal(xs, ys):
    half = xs.shape[0] // 2
    return swap(ys[:half], "xx"), swap(xs[half:], "ctx")


def sum_diagonal(pieces):
    return swap(pieces[3], "xx"), swap(pieces[4], "ctx")


def two_parts(v):
    high = lax.optimization_barrier(bf(v))
    return jnp.concatenate([high, bf(v - f32(high))], axis=1)


def rounded(v, vectors):
    if not vectors:
        return bf(v)
    tail = v[:, -vectors:]
    half = vectors // 2
    return jnp.concatenate([bf(v[:, :-vectors]), two_parts(tail[:, :half] + tail[:, half:])], axis=1)


def sum_beside(pieces, got, vectors=0):
    half = pieces[3].shape[0]
    xs = jnp.concatenate([pieces[1][:half], rounded(f32(pieces[1][half:]) + f32(got[1]), vectors)], 0)
    ys = jnp.concatenate([rounded(f32(pieces[2][:half]) + f32(got[0]), vectors), pieces[2][half:]], 0)
    return swap(xs, "xx"), swap(ys, "ctx")


def sum_along_z(pieces, got, vectors=0):
    count = lax.axis_size("zz")
    me = lax.axis_index("zz")
    zs = rounded(f32(pieces[0]) + f32(got[0]) + f32(got[1]), vectors)
    if not vectors:
        return [lax.optimization_barrier(lax.psum_scatter(zs, "zz", scatter_dimension=0, tiled=True))]
    rows = zs.shape[0] // count
    parts = [lax.dynamic_slice(zs, (me * rows, 0), (rows, zs.shape[1]))]
    for j in range(1, count):
        part = lax.dynamic_slice(zs, ((me ^ j) * rows, 0), (rows, zs.shape[1]))
        parts.append(lax.ppermute(part, "zz", [(i, i ^ j) for i in range(count)]))
    return parts


def sum_pair(parts):
    own = sum(f32(p) for p in parts)
    rows = own.shape[0]
    first, second = own[: rows // 2], own[rows // 2 :]
    here = lax.axis_index("core") == 0
    return jnp.where(here, first, second), swap(jnp.where(here, second, first), "core")


def pair_rows(mine, theirs):
    got = swap(theirs, "core")
    here = lax.axis_index("core") == 0
    return jnp.where(here, jnp.concatenate([mine, got], axis=0), jnp.concatenate([got, mine], axis=0))


def tiles_of(width):
    return [(o, min(TILE, width - o)) for o in range(0, width, TILE)]


def pack_kernel(chunks, core_ref, gate_ref, up_ref, down_ref, *outs):
    core = core_ref[0]
    half = gate_ref.shape[1] // 2
    for side in range(2):
        base = jnp.where(side == 0, core, 1 - core) * half
        for (start, width), out in zip(chunks, outs[side * len(chunks) : (side + 1) * len(chunks)]):
            for o, t in tiles_of(width):
                for k, ref in enumerate((gate_ref, up_ref, down_ref)):
                    at = pl.multiple_of(base + (start + o), LANES)
                    out[:, 3 * o + k * t : 3 * o + (k + 1) * t] = ref[:, pl.ds(at, t)]


def pack(core, gate, up, down, chunks):
    rows = gate.shape[0]
    shapes = [jax.ShapeDtypeStruct((rows, 3 * w), gate.dtype) for _, w in chunks] * 2
    return pl.pallas_call(
        functools.partial(pack_kernel, chunks),
        in_specs=[pl.BlockSpec(memory_space=pltpu.SMEM)] + [whole()] * 3,
        out_specs=[whole()] * len(shapes),
        out_shape=shapes,
        name="pack",
    )(core, gate, up, down)


def unpack_kernel(chunks, core_ref, *refs):
    core = core_ref[0]
    ins, outs = refs[: 2 * len(chunks)], refs[2 * len(chunks) :]
    half = outs[0].shape[1] // 2
    for side in range(2):
        base = jnp.where(side == 0, core, 1 - core) * half
        for (start, width), ref in zip(chunks, ins[side * len(chunks) : (side + 1) * len(chunks)]):
            for o, t in tiles_of(width):
                for k, out in enumerate(outs):
                    at = pl.multiple_of(base + (start + o), LANES)
                    out[:, pl.ds(at, t)] = ref[:, 3 * o + k * t : 3 * o + (k + 1) * t]


def unpack(core, mine, theirs, chunks, width):
    rows = mine[0].shape[0]
    shapes = [jax.ShapeDtypeStruct((rows, width), F32)] * 3
    return pl.pallas_call(
        functools.partial(unpack_kernel, chunks),
        in_specs=[pl.BlockSpec(memory_space=pltpu.SMEM)] + [whole()] * (2 * len(chunks)),
        out_specs=[whole()] * 3,
        out_shape=shapes,
        name="unpack",
    )(core, *mine, *theirs)


def mlp_kernel(last_t, rows, xm, xt, cm, ct, zw, xw, yw, aw, bw, om, ot, gm, gt, dz, dx, dy, da, db,
               xs, cs, oacc, gacc, w, h, low, sem):
    step = pl.program_id(0)
    steps = pl.num_programs(0)
    tokens = xm.shape[0]
    quarter = zw.shape[0]
    half = quarter // 2

    @pl.when(step == 0)
    def _():
        copies = [
            pltpu.make_async_copy(src, dst.at[pl.ds(o, tokens)], sem.at[i])
            for i, (src, dst, o) in enumerate(((xm, xs, 0), (xt, xs, tokens), (cm, cs, 0), (ct, cs, tokens)))
        ]
        for c in copies:
            c.start()
        for c in copies:
            c.wait()

    w[0:quarter] = zw[...]
    w[quarter : 2 * quarter] = xw[...]
    w[2 * quarter : 3 * quarter] = yw[...]
    w[3 * quarter : 3 * quarter + half] = aw[...]
    w[3 * quarter + half :] = bw[...]

    def grads(t):
        for x_ref, a, b in ((xs, 0, t), (xs, t, 2 * t), (cs, 2 * t, 3 * t)):
            d = bf(tn(x_ref[...], h[:, a:b]))
            dz[:, a:b] = d[:quarter]
            dx[:, a:b] = d[quarter : 2 * quarter]
            dy[:, a:b] = d[2 * quarter : 3 * quarter]
            da[:, a:b] = d[3 * quarter : 3 * quarter + half]
            db[:, a:b] = d[3 * quarter + half :]

    def work(t):
        def block(i, carry):
            at = pl.multiple_of(i * rows, rows)
            here = pl.ds(at, rows)
            x = xs[here, :]
            g = nn(x, w[:, :t])
            u = nn(x, w[:, t : 2 * t])
            ga = nn(cs[here, :], w[:, 2 * t : 3 * t])
            sg = 0.5 * jnp.tanh(0.5 * g) + 0.5
            silu = g * sg
            h[here, 2 * t : 3 * t] = bf(silu * u)
            h[here, :t] = bf(ga * u * (sg + silu * (1.0 - sg)))
            h[here, t : 2 * t] = bf(ga * silu)
            old = step > 0
            o = nt(h[here, 2 * t : 3 * t], w[:, 2 * t : 3 * t])
            oacc[here, :] = o + jnp.where(old, oacc[here, :], 0.0)
            gn = nt(h[here, : 2 * t], w[:, : 2 * t])
            gacc[here, :] = gn + jnp.where(old, gacc[here, :], 0.0)
            return carry

        lax.fori_loop(0, 2 * tokens // rows, block, 0)

    def sums_out():
        return [
            pltpu.make_async_copy(low.at[i], dst, sem.at[i])
            for i, dst in enumerate((gt, gm, ot, om))
        ]

    def tile(t):
        work(t)

        @pl.when(step == steps - 1)
        def _():
            for i, (acc, part) in enumerate(((gacc, 1), (gacc, 0), (oacc, 1), (oacc, 0))):
                low[i] = bf(acc[pl.ds(part * tokens, tokens), :])
            for c in sums_out():
                c.start()

        grads(t)

    if last_t == TILE:
        tile(TILE)
    else:
        @pl.when(step < steps - 1)
        def _():
            tile(TILE)

        @pl.when(step == steps - 1)
        def _():
            tile(last_t)

    @pl.when(step == steps - 1)
    def _():
        for c in sums_out():
            c.wait()


def mlp(xm, xt, cm, ct, pieces, rows=1024):
    tokens, width = xm.shape
    cols = pieces[0].shape[1] // 3
    steps = pl.cdiv(cols, TILE)
    last_t = cols - (steps - 1) * TILE
    block = lambda p: pl.BlockSpec((p.shape[0], 3 * TILE), lambda i: (0, i))
    any_space = pl.BlockSpec(memory_space=pl.ANY)
    lo = jax.ShapeDtypeStruct((tokens, width), BF16)
    return pl.pallas_call(
        functools.partial(mlp_kernel, last_t, rows),
        grid=(steps,),
        in_specs=[any_space] * 4 + [block(p) for p in pieces],
        out_specs=[any_space] * 4 + [block(p) for p in pieces],
        out_shape=[lo] * 4 + [jax.ShapeDtypeStruct(p.shape, BF16) for p in pieces],
        scratch_shapes=[
            pltpu.VMEM((2 * tokens, width), BF16),
            pltpu.VMEM((2 * tokens, width), BF16),
            pltpu.VMEM((2 * tokens, width), F32),
            pltpu.VMEM((2 * tokens, width), F32),
            pltpu.VMEM((width, 3 * TILE), BF16),
            pltpu.VMEM((2 * tokens, 3 * TILE), BF16),
            pltpu.VMEM((4, tokens, width), BF16),
            pltpu.SemaphoreType.DMA((4,)),
        ],
        compiler_params=pltpu.CompilerParams(vmem_limit_bytes=VMEM_CAP),
        cost_estimate=pl.CostEstimate(flops=9 * 2 * 2 * tokens * width * cols, bytes_accessed=12 * width * cols, transcendentals=0),
        name="feed_forward",
    )(xm, xt, cm, ct, *pieces)


def spans(info_ref, qi, bq, bk, length):
    first = info_ref[0] * length + qi * bq
    last = first + bq - 1
    top = last + 1
    starts = (info_ref[1], info_ref[2])
    for s in starts:
        top = jnp.where((s <= last) & (s + IMG > first), jnp.maximum(top, s + IMG), top)
    return first, (first + 1) // bk, (top + bk - 1) // bk, starts


def allowed_tile(first, key_first, starts, bk, bq):
    kp = key_first + lax.broadcasted_iota(jnp.int32, (bk, bq), 0)
    qp = first + lax.broadcasted_iota(jnp.int32, (bk, bq), 1)
    ok = kp <= qp
    for s in starts:
        ok = ok | ((kp >= s) & (kp < s + IMG) & (qp >= s) & (qp < s + IMG))
    return ok


def stack_heads(ref, heads):
    return jnp.concatenate([ref[HD * h : HD * (h + 1), :] for h in range(heads)], axis=1)


def attn_fwd_kernel(bk, info_ref, q_ref, loc_ref, rem_ref, o_ref, rest_ref, lse_ref, k3, vt3):
    qi = pl.program_id(0)
    length = loc_ref.shape[1]
    blocks = length // bk
    heads = q_ref.shape[0] // HD
    bq = q_ref.shape[1]

    @pl.when(qi == 0)
    def _():
        for side, ref in enumerate((loc_ref, rem_ref)):
            for b in range(blocks):
                cols = slice(b * bk, (b + 1) * bk)
                k3[side * blocks + b] = jnp.transpose(ref[:HD, cols])
                vt3[side * blocks + b, :HD] = ref[HD:, cols]
                vt3[side * blocks + b, HD:] = jnp.ones((16, bk), BF16)

    first, n_full, n_all, starts = spans(info_ref, qi, bq, bk, length)
    q = stack_heads(q_ref, heads)
    width = heads * bq
    shift = info_ref[0] * blocks

    def step(b, carry, masked):
        top, acc = carry
        slot = lax.rem(b + shift, 2 * blocks)
        s = nn(k3[slot], q)
        if masked:
            ok = allowed_tile(first, b * bk, starts, bk, bq)
            s = jnp.concatenate([jnp.where(ok, s[:, h * bq : (h + 1) * bq], neg_fill) for h in range(heads)], axis=1)
        new_top = jnp.maximum(top, jnp.max(s, axis=0, keepdims=True))
        p = jnp.exp(s - new_top)
        scale = jnp.exp(top - new_top)
        acc = acc * scale + nn(vt3[slot], bf(p))
        return new_top, acc

    carry = (jnp.full((1, width), neg_fill, F32), jnp.zeros((HD + 16, width), F32))
    carry = lax.fori_loop(0, n_full, functools.partial(step, masked=False), carry)
    top, acc = lax.fori_loop(n_full, n_all, functools.partial(step, masked=True), carry)
    total = acc[HD : HD + 1]
    out = acc[:HD] / total
    low = bf(out)
    rest = bf(out - f32(low))
    for h in range(heads):
        o_ref[HD * h : HD * (h + 1), :] = low[:, h * bq : (h + 1) * bq]
        rest_ref[HD * h : HD * (h + 1), :] = rest[:, h * bq : (h + 1) * bq]
    lse_ref[...] = (top + jnp.log(total)).reshape(lse_ref.shape)


def attn_fwd(info, q, loc, rem, bq, bk):
    group, length = q.shape
    blocks = length // bq
    width = group // HD * bq
    return pl.pallas_call(
        functools.partial(attn_fwd_kernel, bk),
        grid=(blocks,),
        in_specs=[
            pl.BlockSpec(memory_space=pltpu.SMEM),
            pl.BlockSpec((group, bq), lambda i: (0, i)),
            whole(),
            whole(),
        ],
        out_specs=[
            pl.BlockSpec((group, bq), lambda i: (0, i)),
            pl.BlockSpec((group, bq), lambda i: (0, i)),
            pl.BlockSpec((1, 1, width), lambda i: (i, 0, 0)),
        ],
        out_shape=[
            jax.ShapeDtypeStruct((group, length), BF16),
            jax.ShapeDtypeStruct((group, length), BF16),
            jax.ShapeDtypeStruct((blocks, 1, width), F32),
        ],
        scratch_shapes=[
            pltpu.VMEM((2 * length // bk, bk, HD), BF16),
            pltpu.VMEM((2 * length // bk, HD + 16, bk), BF16),
        ],
        compiler_params=pltpu.CompilerParams(vmem_limit_bytes=VMEM_CAP),
        cost_estimate=pl.CostEstimate(flops=16 * group * length * length, bytes_accessed=8 * group * length, transcendentals=group * length * length // HD),
        name="attention",
    )(info, q, loc, rem)


def attn_bwd_kernel(bk, info_ref, q_ref, do_ref, o_ref, rest_ref, lse_ref, loc_ref, rem_ref, rope_q, rope_l, rope_r,
                    dq_ref, dloc_ref, drem_ref, sum_ref, k3, kt3, v3, dk3, dv3):
    qi = pl.program_id(0)
    length = loc_ref.shape[1]
    blocks = length // bk
    heads = q_ref.shape[0] // HD
    bq = q_ref.shape[1]
    hd = HD // 2

    @pl.when(qi == 0)
    def _():
        for side, ref in enumerate((loc_ref, rem_ref)):
            for b in range(blocks):
                cols = slice(b * bk, (b + 1) * bk)
                k3[side * blocks + b] = jnp.transpose(ref[:HD, cols])
                kt3[side * blocks + b] = ref[:HD, cols]
                v3[side * blocks + b] = jnp.transpose(ref[HD:, cols])
        dk3[...] = jnp.zeros_like(dk3)
        dv3[...] = jnp.zeros_like(dv3)

    first, n_full, n_all, starts = spans(info_ref, qi, bq, bk, length)
    q = stack_heads(q_ref, heads)
    do = stack_heads(do_ref, heads)
    o = f32(stack_heads(o_ref, heads)) + f32(stack_heads(rest_ref, heads))
    delta = jnp.sum(f32(do) * o, axis=0, keepdims=True)
    lse = lse_ref[...].reshape(1, heads * bq)
    shift = info_ref[0] * blocks

    def step(b, dq, masked):
        slot = lax.rem(b + shift, 2 * blocks)
        s = nn(k3[slot], q)
        if masked:
            ok = allowed_tile(first, b * bk, starts, bk, bq)
            s = jnp.concatenate([jnp.where(ok, s[:, h * bq : (h + 1) * bq], neg_fill) for h in range(heads)], axis=1)
        p = jnp.exp(s - lse)
        dp = nn(v3[slot], do)
        ds = bf(p * (dp - delta))
        dv3[slot] += nt(do, bf(p))
        dk3[slot] += nt(q, ds)
        return dq + nn(kt3[slot], ds)

    dq = jnp.zeros((HD, heads * bq), F32)
    dq = lax.fori_loop(0, n_full, functools.partial(step, masked=False), dq)
    dq = lax.fori_loop(n_full, n_all, functools.partial(step, masked=True), dq)

    def back(v, table):
        cos, sin = table[:hd], table[hd:]
        a, b = v[:hd], v[hd:]
        return jnp.concatenate([a * cos + b * sin, b * cos - a * sin], axis=0)

    scale = HD**-0.5
    table = rope_q[...]
    for h in range(heads):
        dq_ref[HD * h : HD * (h + 1), :] = bf(back(dq[:, h * bq : (h + 1) * bq] * scale, table))

    @pl.when(qi == pl.num_programs(0) - 1)
    def _():
        fold = jnp.zeros(sum_ref.shape, F32)
        for side, (ref, rope) in enumerate(((dloc_ref, rope_l), (drem_ref, rope_r))):
            for b in range(blocks):
                cols = slice(b * bk, (b + 1) * bk)
                both = jnp.concatenate([back(dk3[side * blocks + b], rope[:, cols]), dv3[side * blocks + b]], axis=0)
                ref[:, cols] = both.astype(ref.dtype)
                for o in range(0, bk, LANES):
                    fold = fold + both[:, o : o + LANES]
        sum_ref[...] = fold


def attn_bwd(info, q, do, o, rest, lse, loc, rem, rope_loc, rope_rem, bq, bk):
    group, length = q.shape
    blocks = length // bq
    width = group // HD * bq
    rows = pl.BlockSpec((group, bq), lambda i: (0, i))
    return pl.pallas_call(
        functools.partial(attn_bwd_kernel, bk),
        grid=(blocks,),
        in_specs=[
            pl.BlockSpec(memory_space=pltpu.SMEM),
            rows, rows, rows, rows,
            pl.BlockSpec((1, 1, width), lambda i: (i, 0, 0)),
            whole(), whole(),
            pl.BlockSpec((HD, bq), lambda i: (0, i)),
            whole(), whole(),
        ],
        out_specs=[rows, whole(), whole(), whole()],
        out_shape=[
            jax.ShapeDtypeStruct((group, length), BF16),
            jax.ShapeDtypeStruct(loc.shape, F32),
            jax.ShapeDtypeStruct(loc.shape, BF16),
            jax.ShapeDtypeStruct((loc.shape[0], LANES), F32),
        ],
        scratch_shapes=[
            pltpu.VMEM((2 * length // bk, bk, HD), BF16),
            pltpu.VMEM((2 * length // bk, HD, bk), BF16),
            pltpu.VMEM((2 * length // bk, bk, HD), BF16),
            pltpu.VMEM((2 * length // bk, HD, bk), F32),
            pltpu.VMEM((2 * length // bk, HD, bk), F32),
        ],
        compiler_params=pltpu.CompilerParams(vmem_limit_bytes=VMEM_CAP),
        cost_estimate=pl.CostEstimate(flops=40 * group * length * length, bytes_accessed=16 * group * length, transcendentals=group * length * length // HD),
        name="attention_back",
    )(info, q, do, o, rest, lse, loc, rem, rope_loc, rope_loc, rope_rem)


def rope_table(first, length):
    half = HD // 2
    inverse = rope_base ** (-(jnp.arange(half).astype(F32) * 2.0 / HD))
    angles = inverse[:, None] * f32(first + jnp.arange(length, dtype=jnp.int32))[None, :]
    return jnp.concatenate([jnp.cos(angles), jnp.sin(angles)], axis=0)


def rope(v, table):
    half = HD // 2
    shaped = v.reshape(-1, 2, half, v.shape[1])
    cos, sin = table[None, :half], table[None, half:]
    a, b = shaped[:, 0], shaped[:, 1]
    return jnp.stack([a * cos - b * sin, b * cos + a * sin], axis=1).reshape(v.shape)


def device_order(rows, count):
    p = jnp.arange(8 * count * rows, dtype=jnp.int32)
    q = p // (count * 2 * rows)
    z = (p // (2 * rows)) % count
    c = (p // rows) % 2
    x_rel = ((q == 1) | (q == 3)).astype(jnp.int32)
    y_rel = (q >= 2).astype(jnp.int32)
    chip = z * 2 + (lax.axis_index("xx") ^ x_rel)
    flat = (chip * 2 + c) * 2 + (lax.axis_index("ctx") ^ y_rel)
    return flat * rows + p % rows


def column(v, rows):
    return jnp.pad(v, (0, rows - v.shape[0]))[:, None]


def shards(
    tokens, image_starts, attn_gain, query_weight, query_bias, key_weight, key_bias, value_weight, value_bias,
    out_weight, mlp_gain, gate_weight, up_weight, down_weight, cotangent,
):
    length, width = tokens.shape
    count = lax.axis_size("zz")
    devices = 8 * count
    rows = width // devices
    core = lax.axis_index("core")
    ctx = lax.axis_index("ctx")
    core_arr = core.reshape(1).astype(jnp.int32)
    feat = query_weight.shape[1]
    kv_feat = key_weight.shape[1]
    ff = gate_weight.shape[1]
    half_ff = ff // 2
    units = half_ff // LANES
    cuts = [0, units // 5 * 2 + 2, units]
    chunks = tuple((a * LANES, (b - a) * LANES) for a, b in zip(cuts, cuts[1:]))
    n = len(chunks)
    own_first = core == 0

    extras = jnp.concatenate(
        [column(v, rows) for v in (attn_gain, mlp_gain, query_bias, key_bias, value_bias)]
        + [jnp.zeros((rows, EXTRA - 5), BF16)], axis=1)
    fh, kh = feat // 2, kv_feat // 2
    sides = [
        jnp.concatenate([query_weight[:, s * fh : (s + 1) * fh], key_weight[:, s * kh : (s + 1) * kh],
                         value_weight[:, s * kh : (s + 1) * kh], out_weight[:, s * fh : (s + 1) * fh], extras], axis=1)
        for s in range(2)
    ]
    a_own = pair_rows(jnp.where(own_first, sides[0], sides[1]), jnp.where(own_first, sides[1], sides[0]))
    tokens, cotangent = after((tokens, cotangent), a_own)
    a_zs = along_z(a_own, True)
    gate_weight, up_weight, down_weight = after((gate_weight, up_weight, down_weight), a_own)
    packed = pack(core_arr, gate_weight, up_weight, down_weight, chunks)
    own = [pair_rows(packed[i], packed[n + i]) for i in range(n)]
    f_zs = [along_z(v, False) for v in own]

    natural = device_order(rows, count)
    to_dev = bf(jnp.arange(width, dtype=jnp.int32)[:, None] == natural[None, :])
    x = nn(tokens, to_dev)
    r1 = lax.rsqrt(jnp.mean(x * x, axis=-1, keepdims=True) + eps)
    table = rope_table(ctx * length, length)
    table_rem = rope_table((1 - ctx) * length, length)

    a_xs, a_ys = beside(a_zs)
    a_pieces = [a_zs, a_xs, a_ys, *diagonal(a_xs, a_ys)]
    w_mine = jnp.concatenate(a_pieces, axis=0)
    w_side = [w_mine, swap(w_mine, "core")]

    q0, k0, v0, o0, e0 = 0, fh, fh + kh, fh + 2 * kh, 2 * fh + 2 * kh
    extra_rel = w_mine[:, e0:]
    gains = jnp.transpose(f32(extra_rel[:, :2]))
    gain_attn, gain_mlp = gains[0:1], gains[1:2]
    bias_nat = nn(to_dev, extra_rel)
    q_bias = bias_nat[:, 2]
    kv_rows = kv_feat // devices
    k_bias = bias_nat[:, 3].reshape(devices, rows)[:, :kv_rows].reshape(-1)
    v_bias = bias_nat[:, 4].reshape(devices, rows)[:, :kv_rows].reshape(-1)

    def by_side(v):
        lo, hi = v[: v.shape[0] // 2], v[v.shape[0] // 2 :]
        return jnp.where(own_first, lo, hi), jnp.where(own_first, hi, lo)

    normed_one = bf(x * r1 * gain_attn)
    keys_values = []
    for w_all, kb, vb in zip(w_side, by_side(k_bias), by_side(v_bias)):
        kv = lax.dot_general(w_all[:, k0:o0], normed_one, (((0,), (1,)), ((), ())), preferred_element_type=F32)
        kv = kv + jnp.concatenate([kb, vb])[:, None]
        keys_values.append(jnp.concatenate([bf(rope(kv[:kh], table)), bf(kv[kh:])], axis=0))
    kv_rem = swap(jnp.concatenate(keys_values, axis=0), "ctx")
    kv_rem = [kv_rem[: 2 * kh], kv_rem[2 * kh :]]
    queries = []
    for w_all, qb in zip(w_side, by_side(q_bias)):
        q = lax.dot_general(w_all[:, :k0], after(normed_one, *keys_values), (((0,), (1,)), ((), ())), preferred_element_type=F32)
        queries.append(bf(rope(q + qb[:, None], table) * HD**-0.5))
    f_xy = [None] * n
    f_diag = [None] * n
    f_xs = swap(after(f_zs[0], normed_one), "xx")
    f_ys = swap(after(f_zs[0], *kv_rem), "ctx")
    f_xy[0] = (f_xs, f_ys)

    info = jnp.concatenate([ctx.reshape(1).astype(jnp.int32), image_starts[0]])
    bq = min(256, length)
    bk = min(256, length)
    queries[0] = after(queries[0], f_zs[0])
    att0, rest0, lse0 = attn_fwd(info, queries[0], keys_values[0], kv_rem[0], bq, bk)
    f_xy[0] = after(f_xy[0], att0)
    f_diag[0] = diagonal(*f_xy[0])
    f_zs[1] = after(f_zs[1], att0)
    f_xy[1] = beside(f_zs[1])
    queries[1] = after(queries[1], f_xy[0], f_zs[1])
    att1, rest1, lse1 = attn_fwd(info, queries[1], keys_values[1], kv_rem[1], bq, bk)
    f_xy[1] = after(f_xy[1], att1)
    f_diag[1] = diagonal(*f_xy[1])
    for i in range(2, n):
        f_zs[i] = after(f_zs[i], att1)
        f_xy[i] = beside(f_zs[i])
    attended, rest, lse = [att0, att1], [rest0, rest1], [lse0, lse1]

    cotangent = after(cotangent, att0)
    cot = bf(nn(cotangent, to_dev))
    cot_theirs = swap(cot, "core")
    hidden = x
    for a, w_all in zip(attended, w_side):
        hidden = hidden + lax.dot_general(a, w_all[:, o0:e0], (((0,), (1,)), ((), ())), preferred_element_type=F32)
    r2 = lax.rsqrt(jnp.mean(hidden * hidden, axis=-1, keepdims=True) + eps)
    normed_two = bf(hidden * r2 * gain_mlp)
    normed_theirs = swap(normed_two, "core")

    results, got_d, got_b, got_z = [], [None] * n, [None] * n, [None] * n
    x_in = normed_two
    for i in range(n):
        r = mlp(x_in, normed_theirs, cot, cot_theirs, [f_zs[i], *f_xy[i], *f_diag[i]])
        results.append(r)
        x_in = after(normed_two, r[2])
        if i + 2 < n:
            f_xy[i + 2] = after(f_xy[i + 2], r[2])
            f_diag[i + 2] = diagonal(*f_xy[i + 2])
        got_d[i] = sum_diagonal(r[4:])
        if i > 0:
            got_d[i - 1] = after(got_d[i - 1], r[2])
            got_b[i - 1] = sum_beside(results[i - 1][4:], got_d[i - 1])

    def total(a, b):
        mine = sum(f32(r[a]) for r in results)
        return mine + f32(swap(bf(sum(f32(r[b]) for r in results)), "core"))

    grad_two = total(2, 3)
    mlp_gain_grad = jnp.sum(grad_two * hidden * r2, axis=0)
    u = grad_two * gain_mlp
    grad_hidden = f32(cot) + r2 * u - hidden * (r2 * r2 * r2) * jnp.mean(u * hidden, axis=-1, keepdims=True)
    grad_attn = bf(grad_hidden)
    grad_mixed = [
        bf(lax.dot_general(w_all[:, o0:e0], grad_attn, (((0,), (1,)), ((), ())), preferred_element_type=F32)) for w_all in w_side
    ]

    lows, d_sums = [], []
    back = [None, None]
    for s in range(2):
        do = grad_mixed[s]
        if s == 1:
            do = after(do, back[0][0])
            for i in range(n - 1):
                got_b[i] = after(got_b[i], back[0][0])
                got_z[i] = sum_along_z(results[i][4:], got_b[i])
            got_d[n - 1] = after(got_d[n - 1], back[0][0])
            got_b[n - 1] = sum_beside(results[n - 1][4:], got_d[n - 1])
        back[s] = attn_bwd(info, queries[s], do, attended[s], rest[s], lse[s], keys_values[s], kv_rem[s], table, table_rem, bq, bk)
    got_b[n - 1] = after(got_b[n - 1], back[1][0])
    got_z[n - 1] = sum_along_z(results[n - 1][4:], got_b[n - 1])
    for s in range(2):
        query_low, d_loc, d_rem, _ = back[s]
        kv_low = bf(d_loc + f32(swap(d_rem, "ctx")))
        lows.append(jnp.concatenate([query_low, kv_low], axis=0))

    out_sum = total(0, 1)
    output = bf(nt(bf(hidden + out_sum), to_dev))
    mlp_out = [sum_pair(z) for z in got_z]
    gate_grad, up_grad, down_grad = unpack(core_arr, [m[0] for m in mlp_out], [m[1] for m in mlp_out], chunks, ff)

    out_grad = [lax.dot_general(grad_attn, a, (((0,), (1,)), ((), ())), preferred_element_type=F32) for a in attended]
    grad_one = 0.0
    for low, w_all in zip(lows, w_side):
        grad_one = grad_one + lax.dot_general(low, w_all[:, :o0], (((0,), (1,)), ((), ())), preferred_element_type=F32)
    w = grad_one * gain_attn
    tokens_grad_dev = grad_hidden + r1 * w - x * (r1 * r1 * r1) * jnp.mean(w * x, axis=-1, keepdims=True)
    tokens_grad = bf(nt(bf(tokens_grad_dev), to_dev))
    attn_gain_grad = jnp.sum(grad_one * x * r1, axis=0)
    qkv_grad = [lax.dot_general(normed_one, low, (((0,), (1,)), ((), ())), preferred_element_type=F32) for low in lows]
    bias_grad = [jnp.concatenate([jnp.sum(f32(b[0]), axis=1), jnp.sum(b[3], axis=1)]) for b in back]

    def whole_order(a, b):
        return jnp.where(own_first, jnp.concatenate([a, b]), jnp.concatenate([b, a]))

    def spread(v):
        return jnp.pad(v.reshape(devices, -1), ((0, 0), (0, rows - v.shape[0] // devices))).reshape(-1)

    qb, kb, vb = [whole_order(bias_grad[0][a:b], bias_grad[1][a:b]) for a, b in ((q0, k0), (k0, v0), (v0, o0))]
    nat_cols = jnp.stack([qb, spread(kb), spread(vb)], axis=0)
    dev_cols = nn(two_parts(nat_cols.T).T, to_dev)
    dev_cols = dev_cols[:3] + dev_cols[3:]
    vec_cols = jnp.concatenate([attn_gain_grad[None], mlp_gain_grad[None], dev_cols, jnp.zeros((EXTRA // 2 - 5, width), F32)], axis=0)
    extra_grad = two_parts(jnp.transpose(vec_cols))
    g_mine = jnp.concatenate([bf(qkv_grad[0]), bf(out_grad[0]), extra_grad], axis=1)
    g_theirs = jnp.concatenate([bf(qkv_grad[1]), bf(out_grad[1])], axis=1)
    got = swap(g_theirs, "core")
    g_sum = jnp.concatenate([bf(f32(g_mine[:, :e0]) + f32(got)), g_mine[:, e0:]], axis=1)
    quarter = width // 4
    bounds = [0, quarter, 2 * quarter, 3 * quarter, 3 * quarter + quarter // 2, width]
    g_pieces = [g_sum[a:b] for a, b in zip(bounds, bounds[1:])]
    g_got = sum_beside(g_pieces, sum_diagonal(g_pieces), EXTRA)
    a_mine, a_theirs = sum_pair(sum_along_z(g_pieces, g_got, EXTRA))

    def natural_cols(a, b):
        lo, hi = a_mine[:, a:b], a_theirs[:, a:b]
        return jnp.where(own_first, jnp.concatenate([lo, hi], axis=1), jnp.concatenate([hi, lo], axis=1))

    extra = a_mine[:, e0:] + a_theirs[:, e0:]
    extra = extra[:, : EXTRA // 2] + extra[:, EXTRA // 2 :]
    return (
        output,
        tokens_grad,
        extra[:, 0],
        natural_cols(q0, k0),
        extra[:, 2],
        natural_cols(k0, v0),
        extra[:kv_rows, 3],
        natural_cols(v0, o0),
        extra[:kv_rows, 4],
        natural_cols(o0, e0),
        extra[:, 1],
        gate_grad,
        up_grad,
        down_grad,
    )


def solution(mesh):
    dp, ctx = mesh.devices.shape
    fine = Mesh(mesh.devices.reshape(dp // 4, 2, 2, ctx), ("zz", "xx", "core", "ctx"))
    every = ("zz", "xx", "core", "ctx")
    mat, vec = P(every, None), P(every)
    placed = (mat, P(("zz", "xx", "core"), None), vec, mat, vec, mat, vec, mat, vec, mat, vec, mat, mat, mat, mat)
    outs = (mat, mat, vec, mat, vec, mat, vec, mat, vec, mat, vec, mat, mat, mat)
    return jax.shard_map(shards, mesh=fine, in_specs=placed, out_specs=outs, check_vma=False)
```

time: 2490 us -> 567 us (0.23)
  blocking collectives: 1360 us -> 0 us
  matrix products: 704 us -> 57.7 us
  local copies, waits for them, and re-layouts: 237 us -> 37.6 us
  Pallas kernels: 0 us -> 195 us
  waiting for transfers between devices: 15.3 us -> 84.8 us
  starting transfers between devices: 75.9 us -> 109 us
    unnamed x3 -> x0, blocking collectives: 1220 us -> none
    dot_general x35 -> x20, matrix products: 704 us -> 57.7 us  [the longest x2 10.4 us: shards(): lax.dot_general(a, w_all[:, o0:e0], (((0,), (1,)), ((), ())), preferred_e...]
    pallas_call x0 -> x8, Pallas kernels: none -> 195 us  [the longest x2 116 us: mlp(): pl.pallas_call(functools.partial(mlp_kernel, last_t, rows), grid=(steps,)...]
    all_gather x4 -> x0, blocking collectives: 139 us -> none  [the longest x1 68 us: shards(): lax.all_gather(value_weight, ('dp', 'ctx'), axis=0, tiled=True)]
    unnamed x189 -> x135, local copies, waits for them, and re-layouts: 147 us -> 9.92 us
    ppermute x0 -> x45, starting transfers between devices: none -> 109 us  [the longest x39 101 us: swap(): return lax.ppermute(v, axis, SWAP)]
    ppermute x0 -> x45, waiting for transfers between devices: none -> 84.7 us  [the longest x3 47.4 us: sum_along_z(): parts.append(lax.ppermute(part, 'zz', [(i, i ^ j) for i in range(count)]))]
    unnamed x25 -> x1, starting transfers between devices: 75.7 us -> 0.21 us
  transfers between devices with their start and end apart: 32 -> 49, of which waited for: 2 -> 12; matrix products, arithmetic and copies ran while one was open for 61% -> 26% of each run, Pallas kernels for 0% -> 34%
where the time goes in v1:
time: 567 us; the launch traced here: 560 us
  Pallas kernels  195 us (34%)
  starting transfers between devices  109 us (19%)
  waiting for transfers between devices  84.8 us (15%)
  other arithmetic  61 us (11%)
  matrix products  57.7 us (10%)
  local copies, waits for them, and re-layouts  37.6 us (7%)
  between operations  15.3 us (3%)
    pallas_call x2, Pallas kernels, mlp(): pl.pallas_call(functools.partial(mlp_kernel, last_t, rows), grid=(steps,)...  116 us
    ppermute x39, starting transfers between devices, swap(): return lax.ppermute(v, axis, SWAP)  101 us
    ppermute x3, waiting for transfers between devices, sum_along_z(): parts.append(lax.ppermute(part, 'zz', [(i, i ^ j) for i in range(count)]))  47.4 us
    pallas_call x2, Pallas kernels, attn_bwd(): pl.pallas_call(functools.partial(attn_bwd_kernel, bk), grid=(blocks,), in...  44.3 us
    ppermute x39, waiting for transfers between devices, swap(): return lax.ppermute(v, axis, SWAP)  37.3 us
    pallas_call x2, Pallas kernels, attn_fwd(): pl.pallas_call(functools.partial(attn_fwd_kernel, bk), grid=(blocks,), in...  29.6 us
    convert_element_type x26, other arithmetic, bf(): return v.astype(BF16)  28.8 us
  transfers between devices with their start and end apart: 49, of which 12 were waited for; matrix products, arithmetic and copies ran while one was open for 26% of the time, Pallas kernels for 34%

profile of v1, /device:TPU:9, one launch (start us, length us, event | category | flops | bytes accessed | tf_op | source)
XLA Modules:
  0.0 560.2 jit_solution(4374952841423357170)
XLA Ops:
  17.8 2.2 pack.1
  20.7 2.5 collective-permute-start.2
  25.3 4.0 multiply_reduce_fusion.5
  29.3 5.1 copy.176
  41.0 9.7 %collective-permute-done.5 = bf16[224,1152]{1,0:T(8,128)(2,1)S(1)} collective-permute-done((bf16[224,1152]{1,0:T(8,128)(2,1)S(1)}, bf16[224,1152]{1,0:T(8,128)(2,1)S(1)}, u32[]{:S(2)}, u32[]{:S(2)}) %collective-permute-start.5) | collective-permute-done | bytes 516128 | tf_op jit(solution)/shard_map/ppermute | solution.py:48
  54.2 3.3 collective-permute-done.6
  64.6 2.4 multiply_convert_fusion.1
  67.0 2.2 convolution_add_fusion.4
  77.4 2.4 convolution_add_fusion.1
  82.7 5.4 collective-permute-done.10
  90.3 14.9 %attention.2 = (bf16[448,1024]{1,0:T(8,128)(2,1)}, bf16[448,1024]{1,0:T(8,128)(2,1)}, f32[4,1,1792]{2,1,0:T(1,128)}) custom-call(s32[3]{0:T(128)} %pad_add_fusion.info_ref, bf16[448,1024]{1,0:T(8,128)(2,1)} %bitcast.75, bf16[128,1024]{1,0:T(8,128)(2,1)} %pad_maximum_fusion.15.loc_ref, bf16[128,1024]{1,0:T(8,128)(2,1)} %get-tuple-element.210.rem_ref), custom_call_target="tpu_custom_call" | custom-call | flops 7516192768 | bytes 3670016 | tf_op jit(solution)/shard_map/attention/pallas_call | solution.py:382
  105.3 12.0 %collective-permute-start.19 = (bf16[224,4224]{1,0:T(8,128)(2,1)}, bf16[224,4224]{1,0:T(8,128)(2,1)}, u32[]{:S(2)}, u32[]{:S(2)}) collective-permute-start(bf16[224,4224]{1,0:T(8,128)(2,1)} %all-gather.5.cloned.1.call-done.zw), channel_id=1, source_target_pairs={{0,1},{1,0},{2,3},{3,2},{4,5},{5,4},{6,7},{7,6},{8,9},{9,8},{10,11... | collective-permute-start | bytes 5677064 | tf_op jit(solution)/shard_map/ppermute | solution.py:48
  117.2 3.8 fusion.12.cm
  122.9 4.8 fusion.32
  127.7 14.7 %attention.3 = (bf16[448,1024]{1,0:T(8,128)(2,1)}, bf16[448,1024]{1,0:T(8,128)(2,1)}, f32[4,1,1792]{2,1,0:T(1,128)}) custom-call(s32[3]{0:T(128)} %pad_add_fusion.info_ref, bf16[448,1024]{1,0:T(8,128)(2,1)} %bitcast.73, bf16[128,1024]{1,0:T(8,128)(2,1)} %pad_maximum_fusion.16.loc_ref, bf16[128,1024]{1,0:T(8,128)(2,1)} %get-tuple-element.209.rem_ref), custom_call_target="tpu_custom_call" | custom-call | flops 7516192768 | bytes 3670016 | tf_op jit(solution)/shard_map/attention/pallas_call | solution.py:382
  142.4 5.7 %multiply_reduce_fusion.4 = (f32[1024]{0:T(1024)S(1)}, f32[1024,896]{1,0:T(8,128)S(1)}) fusion(bf16[448,1024]{1,0:T(8,128)(2,1)} %get-tuple-element.96.o_ref, bf16[896,1152]{1,0:T(8,128)(2,1)} %collective-permute-done.8, f32[1024,896]{1,0:T(8,128)} %copy.176, f32[1024,896]{1,0:T(8,128)} %fusion.32), kind=kOutput, calls=%fused_computation.13 | convolution fusion | flops 825752576 | bytes 12849152 | tf_op jit(solution)/shard_map/dot_general | solution.py:651
  153.0 10.9 %collective-permute-start.17 = (bf16[112,3072]{1,0:T(8,128)(2,1)S(1)}, bf16[112,3072]{1,0:T(8,128)(2,1)S(1)}, u32[]{:S(2)}, u32[]{:S(2)}) collective-permute-start(bf16[112,3072]{1,0:T(8,128)(2,1)S(1)} %slice.416), channel_id=1, source_target_pairs={{0,1},{1,0},{2,3},{3,2},{4,5},{5,4},{6,7},{7,6},{8,9},{9,8},{10,11... | collective-permute-start | bytes 2064392 | tf_op jit(solution)/shard_map/ppermute | solution.py:48
  165.3 2.2 slice.417
  168.0 2.2 slice.418
  170.2 8.8 %collective-permute-done.17.bw = bf16[112,3072]{1,0:T(8,128)(2,1)S(1)} collective-permute-done((bf16[112,3072]{1,0:T(8,128)(2,1)S(1)}, bf16[112,3072]{1,0:T(8,128)(2,1)S(1)}, u32[]{:S(2)}, u32[]{:S(2)}) %collective-permute-start.17) | collective-permute-done | bytes 688160 | tf_op jit(solution)/shard_map/ppermute | solution.py:48
  179.9 47.2 %feed_forward.2 = (bf16[1024,896]{1,0:T(8,128)(2,1)}, bf16[1024,896]{1,0:T(8,128)(2,1)}, bf16[1024,896]{1,0:T(8,128)(2,1)}, bf16[1024,896]{1,0:T(8,128)(2,1)}, b...) custom-call(bf16[1024,896]{1,0:T(8,128)(2,1)} %copy-done.24, ...), custom_call_target="tpu_custom_call" | custom-call | flops 33822867456 | bytes 11010048 | tf_op jit(solution)/shard_map/feed_forward/pallas_call | solution.py:286
  229.4 68.7 %feed_forward.3 = (bf16[1024,896]{1,0:T(8,128)(2,1)}, bf16[1024,896]{1,0:T(8,128)(2,1)}, bf16[1024,896]{1,0:T(8,128)(2,1)}, bf16[1024,896]{1,0:T(8,128)(2,1)}, b...) custom-call(bf16[1024,896]{1,0:T(8,128)(2,1)} %copy-done.24, ...), custom_call_target="tpu_custom_call" | custom-call | flops 46506442752 | bytes 15138816 | tf_op jit(solution)/shard_map/feed_forward/pallas_call | solution.py:286
  298.2 2.1 add_convert_fusion.2
  300.3 2.8 collective-permute-start.23
  317.3 3.1 fusion.87
  320.3 2.7 convolution_convert_fusion.3.do_ref
  323.1 21.9 %attention_back.2 = (bf16[448,1024]{1,0:T(8,128)(2,1)}, f32[128,1024]{1,0:T(8,128)}, bf16[128,1024]{1,0:T(8,128)(2,1)}, f32[128,128]{1,0:T(8,128)}) custom-call(s32[3]{0:T(128)} %pad_add_fusion.info_ref, bf16[448,1024]{1,0:T(8,128)(2,1)} %bitcast.76, bf16[448,1024]{1,0:T(8,128)(2,1)} %convolution_convert_fusion.3.do_ref, ...), custom_call_target="tpu_custom_call" | custom-call | flops 18790481920 | bytes 7340032 | tf_op jit(solution)/shard_map/attention_back/pallas_call | solution.py:484
  348.1 17.9 %collective-permute-start.42 = (bf16[224,4224]{1,0:T(8,128)(2,1)}, bf16[224,4224]{1,0:T(8,128)(2,1)}, u32[]{:S(2)}, u32[]{:S(2)}) collective-permute-start(bf16[224,4224]{1,0:T(8,128)(2,1)} %pad_maximum_fusion.2), channel_id=1, source_target_pairs={{0,1},{1,0},{2,3},{3,2},{4,5},{5,4},{6,7},{7,6},{8,9},{9,8},{10,11... | collective-permute-start | bytes 5677064 | tf_op jit(solution)/shard_map/ppermute | solution.py:48
  369.0 2.2 collective-permute-start.41
  371.2 4.0 convolution_convert_fusion.2.do_ref
  375.2 22.3 %attention_back.3 = (bf16[448,1024]{1,0:T(8,128)(2,1)}, f32[128,1024]{1,0:T(8,128)}, bf16[128,1024]{1,0:T(8,128)(2,1)}, f32[128,128]{1,0:T(8,128)}) custom-call(s32[3]{0:T(128)} %pad_add_fusion.info_ref, bf16[448,1024]{1,0:T(8,128)(2,1)} %bitcast.74, bf16[448,1024]{1,0:T(8,128)(2,1)} %convolution_convert_fusion.2.do_ref, ...), custom_call_target="tpu_custom_call" | custom-call | flops 18790481920 | bytes 7340032 | tf_op jit(solution)/shard_map/attention_back/pallas_call | solution.py:484
  407.0 18.2 %collective-permute-start.24 = (bf16[128,1024]{1,0:T(8,128)(2,1)}, bf16[128,1024]{1,0:T(8,128)(2,1)}, u32[]{:S(2)}, u32[]{:S(2)}) collective-permute-start(bf16[128,1024]{1,0:T(8,128)(2,1)} %get-tuple-element.114), channel_id=1, source_target_pairs={{0,1},{1,0},{2,3},{3,2},{4,5},{5,4},{6,7},{7,6},{8,9},{9,8},{10,11... | collective-permute-start | bytes 786440 | tf_op jit(solution)/shard_map/ppermute | solution.py:48
  425.3 5.4 fusion.13
  432.0 3.6 add_convert_fusion.5
  438.9 2.6 convolution_convert_fusion
  443.7 3.1 fusion.21
  447.9 2.6 multiply_reduce_fusion.1
  454.9 2.5 collective-permute-start.29
  457.5 4.4 fusion.14
  466.8 4.6 add_convert_fusion
  471.4 4.7 collective-permute-done.28
  479.5 3.0 collective-permute-start.31
  486.2 3.9 collective-permute-start.43
  490.1 16.0 %collective-permute-done.31 = bf16[56,1152]{0,1:T(8,128)(2,1)} collective-permute-done((bf16[56,1152]{0,1:T(8,128)(2,1)S(1)}, bf16[56,1152]{0,1:T(8,128)(2,1)}, u32[]{:S(2)}, u32[]{:S(2)}) %collective-permute-start.31) | collective-permute-done | bytes 129056 | tf_op jit(solution)/shard_map/ppermute | solution.py:116
  506.2 2.9 collective-permute-done.32
  509.1 28.5 %collective-permute-done.33 = bf16[56,1152]{0,1:T(8,128)(2,1)} collective-permute-done((bf16[56,1152]{0,1:T(8,128)(2,1)S(1)}, bf16[56,1152]{0,1:T(8,128)(2,1)}, u32[]{:S(2)}, u32[]{:S(2)}) %collective-permute-start.33) | collective-permute-done | bytes 129056 | tf_op jit(solution)/shard_map/ppermute | solution.py:116
  539.5 2.5 collective-permute-start.34
  550.6 2.8 unpack.1
  (381 shorter events, 119.7 us)
Async XLA Ops:
  7.2 62.5 %all-gather.3.cloned.1.call-start = ((), (), s32[]{:S(2)}) async-start(), calls=%async_computation.2 | async-start | bytes 1720320 | tf_op jit(solution)/shard_map/all_gather | solution.py:62
  19.9 3.4 collective-permute-start.9
  20.6 15.7 %collective-permute-start.1 = (bf16[56,1152]{1,0:T(8,128)(2,1)S(1)}, bf16[56,1152]{1,0:T(8,128)(2,1)S(1)}, u32[]{:S(2)}, u32[]{:S(2)}) collective-permute-start(bf16[56,1152]{1,0:T(8,128)(2,1)S(1)} %get-tuple-element.183), channel_id=1, source_target_pairs={{0,8},{8,0},{16,24},{24,16},{1,9},{9,1},{17,25},{25,17},{2,10},{10... | collective-permute-start | bytes 387080 | tf_op jit(solution)/shard_map/ppermute | solution.py:68
  20.7 15.6 %collective-permute-start.2 = (bf16[56,1152]{1,0:T(8,128)(2,1)S(1)}, bf16[56,1152]{1,0:T(8,128)(2,1)S(1)}, u32[]{:S(2)}, u32[]{:S(2)}) collective-permute-start(bf16[56,1152]{1,0:T(8,128)(2,1)S(1)} %get-tuple-element.183), channel_id=1, source_target_pairs={{0,16},{8,24},{16,0},{24,8},{1,17},{9,25},{17,1},{25,9},{2,18},{10... | collective-permute-start | bytes 387080 | tf_op jit(solution)/shard_map/ppermute | solution.py:68
  23.1 13.2 %collective-permute-start.3 = (bf16[56,1152]{1,0:T(8,128)(2,1)S(1)}, bf16[56,1152]{1,0:T(8,128)(2,1)S(1)}, u32[]{:S(2)}, u32[]{:S(2)}) collective-permute-start(bf16[56,1152]{1,0:T(8,128)(2,1)S(1)} %get-tuple-element.183), channel_id=1, source_target_pairs={{0,24},{8,16},{16,8},{24,0},{1,25},{9,17},{17,9},{25,1},{2,26},{10... | collective-permute-start | bytes 387080 | tf_op jit(solution)/shard_map/ppermute | solution.py:68
  25.2 79.9 %all-gather.5.cloned.1.call-start = ((), (), s32[]{:S(2)}) async-start(), calls=%async_computation.3 | async-start | bytes 2365440 | tf_op jit(solution)/shard_map/all_gather | solution.py:62
  34.3 5.4 collective-permute-start.13
  36.3 14.8 %collective-permute-start.4 = (bf16[224,1152]{1,0:T(8,128)(2,1)S(1)}, bf16[224,1152]{1,0:T(8,128)(2,1)S(1)}, u32[]{:S(2)}, u32[]{:S(2)}) collective-permute-start(bf16[224,1152]{1,0:T(8,128)(2,1)S(1)} %constant_dynamic-update-slice_fusion.5), channel_id=1, source_target_pairs={{0,4},{4,0},{1,5},{5,1},{2,6},{6,2},{3,7},{7,3},{8,12},{12,8},{9,1... | collective-permute-start | bytes 1548296 | tf_op jit(solution)/shard_map/ppermute | solution.py:48
  37.6 13.1 %collective-permute-start.5 = (bf16[224,1152]{1,0:T(8,128)(2,1)S(1)}, bf16[224,1152]{1,0:T(8,128)(2,1)S(1)}, u32[]{:S(2)}, u32[]{:S(2)}) collective-permute-start(bf16[224,1152]{1,0:T(8,128)(2,1)S(1)} %constant_dynamic-update-slice_fusion.5), channel_id=1, source_target_pairs={{0,1},{1,0},{2,3},{3,2},{4,5},{5,4},{6,7},{7,6},{8,9},{9,8},{10,11... | collective-permute-start | bytes 1548296 | tf_op jit(solution)/shard_map/ppermute | solution.py:48
  40.7 443.7 %reduce-scatter.5.cloned.1.call-start = ((), (), s32[]{:S(2)}) async-start(), calls=%async_computation.4 | async-start | bytes 1720320 | tf_op jit(solution)/shard_map/reduce_scatter | solution.py:111
  50.7 6.8 %collective-permute-start.6 = (bf16[112,1152]{1,0:T(8,128)(2,1)S(1)}, bf16[112,1152]{1,0:T(8,128)(2,1)S(1)}, u32[]{:S(2)}, u32[]{:S(2)}) collective-permute-start(bf16[112,1152]{1,0:T(8,128)(2,1)S(1)} %slice.474), channel_id=1, source_target_pairs={{0,4},{4,0},{1,5},{5,1},{2,6},{6,2},{3,7},{7,3},{8,12},{12,8},{9,1... | collective-permute-start | bytes 774152 | tf_op jit(solution)/shard_map/ppermute | solution.py:48
  51.2 7.1 %collective-permute-start.7 = (bf16[112,1152]{1,0:T(8,128)(2,1)S(1)}, bf16[112,1152]{1,0:T(8,128)(2,1)S(1)}, u32[]{:S(2)}, u32[]{:S(2)}) collective-permute-start(bf16[112,1152]{1,0:T(8,128)(2,1)S(1)} %slice.475), channel_id=1, source_target_pairs={{0,1},{1,0},{2,3},{3,2},{4,5},{5,4},{6,7},{7,6},{8,9},{9,8},{10,11... | collective-permute-start | bytes 774152 | tf_op jit(solution)/shard_map/ppermute | solution.py:48
  58.9 11.6 %collective-permute-start.8 = (bf16[896,1152]{1,0:T(8,128)(2,1)}, bf16[896,1152]{1,0:T(8,128)(2,1)}, u32[]{:S(2)}, u32[]{:S(2)}) collective-permute-start(bf16[896,1152]{1,0:T(8,128)(2,1)} %constant_dynamic-update-slice_fusion), channel_id=1, source_target_pairs={{0,2},{2,0},{1,3},{3,1},{4,6},{6,4},{5,7},{7,5},{8,10},{10,8},{9,1... | collective-permute-start | bytes 6193160 | tf_op jit(solution)/shard_map/ppermute | solution.py:48
  69.7 58.0 %collective-permute-start.11 = (bf16[224,3072]{1,0:T(8,128)(2,1)}, bf16[224,3072]{1,0:T(8,128)(2,1)}, u32[]{:S(2)}, u32[]{:S(2)}) collective-permute-start(bf16[224,3072]{1,0:T(8,128)(2,1)} %all-gather.3.cloned.1.call-done.zw), channel_id=1, source_target_pairs={{0,4},{4,0},{1,5},{5,1},{2,6},{6,2},{3,7},{7,3},{8,12},{12,8},{9,1... | collective-permute-start | bytes 4128776 | tf_op jit(solution)/shard_map/ppermute | solution.py:48
  74.7 13.4 %collective-permute-start.10 = (bf16[256,1024]{1,0:T(8,128)(2,1)S(1)}, bf16[256,1024]{1,0:T(8,128)(2,1)S(1)}, u32[]{:S(2)}, u32[]{:S(2)}) collective-permute-start(bf16[256,1024]{1,0:T(8,128)(2,1)S(1)} %pad_maximum_fusion.14), channel_id=1, source_target_pairs={{0,1},{1,0},{2,3},{3,2},{4,5},{5,4},{6,7},{7,6},{8,9},{9,8},{10,11... | collective-permute-start | bytes 1572872 | tf_op jit(solution)/shard_map/ppermute | solution.py:48
  88.9 38.8 %collective-permute-start.12 = (bf16[224,3072]{1,0:T(8,128)(2,1)}, bf16[224,3072]{1,0:T(8,128)(2,1)}, u32[]{:S(2)}, u32[]{:S(2)}) collective-permute-start(bf16[224,3072]{1,0:T(8,128)(2,1)} %all-gather.3.cloned.1.call-done.zw), channel_id=1, source_target_pairs={{0,1},{1,0},{2,3},{3,2},{4,5},{5,4},{6,7},{7,6},{8,9},{9,8},{10,11... | collective-permute-start | bytes 4128776 | tf_op jit(solution)/shard_map/ppermute | solution.py:48
  105.2 47.8 %collective-permute-start.18 = (bf16[224,4224]{1,0:T(8,128)(2,1)}, bf16[224,4224]{1,0:T(8,128)(2,1)}, u32[]{:S(2)}, u32[]{:S(2)}) collective-permute-start(bf16[224,4224]{1,0:T(8,128)(2,1)} %all-gather.5.cloned.1.call-done.zw), channel_id=1, source_target_pairs={{0,4},{4,0},{1,5},{5,1},{2,6},{6,2},{3,7},{7,3},{8,12},{12,8},{9,1... | collective-permute-start | bytes 5677064 | tf_op jit(solution)/shard_map/ppermute | solution.py:48
  105.3 60.0 %collective-permute-start.19 = (bf16[224,4224]{1,0:T(8,128)(2,1)}, bf16[224,4224]{1,0:T(8,128)(2,1)}, u32[]{:S(2)}, u32[]{:S(2)}) collective-permute-start(bf16[224,4224]{1,0:T(8,128)(2,1)} %all-gather.5.cloned.1.call-done.zw), channel_id=1, source_target_pairs={{0,1},{1,0},{2,3},{3,2},{4,5},{5,4},{6,7},{7,6},{8,9},{9,8},{10,11... | collective-permute-start | bytes 5677064 | tf_op jit(solution)/shard_map/ppermute | solution.py:48
  121.0 49.2 %collective-permute-start.15 = (bf16[1024,896]{1,0:T(8,128)(2,1)S(1)}, bf16[1024,896]{1,0:T(8,128)(2,1)}, u32[]{:S(2)}, u32[]{:S(2)}) collective-permute-start(bf16[1024,896]{1,0:T(8,128)(2,1)S(1)} %fusion.12.cm), channel_id=1, source_target_pairs={{0,2},{2,0},{1,3},{3,1},{4,6},{6,4},{5,7},{7,5},{8,10},{10,8},{9,1... | collective-permute-start | bytes 5505032 | tf_op jit(solution)/shard_map/ppermute | solution.py:48
  149.9 30.0 %collective-permute-start.14 = (bf16[1024,896]{1,0:T(8,128)(2,1)S(1)}, bf16[1024,896]{1,0:T(8,128)(2,1)}, u32[]{:S(2)}, u32[]{:S(2)}) collective-permute-start(bf16[1024,896]{1,0:T(8,128)(2,1)S(1)} %multiply_convert_fusion.xm), channel_id=1, source_target_pairs={{0,2},{2,0},{1,3},{3,1},{4,6},{6,4},{5,7},{7,5},{8,10},{10,8},{9,1... | collective-permute-start | bytes 5505032 | tf_op jit(solution)/shard_map/ppermute | solution.py:48
  152.9 17.3 %collective-permute-start.16 = (bf16[112,3072]{1,0:T(8,128)(2,1)S(1)}, bf16[112,3072]{1,0:T(8,128)(2,1)S(1)}, u32[]{:S(2)}, u32[]{:S(2)}) collective-permute-start(bf16[112,3072]{1,0:T(8,128)(2,1)S(1)} %slice.415), channel_id=1, source_target_pairs={{0,4},{4,0},{1,5},{5,1},{2,6},{6,2},{3,7},{7,3},{8,12},{12,8},{9,1... | collective-permute-start | bytes 2064392 | tf_op jit(solution)/shard_map/ppermute | solution.py:48
  153.0 26.1 %collective-permute-start.17 = (bf16[112,3072]{1,0:T(8,128)(2,1)S(1)}, bf16[112,3072]{1,0:T(8,128)(2,1)S(1)}, u32[]{:S(2)}, u32[]{:S(2)}) collective-permute-start(bf16[112,3072]{1,0:T(8,128)(2,1)S(1)} %slice.416), channel_id=1, source_target_pairs={{0,1},{1,0},{2,3},{3,2},{4,5},{5,4},{6,7},{7,6},{8,9},{9,8},{10,11... | collective-permute-start | bytes 2064392 | tf_op jit(solution)/shard_map/ppermute | solution.py:48
  167.5 61.9 %collective-permute-start.20 = (bf16[112,4224]{1,0:T(8,128)(2,1)}, bf16[112,4224]{1,0:T(8,128)(2,1)}, u32[]{:S(2)}, u32[]{:S(2)}) collective-permute-start(bf16[112,4224]{1,0:T(8,128)(2,1)} %slice.417), channel_id=1, source_target_pairs={{0,4},{4,0},{1,5},{5,1},{2,6},{6,2},{3,7},{7,3},{8,12},{12,8},{9,1... | collective-permute-start | bytes 2838536 | tf_op jit(solution)/shard_map/ppermute | solution.py:48
  170.2 59.2 %collective-permute-start.21 = (bf16[112,4224]{1,0:T(8,128)(2,1)}, bf16[112,4224]{1,0:T(8,128)(2,1)}, u32[]{:S(2)}, u32[]{:S(2)}) collective-permute-start(bf16[112,4224]{1,0:T(8,128)(2,1)} %slice.418), channel_id=1, source_target_pairs={{0,1},{1,0},{2,3},{3,2},{4,5},{5,4},{6,7},{7,6},{8,9},{9,8},{10,11... | collective-permute-start | bytes 2838536 | tf_op jit(solution)/shard_map/ppermute | solution.py:48
  227.1 80.8 %collective-permute-start.35 = (bf16[112,3072]{1,0:T(8,128)(2,1)}, bf16[112,3072]{1,0:T(8,128)(2,1)}, u32[]{:S(2)}, u32[]{:S(2)}) collective-permute-start(bf16[112,3072]{1,0:T(8,128)(2,1)} %get-tuple-element.125), channel_id=1, source_target_pairs={{0,4},{4,0},{1,5},{5,1},{2,6},{6,2},{3,7},{7,3},{8,12},{12,8},{9,1... | collective-permute-start | bytes 2064392 | tf_op jit(solution)/shard_map/ppermute | solution.py:48
  227.7 80.7 %collective-permute-start.36 = (bf16[112,3072]{1,0:T(8,128)(2,1)}, bf16[112,3072]{1,0:T(8,128)(2,1)}, u32[]{:S(2)}, u32[]{:S(2)}) collective-permute-start(bf16[112,3072]{1,0:T(8,128)(2,1)} %get-tuple-element.126), channel_id=1, source_target_pairs={{0,1},{1,0},{2,3},{3,2},{4,5},{5,4},{6,7},{7,6},{8,9},{9,8},{10,11... | collective-permute-start | bytes 2064392 | tf_op jit(solution)/shard_map/ppermute | solution.py:48
  300.3 14.6 %collective-permute-start.23 = (bf16[1024,896]{1,0:T(8,128)(2,1)S(1)}, bf16[1024,896]{1,0:T(8,128)(2,1)S(1)}, u32[]{:S(2)}, u32[]{:S(2)}) collective-permute-start(bf16[1024,896]{1,0:T(8,128)(2,1)S(1)} %add_convert_fusion.2), channel_id=1, source_target_pairs={{0,2},{2,0},{1,3},{3,1},{4,6},{6,4},{5,7},{7,5},{8,10},{10,8},{9,1... | collective-permute-start | bytes 5505032 | tf_op jit(solution)/shard_map/ppermute | solution.py:48
  303.1 41.9 %collective-permute-start.39 = (bf16[112,4224]{1,0:T(8,128)(2,1)}, bf16[112,4224]{1,0:T(8,128)(2,1)}, u32[]{:S(2)}, u32[]{:S(2)}) collective-permute-start(bf16[112,4224]{1,0:T(8,128)(2,1)} %get-tuple-element.134), channel_id=1, source_target_pairs={{0,4},{4,0},{1,5},{5,1},{2,6},{6,2},{3,7},{7,3},{8,12},{12,8},{9,1... | collective-permute-start | bytes 2838536 | tf_op jit(solution)/shard_map/ppermute | solution.py:48
  304.0 41.0 %collective-permute-start.40 = (bf16[112,4224]{1,0:T(8,128)(2,1)}, bf16[112,4224]{1,0:T(8,128)(2,1)}, u32[]{:S(2)}, u32[]{:S(2)}) collective-permute-start(bf16[112,4224]{1,0:T(8,128)(2,1)} %get-tuple-element.135), channel_id=1, source_target_pairs={{0,1},{1,0},{2,3},{3,2},{4,5},{5,4},{6,7},{7,6},{8,9},{9,8},{10,11... | collective-permute-start | bytes 2838536 | tf_op jit(solution)/shard_map/ppermute | solution.py:48
  307.9 99.1 %collective-permute-start.22 = (bf16[1024,896]{1,0:T(8,128)(2,1)}, bf16[1024,896]{1,0:T(8,128)(2,1)}, u32[]{:S(2)}, u32[]{:S(2)}) collective-permute-start(bf16[1024,896]{1,0:T(8,128)(2,1)} %add_convert_fusion.4), channel_id=1, source_target_pairs={{0,2},{2,0},{1,3},{3,1},{4,6},{6,4},{5,7},{7,5},{8,10},{10,8},{9,1... | collective-permute-start | bytes 5505032 | tf_op jit(solution)/shard_map/ppermute | solution.py:48
  310.9 119.8 %collective-permute-start.38 = (bf16[224,3072]{1,0:T(8,128)(2,1)}, bf16[224,3072]{1,0:T(8,128)(2,1)}, u32[]{:S(2)}, u32[]{:S(2)}) collective-permute-start(bf16[224,3072]{1,0:T(8,128)(2,1)} %pad_maximum_fusion.5), channel_id=1, source_target_pairs={{0,1},{1,0},{2,3},{3,2},{4,5},{5,4},{6,7},{7,6},{8,9},{9,8},{10,11... | collective-permute-start | bytes 4128776 | tf_op jit(solution)/shard_map/ppermute | solution.py:48
  314.9 117.1 %collective-permute-start.37 = (bf16[224,3072]{1,0:T(8,128)(2,1)}, bf16[224,3072]{1,0:T(8,128)(2,1)}, u32[]{:S(2)}, u32[]{:S(2)}) collective-permute-start(bf16[224,3072]{1,0:T(8,128)(2,1)} %pad_maximum_fusion.4), channel_id=1, source_target_pairs={{0,4},{4,0},{1,5},{5,1},{2,6},{6,2},{3,7},{7,3},{8,12},{12,8},{9,1... | collective-permute-start | bytes 4128776 | tf_op jit(solution)/shard_map/ppermute | solution.py:48
  348.1 113.8 %collective-permute-start.42 = (bf16[224,4224]{1,0:T(8,128)(2,1)}, bf16[224,4224]{1,0:T(8,128)(2,1)}, u32[]{:S(2)}, u32[]{:S(2)}) collective-permute-start(bf16[224,4224]{1,0:T(8,128)(2,1)} %pad_maximum_fusion.2), channel_id=1, source_target_pairs={{0,1},{1,0},{2,3},{3,2},{4,5},{5,4},{6,7},{7,6},{8,9},{9,8},{10,11... | collective-permute-start | bytes 5677064 | tf_op jit(solution)/shard_map/ppermute | solution.py:48
  369.0 92.9 %collective-permute-start.41 = (bf16[224,4224]{1,0:T(8,128)(2,1)}, bf16[224,4224]{1,0:T(8,128)(2,1)}, u32[]{:S(2)}, u32[]{:S(2)}) collective-permute-start(bf16[224,4224]{1,0:T(8,128)(2,1)} %pad_maximum_fusion.1), channel_id=1, source_target_pairs={{0,4},{4,0},{1,5},{5,1},{2,6},{6,2},{3,7},{7,3},{8,12},{12,8},{9,1... | collective-permute-start | bytes 5677064 | tf_op jit(solution)/shard_map/ppermute | solution.py:48
  407.0 39.8 %collective-permute-start.24 = (bf16[128,1024]{1,0:T(8,128)(2,1)}, bf16[128,1024]{1,0:T(8,128)(2,1)}, u32[]{:S(2)}, u32[]{:S(2)}) collective-permute-start(bf16[128,1024]{1,0:T(8,128)(2,1)} %get-tuple-element.114), channel_id=1, source_target_pairs={{0,1},{1,0},{2,3},{3,2},{4,5},{5,4},{6,7},{7,6},{8,9},{9,8},{10,11... | collective-permute-start | bytes 786440 | tf_op jit(solution)/shard_map/ppermute | solution.py:48
  430.6 7.1 %collective-permute-start.25 = (bf16[128,1024]{1,0:T(8,128)(2,1)}, bf16[128,1024]{1,0:T(8,128)(2,1)}, u32[]{:S(2)}, u32[]{:S(2)}) collective-permute-start(bf16[128,1024]{1,0:T(8,128)(2,1)} %get-tuple-element.120), channel_id=1, source_target_pairs={{0,1},{1,0},{2,3},{3,2},{4,5},{5,4},{6,7},{7,6},{8,9},{9,8},{10,11... | collective-permute-start | bytes 786440 | tf_op jit(solution)/shard_map/ppermute | solution.py:48
  435.6 108.9 %reduce-scatter.7.cloned.1.call-start = ((), (), s32[]{:S(2)}) async-start(), calls=%async_computation.5 | async-start | bytes 2365440
  441.7 10.5 %collective-permute-start.26 = (bf16[896,1024]{0,1:T(8,128)(2,1)S(1)}, bf16[896,1024]{0,1:T(8,128)(2,1)S(1)}, u32[]{:S(2)}, u32[]{:S(2)}) collective-permute-start(bf16[896,1024]{0,1:T(8,128)(2,1)S(1)} %pad_maximum_fusion.3), channel_id=1, source_target_pairs={{0,2},{2,0},{1,3},{3,1},{4,6},{6,4},{5,7},{7,5},{8,10},{10,8},{9,1... | collective-permute-start | bytes 5505032 | tf_op jit(solution)/shard_map/ppermute | solution.py:48
  453.3 8.6 %collective-permute-start.27 = (bf16[112,1152]{0,1:T(8,128)(2,1)S(1)}, bf16[112,1152]{0,1:T(8,128)(2,1)S(1)}, u32[]{:S(2)}, u32[]{:S(2)}) collective-permute-start(bf16[112,1152]{0,1:T(8,128)(2,1)S(1)} %get-tuple-element.191), channel_id=1, source_target_pairs={{0,1},{1,0},{2,3},{3,2},{4,5},{5,4},{6,7},{7,6},{8,9},{9,8},{10,11... | collective-permute-start | bytes 774152 | tf_op jit(solution)/shard_map/ppermute | solution.py:48
  454.9 8.7 %collective-permute-start.29 = (bf16[112,1152]{0,1:T(8,128)(2,1)S(1)}, bf16[112,1152]{0,1:T(8,128)(2,1)S(1)}, u32[]{:S(2)}, u32[]{:S(2)}) collective-permute-start(bf16[112,1152]{0,1:T(8,128)(2,1)S(1)} %get-tuple-element.190), channel_id=1, source_target_pairs={{0,4},{4,0},{1,5},{5,1},{2,6},{6,2},{3,7},{7,3},{8,12},{12,8},{9,1... | collective-permute-start | bytes 774152 | tf_op jit(solution)/shard_map/ppermute | solution.py:48
  464.5 11.6 %collective-permute-start.28 = (bf16[224,1152]{1,0:T(8,128)(2,1)S(1)}, bf16[224,1152]{1,0:T(8,128)(2,1)S(1)}, u32[]{:S(2)}, u32[]{:S(2)}) collective-permute-start(bf16[224,1152]{1,0:T(8,128)(2,1)S(1)} %copy.192), channel_id=1, source_target_pairs={{0,4},{4,0},{1,5},{5,1},{2,6},{6,2},{3,7},{7,3},{8,12},{12,8},{9,1... | collective-permute-start | bytes 1548296 | tf_op jit(solution)/shard_map/ppermute | solution.py:48
  466.4 11.0 %collective-permute-start.30 = (bf16[224,1152]{1,0:T(8,128)(2,1)S(1)}, bf16[224,1152]{1,0:T(8,128)(2,1)S(1)}, u32[]{:S(2)}, u32[]{:S(2)}) collective-permute-start(bf16[224,1152]{1,0:T(8,128)(2,1)S(1)} %copy.194), channel_id=1, source_target_pairs={{0,1},{1,0},{2,3},{3,2},{4,5},{5,4},{6,7},{7,6},{8,9},{9,8},{10,11... | collective-permute-start | bytes 1548296 | tf_op jit(solution)/shard_map/ppermute | solution.py:48
  479.5 26.7 %collective-permute-start.31 = (bf16[56,1152]{0,1:T(8,128)(2,1)S(1)}, bf16[56,1152]{0,1:T(8,128)(2,1)}, u32[]{:S(2)}, u32[]{:S(2)}) collective-permute-start(bf16[56,1152]{0,1:T(8,128)(2,1)S(1)} %get-tuple-element.204), channel_id=1, source_target_pairs={{0,8},{8,0},{16,24},{24,16},{1,9},{9,1},{17,25},{25,17},{2,10},{10... | collective-permute-start | bytes 387080 | tf_op jit(solution)/shard_map/ppermute | solution.py:116
  482.5 26.6 %collective-permute-start.32 = (bf16[56,1152]{0,1:T(8,128)(2,1)S(1)}, bf16[56,1152]{0,1:T(8,128)(2,1)}, u32[]{:S(2)}, u32[]{:S(2)}) collective-permute-start(bf16[56,1152]{0,1:T(8,128)(2,1)S(1)} %get-tuple-element.206), channel_id=1, source_target_pairs={{0,16},{8,24},{16,0},{24,8},{1,17},{9,25},{17,1},{25,9},{2,18},{10... | collective-permute-start | bytes 387080 | tf_op jit(solution)/shard_map/ppermute | solution.py:116
  484.2 53.4 %collective-permute-start.33 = (bf16[56,1152]{0,1:T(8,128)(2,1)S(1)}, bf16[56,1152]{0,1:T(8,128)(2,1)}, u32[]{:S(2)}, u32[]{:S(2)}) collective-permute-start(bf16[56,1152]{0,1:T(8,128)(2,1)S(1)} %get-tuple-element.205), channel_id=1, source_target_pairs={{0,24},{8,16},{16,8},{24,0},{1,25},{9,17},{17,9},{25,1},{2,26},{10... | collective-permute-start | bytes 387080 | tf_op jit(solution)/shard_map/ppermute | solution.py:116
  486.2 63.5 %collective-permute-start.43 = (f32[28,3072]{1,0:T(8,128)S(1)}, f32[28,3072]{1,0:T(8,128)S(1)}, u32[]{:S(2)}, u32[]{:S(2)}) collective-permute-start(f32[28,3072]{1,0:T(8,128)S(1)} %get-tuple-element.196), channel_id=1, source_target_pairs={{0,2},{2,0},{1,3},{3,1},{4,6},{6,4},{5,7},{7,5},{8,10},{10,8},{9,1... | collective-permute-start | bytes 1032200 | tf_op jit(solution)/shard_map/ppermute | solution.py:48
  539.5 3.5 collective-permute-start.34
  546.7 3.0 collective-permute-start.44
  (61 other events, 619.1 us)
Sparse Core Ops, SparseCore 0:
  25.3 35.4 all-gather.2
  63.0 40.8 all-gather.4
  435.8 35.9 reduce-scatter.4
  474.0 66.6 reduce-scatter.6

commit v2 on v1

--- a/solution.py
+++ b/solution.py
@@ -98,16 +98,19 @@
 
 def sum_beside(pieces, got, vectors=0):
     half = pieces[3].shape[0]
-    xs = jnp.concatenate([pieces[1][:half], rounded(f32(pieces[1][half:]) + f32(got[1]), vectors)], 0)
-    ys = jnp.concatenate([rounded(f32(pieces[2][:half]) + f32(got[0]), vectors), pieces[2][half:]], 0)
+    xs = rounded(f32(pieces[1]) + jnp.pad(f32(got[1]), ((half, 0), (0, 0))), vectors)
+    ys = rounded(f32(pieces[2]) + jnp.pad(f32(got[0]), ((0, half), (0, 0))), vectors)
     return swap(xs, "xx"), swap(ys, "ctx")
 
 
-def sum_along_z(pieces, got, vectors=0):
+def sum_own(pieces, got, vectors=0):
+    return rounded(f32(pieces[0]) + f32(got[0]) + f32(got[1]), vectors)
+
+
+def sum_along_z(zs, direct):
     count = lax.axis_size("zz")
     me = lax.axis_index("zz")
-    zs = rounded(f32(pieces[0]) + f32(got[0]) + f32(got[1]), vectors)
-    if not vectors:
+    if not direct:
         return [lax.optimization_barrier(lax.psum_scatter(zs, "zz", scatter_dimension=0, tiled=True))]
     rows = zs.shape[0] // count
     parts = [lax.dynamic_slice(zs, (me * rows, 0), (rows, zs.shape[1]))]
@@ -680,23 +683,26 @@
         bf(lax.dot_general(w_all[:, o0:e0], grad_attn, (((0,), (1,)), ((), ())), preferred_element_type=F32)) for w_all in w_side
     ]
 
-    lows, d_sums = [], []
     back = [None, None]
+    lows, kv_got = [], [None, None]
     for s in range(2):
         do = grad_mixed[s]
         if s == 1:
-            do = after(do, back[0][0])
+            zs = []
             for i in range(n - 1):
-                got_b[i] = after(got_b[i], back[0][0])
-                got_z[i] = sum_along_z(results[i][4:], got_b[i])
+                zs.append(sum_own(results[i][4:], after(got_b[i], back[0][0])))
+                got_z[i] = sum_along_z(zs[i], False)
             got_d[n - 1] = after(got_d[n - 1], back[0][0])
             got_b[n - 1] = sum_beside(results[n - 1][4:], got_d[n - 1])
+            do = after(do, back[0][0], *zs)
         back[s] = attn_bwd(info, queries[s], do, attended[s], rest[s], lse[s], keys_values[s], kv_rem[s], table, table_rem, bq, bk)
-    got_b[n - 1] = after(got_b[n - 1], back[1][0])
-    got_z[n - 1] = sum_along_z(results[n - 1][4:], got_b[n - 1])
+        kv_got[s] = swap(back[s][2], "ctx")
+    zs_last = sum_own(results[n - 1][4:], after(got_b[n - 1], back[1][0]))
+    got_z[n - 1] = sum_along_z(zs_last, False)
+    back[1] = after(back[1], zs_last)
     for s in range(2):
         query_low, d_loc, d_rem, _ = back[s]
-        kv_low = bf(d_loc + f32(swap(d_rem, "ctx")))
+        kv_low = bf(d_loc + f32(kv_got[s]))
         lows.append(jnp.concatenate([query_low, kv_low], axis=0))
 
     out_sum = total(0, 1)
@@ -735,7 +741,7 @@
     bounds = [0, quarter, 2 * quarter, 3 * quarter, 3 * quarter + quarter // 2, width]
     g_pieces = [g_sum[a:b] for a, b in zip(bounds, bounds[1:])]
     g_got = sum_beside(g_pieces, sum_diagonal(g_pieces), EXTRA)
-    a_mine, a_theirs = sum_pair(sum_along_z(g_pieces, g_got, EXTRA))
+    a_mine, a_theirs = sum_pair(sum_along_z(sum_own(g_pieces, g_got, EXTRA), True))
 
     def natural_cols(a, b):
         lo, hi = a_mine[:, a:b], a_theirs[:, a:b]

time: 567 us -> 542 us (0.956)
  waiting for transfers between devices: 84.8 us -> 58 us
  matrix products: 57.7 us -> 65.1 us
    ppermute x3, waiting for transfers between devices: 47.4 us -> 20.1 us  [sum_along_z(): parts.append(lax.ppermute(part, 'zz', [(i, i ^ j) for i in range(count)]))]
    concatenate x6 -> x0, other arithmetic: 5.81 us -> none  [the longest x3 2.94 us: sum_beside(): jnp.concatenate([pieces[1][:half], rounded(f32(pieces[1][half:]) + f32(go...]
  transfers between devices with their start and end apart: 49 -> 49, of which waited for: 12 -> 11; matrix products, arithmetic and copies ran while one was open for 26% -> 28% of each run, Pallas kernels for 34% -> 36%
where the time goes in v2:
time: 542 us; the launch traced here: 534 us
  Pallas kernels  195 us (36%)
  starting transfers between devices  104 us (19%)
  matrix products  65.1 us (12%)
  other arithmetic  58.8 us (11%)
  waiting for transfers between devices  58 us (11%)
  local copies, waits for them, and re-layouts  37.8 us (7%)
  between operations  15.3 us (3%)
    pallas_call x2, Pallas kernels, mlp(): pl.pallas_call(functools.partial(mlp_kernel, last_t, rows), grid=(steps,)...  116 us
    ppermute x39, starting transfers between devices, swap(): return lax.ppermute(v, axis, SWAP)  95.5 us
    pallas_call x2, Pallas kernels, attn_bwd(): pl.pallas_call(functools.partial(attn_bwd_kernel, bk), grid=(blocks,), in...  44.7 us
    ppermute x39, waiting for transfers between devices, swap(): return lax.ppermute(v, axis, SWAP)  37.8 us
    convert_element_type x26, other arithmetic, bf(): return v.astype(BF16)  33.6 us
    pallas_call x2, Pallas kernels, attn_fwd(): pl.pallas_call(functools.partial(attn_fwd_kernel, bk), grid=(blocks,), in...  29.4 us
    ppermute x3, waiting for transfers between devices, sum_along_z(): parts.append(lax.ppermute(part, 'zz', [(i, i ^ j) for i in range(count)]))  20.1 us
    dot_general x2, matrix products, nt(): lax.dot_general(a, b, (((1,), (1,)), ((), ())), preferred_element_type=F32)  13.3 us
  transfers between devices with their start and end apart: 49, of which 11 were waited for; matrix products, arithmetic and copies ran while one was open for 28% of the time, Pallas kernels for 36%

profile of v2, /device:TPU:9, one launch (start us, length us, event | category | flops | bytes accessed | tf_op | source)
XLA Modules:
  0.0 533.8 jit_solution(3290787861310676272)
XLA Ops:
  21.4 2.5 collective-permute-start.2
  26.0 4.0 multiply_reduce_fusion.5
  29.9 5.1 copy.176
  42.5 9.8 %collective-permute-done.5 = bf16[224,1152]{1,0:T(8,128)(2,1)S(1)} collective-permute-done((bf16[224,1152]{1,0:T(8,128)(2,1)S(1)}, bf16[224,1152]{1,0:T(8,128)(2,1)S(1)}, u32[]{:S(2)}, u32[]{:S(2)}) %collective-permute-start.5) | collective-permute-done | bytes 516128 | tf_op jit(solution)/shard_map/ppermute | solution.py:48
  55.7 3.5 collective-permute-done.6
  66.3 2.4 multiply_convert_fusion.1
  68.7 2.3 convolution_add_fusion.4
  79.0 2.4 convolution_add_fusion.1
  84.4 5.4 %collective-permute-done.10 = bf16[256,1024]{1,0:T(8,128)(2,1)S(1)} collective-permute-done((bf16[256,1024]{1,0:T(8,128)(2,1)S(1)}, bf16[256,1024]{1,0:T(8,128)(2,1)S(1)}, u32[]{:S(2)}, u32[]{:S(2)}) %collective-permute-start.10) | collective-permute-done | bytes 524320 | tf_op jit(solution)/shard_map/ppermute | solution.py:48
  91.9 14.8 %attention.2 = (bf16[448,1024]{1,0:T(8,128)(2,1)}, bf16[448,1024]{1,0:T(8,128)(2,1)}, f32[4,1,1792]{2,1,0:T(1,128)}) custom-call(s32[3]{0:T(128)} %pad_add_fusion.info_ref, bf16[448,1024]{1,0:T(8,128)(2,1)} %bitcast.75, bf16[128,1024]{1,0:T(8,128)(2,1)} %pad_maximum_fusion.14.loc_ref, bf16[128,1024]{1,0:T(8,128)(2,1)} %get-tuple-element.214.rem_ref), custom_call_target="tpu_custom_call" | custom-call | flops 7516192768 | bytes 3670016 | tf_op jit(solution)/shard_map/attention/pallas_call | solution.py:385
  106.8 12.0 %collective-permute-start.19 = (bf16[224,4224]{1,0:T(8,128)(2,1)}, bf16[224,4224]{1,0:T(8,128)(2,1)}, u32[]{:S(2)}, u32[]{:S(2)}) collective-permute-start(bf16[224,4224]{1,0:T(8,128)(2,1)} %all-gather.5.cloned.1.call-done.zw), channel_id=1, source_target_pairs={{0,1},{1,0},{2,3},{3,2},{4,5},{5,4},{6,7},{7,6},{8,9},{9,8},{10,11... | collective-permute-start | bytes 5677064 | tf_op jit(solution)/shard_map/ppermute | solution.py:48
  118.9 3.8 fusion.12.cm
  124.6 3.5 fusion.32
  128.1 14.6 %attention.3 = (bf16[448,1024]{1,0:T(8,128)(2,1)}, bf16[448,1024]{1,0:T(8,128)(2,1)}, f32[4,1,1792]{2,1,0:T(1,128)}) custom-call(s32[3]{0:T(128)} %pad_add_fusion.info_ref, bf16[448,1024]{1,0:T(8,128)(2,1)} %bitcast.73, bf16[128,1024]{1,0:T(8,128)(2,1)} %pad_maximum_fusion.15.loc_ref, bf16[128,1024]{1,0:T(8,128)(2,1)} %get-tuple-element.213.rem_ref), custom_call_target="tpu_custom_call" | custom-call | flops 7516192768 | bytes 3670016 | tf_op jit(solution)/shard_map/attention/pallas_call | solution.py:385
  142.7 5.7 %multiply_reduce_fusion.4 = (f32[1024]{0:T(1024)S(1)}, f32[1024,896]{1,0:T(8,128)S(1)}) fusion(bf16[448,1024]{1,0:T(8,128)(2,1)} %get-tuple-element.99.o_ref, bf16[896,1152]{1,0:T(8,128)(2,1)} %collective-permute-done.8, f32[1024,896]{1,0:T(8,128)} %copy.176, f32[1024,896]{1,0:T(8,128)} %fusion.32), kind=kOutput, calls=%fused_computation.15 | convolution fusion | flops 825752576 | bytes 12849152 | tf_op jit(solution)/shard_map/dot_general | solution.py:654
  153.5 11.8 %collective-permute-start.17 = (bf16[112,3072]{1,0:T(8,128)(2,1)S(1)}, bf16[112,3072]{1,0:T(8,128)(2,1)S(1)}, u32[]{:S(2)}, u32[]{:S(2)}) collective-permute-start(bf16[112,3072]{1,0:T(8,128)(2,1)S(1)} %slice.380), channel_id=1, source_target_pairs={{0,1},{1,0},{2,3},{3,2},{4,5},{5,4},{6,7},{7,6},{8,9},{9,8},{10,11... | collective-permute-start | bytes 2064392 | tf_op jit(solution)/shard_map/ppermute | solution.py:48
  166.7 2.2 slice.381
  171.2 9.7 %collective-permute-done.17.bw = bf16[112,3072]{1,0:T(8,128)(2,1)S(1)} collective-permute-done((bf16[112,3072]{1,0:T(8,128)(2,1)S(1)}, bf16[112,3072]{1,0:T(8,128)(2,1)S(1)}, u32[]{:S(2)}, u32[]{:S(2)}) %collective-permute-start.17) | collective-permute-done | bytes 688160 | tf_op jit(solution)/shard_map/ppermute | solution.py:48
  181.8 47.1 %feed_forward.2 = (bf16[1024,896]{1,0:T(8,128)(2,1)}, bf16[1024,896]{1,0:T(8,128)(2,1)}, bf16[1024,896]{1,0:T(8,128)(2,1)}, bf16[1024,896]{1,0:T(8,128)(2,1)}, b...) custom-call(bf16[1024,896]{1,0:T(8,128)(2,1)} %copy-done.22, ...), custom_call_target="tpu_custom_call" | custom-call | flops 33822867456 | bytes 11010048 | tf_op jit(solution)/shard_map/feed_forward/pallas_call | solution.py:289
  231.2 68.8 %feed_forward.3 = (bf16[1024,896]{1,0:T(8,128)(2,1)}, bf16[1024,896]{1,0:T(8,128)(2,1)}, bf16[1024,896]{1,0:T(8,128)(2,1)}, bf16[1024,896]{1,0:T(8,128)(2,1)}, b...) custom-call(bf16[1024,896]{1,0:T(8,128)(2,1)} %copy-done.22, ...), custom_call_target="tpu_custom_call" | custom-call | flops 46506442752 | bytes 15138816 | tf_op jit(solution)/shard_map/feed_forward/pallas_call | solution.py:289
  307.2 2.6 add_convert_fusion.8
  311.4 2.4 add_convert_fusion.9
  316.1 3.1 fusion.87
  319.2 2.7 convolution_convert_fusion.3.do_ref
  321.9 22.4 %attention_back.2 = (bf16[448,1024]{1,0:T(8,128)(2,1)}, f32[128,1024]{1,0:T(8,128)}, bf16[128,1024]{1,0:T(8,128)(2,1)}, f32[128,128]{1,0:T(8,128)}) custom-call(s32[3]{0:T(128)} %pad_add_fusion.info_ref, bf16[448,1024]{1,0:T(8,128)(2,1)} %bitcast.76, bf16[448,1024]{1,0:T(8,128)(2,1)} %convolution_convert_fusion.3.do_ref, ...), custom_call_target="tpu_custom_call" | custom-call | flops 18790481920 | bytes 7340032 | tf_op jit(solution)/shard_map/attention_back/pallas_call | solution.py:487
  344.4 2.8 add_convert_fusion.1
  347.3 17.5 %collective-permute-start.32 = (bf16[224,4224]{1,0:T(8,128)(2,1)}, bf16[224,4224]{1,0:T(8,128)(2,1)}, u32[]{:S(2)}, u32[]{:S(2)}) collective-permute-start(bf16[224,4224]{1,0:T(8,128)(2,1)} %add_convert_fusion.1), channel_id=1, source_target_pairs={{0,1},{1,0},{2,3},{3,2},{4,5},{5,4},{6,7},{7,6},{8,9},{9,8},{10,11... | collective-permute-start | bytes 5677064 | tf_op jit(solution)/shard_map/ppermute | solution.py:48
  364.8 2.9 add_convert_fusion.2
  367.7 2.3 collective-permute-start.31
  370.3 3.2 convolution_convert_fusion.5
  374.6 3.2 convolution_convert_fusion.4
  377.8 4.1 convolution_convert_fusion.2.do_ref
  382.0 5.3 fusion.13
  387.3 3.6 add_convert_fusion.7
  391.0 22.2 %attention_back.3 = (bf16[448,1024]{1,0:T(8,128)(2,1)}, f32[128,1024]{1,0:T(8,128)}, bf16[128,1024]{1,0:T(8,128)(2,1)}, f32[128,128]{1,0:T(8,128)}) custom-call(s32[3]{0:T(128)} %pad_add_fusion.info_ref, bf16[448,1024]{1,0:T(8,128)(2,1)} %bitcast.74, bf16[448,1024]{1,0:T(8,128)(2,1)} %convolution_convert_fusion.2.do_ref, ...), custom_call_target="tpu_custom_call" | custom-call | flops 18790481920 | bytes 7340032 | tf_op jit(solution)/shard_map/attention_back/pallas_call | solution.py:487
  413.2 18.9 %collective-permute-start.33 = (bf16[128,1024]{1,0:T(8,128)(2,1)}, bf16[128,1024]{1,0:T(8,128)(2,1)}, u32[]{:S(2)}, u32[]{:S(2)}) collective-permute-start(bf16[128,1024]{1,0:T(8,128)(2,1)} %get-tuple-element.132), channel_id=1, source_target_pairs={{0,1},{1,0},{2,3},{3,2},{4,5},{5,4},{6,7},{7,6},{8,9},{9,8},{10,11... | collective-permute-start | bytes 786440 | tf_op jit(solution)/shard_map/ppermute | solution.py:48
  432.2 2.3 convolution_convert_fusion.1
  434.5 4.0 add_convert_fusion
  443.4 3.2 collective-permute-start.34
  447.8 3.5 fusion.21
  451.5 4.0 multiply_reduce_fusion.1
  459.9 7.1 %collective-permute-done.35 = bf16[112,1152]{0,1:T(8,128)(2,1)S(1)} collective-permute-done((bf16[112,1152]{0,1:T(8,128)(2,1)S(1)}, bf16[112,1152]{0,1:T(8,128)(2,1)S(1)}, u32[]{:S(2)}, u32[]{:S(2)}) %collective-permute-start.35) | collective-permute-done | bytes 258080 | tf_op jit(solution)/shard_map/ppermute | solution.py:48
  470.8 8.0 %fusion.14 = bf16[1024,896]{1,0:T(8,128)(2,1)} fusion(f32[1024,896]{1,0:T(8,128)} %copy.176, f32[1024,896]{1,0:T(8,128)} %get-tuple-element.187, f32[1024,896]{1,0:T(8,128)} %get-tuple-element.264, f32[1024]{0:T(1024)S(1)} %broadcast_multiply_fusion, f32[1024]{0:T(1024)S(1)} %copy-done.53, f32[896]{0:T(1024)S(1)} %copy-done.48, f32[1024]{0:T(1024)S(1)} %copy-done.51, ...), kind=kOutput, calls=%fused_computation.44 | convolution fusion | flops 1652310016 | bytes 12864512 | tf_op jit(solution)/shard_map/dot_general | solution.py:40
  483.6 5.1 collective-permute-start.40
  489.5 3.1 collective-permute-start.43
  492.5 13.8 %collective-permute-done.40 = bf16[56,1152]{0,1:T(8,128)(2,1)S(1)} collective-permute-done((bf16[56,1152]{0,1:T(8,128)(2,1)S(1)}, bf16[56,1152]{0,1:T(8,128)(2,1)S(1)}, u32[]{:S(2)}, u32[]{:S(2)}) %collective-permute-start.40) | collective-permute-done | bytes 129056 | tf_op jit(solution)/shard_map/ppermute | solution.py:119
  506.3 6.3 %collective-permute-done.41 = bf16[56,1152]{0,1:T(8,128)(2,1)S(1)} collective-permute-done((bf16[56,1152]{0,1:T(8,128)(2,1)S(1)}, bf16[56,1152]{0,1:T(8,128)(2,1)S(1)}, u32[]{:S(2)}, u32[]{:S(2)}) %collective-permute-start.41) | collective-permute-done | bytes 129056 | tf_op jit(solution)/shard_map/ppermute | solution.py:119
  524.2 2.8 unpack.1
  (385 shorter events, 104.4 us)
Async XLA Ops:
  7.2 64.2 %all-gather.3.cloned.1.call-start = ((), (), s32[]{:S(2)}) async-start(), calls=%async_computation.2 | async-start | bytes 1720320 | tf_op jit(solution)/shard_map/all_gather | solution.py:62
  20.6 3.4 collective-permute-start.9
  21.3 15.7 %collective-permute-start.1 = (bf16[56,1152]{1,0:T(8,128)(2,1)}, bf16[56,1152]{1,0:T(8,128)(2,1)}, u32[]{:S(2)}, u32[]{:S(2)}) collective-permute-start(bf16[56,1152]{1,0:T(8,128)(2,1)} %get-tuple-element.189), channel_id=1, source_target_pairs={{0,8},{8,0},{16,24},{24,16},{1,9},{9,1},{17,25},{25,17},{2,10},{10... | collective-permute-start | bytes 387080 | tf_op jit(solution)/shard_map/ppermute | solution.py:68
  21.4 16.5 %collective-permute-start.2 = (bf16[56,1152]{1,0:T(8,128)(2,1)}, bf16[56,1152]{1,0:T(8,128)(2,1)S(1)}, u32[]{:S(2)}, u32[]{:S(2)}) collective-permute-start(bf16[56,1152]{1,0:T(8,128)(2,1)} %get-tuple-element.189), channel_id=1, source_target_pairs={{0,16},{8,24},{16,0},{24,8},{1,17},{9,25},{17,1},{25,9},{2,18},{10... | collective-permute-start | bytes 387080 | tf_op jit(solution)/shard_map/ppermute | solution.py:68
  23.8 14.1 %collective-permute-start.3 = (bf16[56,1152]{1,0:T(8,128)(2,1)}, bf16[56,1152]{1,0:T(8,128)(2,1)S(1)}, u32[]{:S(2)}, u32[]{:S(2)}) collective-permute-start(bf16[56,1152]{1,0:T(8,128)(2,1)} %get-tuple-element.189), channel_id=1, source_target_pairs={{0,24},{8,16},{16,8},{24,0},{1,25},{9,17},{17,9},{25,1},{2,26},{10... | collective-permute-start | bytes 387080 | tf_op jit(solution)/shard_map/ppermute | solution.py:68
  25.9 80.8 %all-gather.5.cloned.1.call-start = ((), (), s32[]{:S(2)}) async-start(), calls=%async_computation.3 | async-start | bytes 2365440 | tf_op jit(solution)/shard_map/all_gather | solution.py:62
  35.0 6.3 %collective-permute-start.13 = (bf16[28,4224]{1,0:T(8,128)(2,1)S(1)}, bf16[28,4224]{1,0:T(8,128)(2,1)S(1)}, u32[]{:S(2)}, u32[]{:S(2)}) collective-permute-start(bf16[28,4224]{1,0:T(8,128)(2,1)S(1)} %copy-done.60), channel_id=1, source_target_pairs={{0,2},{2,0},{1,3},{3,1},{4,6},{6,4},{5,7},{7,5},{8,10},{10,8},{9,1... | collective-permute-start | bytes 709640 | tf_op jit(solution)/shard_map/ppermute | solution.py:48
  38.0 14.8 %collective-permute-start.4 = (bf16[224,1152]{1,0:T(8,128)(2,1)S(1)}, bf16[224,1152]{1,0:T(8,128)(2,1)S(1)}, u32[]{:S(2)}, u32[]{:S(2)}) collective-permute-start(bf16[224,1152]{1,0:T(8,128)(2,1)S(1)} %constant_dynamic-update-slice_fusion.5), channel_id=1, source_target_pairs={{0,4},{4,0},{1,5},{5,1},{2,6},{6,2},{3,7},{7,3},{8,12},{12,8},{9,1... | collective-permute-start | bytes 1548296 | tf_op jit(solution)/shard_map/ppermute | solution.py:48
  39.2 13.2 %collective-permute-start.5 = (bf16[224,1152]{1,0:T(8,128)(2,1)S(1)}, bf16[224,1152]{1,0:T(8,128)(2,1)S(1)}, u32[]{:S(2)}, u32[]{:S(2)}) collective-permute-start(bf16[224,1152]{1,0:T(8,128)(2,1)S(1)} %constant_dynamic-update-slice_fusion.5), channel_id=1, source_target_pairs={{0,1},{1,0},{2,3},{3,2},{4,5},{5,4},{6,7},{7,6},{8,9},{9,8},{10,11... | collective-permute-start | bytes 1548296 | tf_op jit(solution)/shard_map/ppermute | solution.py:48
  42.3 436.5 %reduce-scatter.5.cloned.1.call-start = ((), (), s32[]{:S(2)}) async-start(), calls=%async_computation.4 | async-start | bytes 1720320 | tf_op jit(solution)/shard_map/reduce_scatter | solution.py:114
  52.4 6.9 %collective-permute-start.6 = (bf16[112,1152]{1,0:T(8,128)(2,1)S(1)}, bf16[112,1152]{1,0:T(8,128)(2,1)S(1)}, u32[]{:S(2)}, u32[]{:S(2)}) collective-permute-start(bf16[112,1152]{1,0:T(8,128)(2,1)S(1)} %slice.428), channel_id=1, source_target_pairs={{0,4},{4,0},{1,5},{5,1},{2,6},{6,2},{3,7},{7,3},{8,12},{12,8},{9,1... | collective-permute-start | bytes 774152 | tf_op jit(solution)/shard_map/ppermute | solution.py:48
  52.8 7.3 %collective-permute-start.7 = (bf16[112,1152]{1,0:T(8,128)(2,1)S(1)}, bf16[112,1152]{1,0:T(8,128)(2,1)S(1)}, u32[]{:S(2)}, u32[]{:S(2)}) collective-permute-start(bf16[112,1152]{1,0:T(8,128)(2,1)S(1)} %slice.429), channel_id=1, source_target_pairs={{0,1},{1,0},{2,3},{3,2},{4,5},{5,4},{6,7},{7,6},{8,9},{9,8},{10,11... | collective-permute-start | bytes 774152 | tf_op jit(solution)/shard_map/ppermute | solution.py:48
  60.7 11.5 %collective-permute-start.8 = (bf16[896,1152]{1,0:T(8,128)(2,1)}, bf16[896,1152]{1,0:T(8,128)(2,1)}, u32[]{:S(2)}, u32[]{:S(2)}) collective-permute-start(bf16[896,1152]{1,0:T(8,128)(2,1)} %constant_dynamic-update-slice_fusion), channel_id=1, source_target_pairs={{0,2},{2,0},{1,3},{3,1},{4,6},{6,4},{5,7},{7,5},{8,10},{10,8},{9,1... | collective-permute-start | bytes 6193160 | tf_op jit(solution)/shard_map/ppermute | solution.py:48
  71.4 56.7 %collective-permute-start.11 = (bf16[224,3072]{1,0:T(8,128)(2,1)}, bf16[224,3072]{1,0:T(8,128)(2,1)}, u32[]{:S(2)}, u32[]{:S(2)}) collective-permute-start(bf16[224,3072]{1,0:T(8,128)(2,1)} %all-gather.3.cloned.1.call-done.zw), channel_id=1, source_target_pairs={{0,4},{4,0},{1,5},{5,1},{2,6},{6,2},{3,7},{7,3},{8,12},{12,8},{9,1... | collective-permute-start | bytes 4128776 | tf_op jit(solution)/shard_map/ppermute | solution.py:48
  76.4 13.4 %collective-permute-start.10 = (bf16[256,1024]{1,0:T(8,128)(2,1)S(1)}, bf16[256,1024]{1,0:T(8,128)(2,1)S(1)}, u32[]{:S(2)}, u32[]{:S(2)}) collective-permute-start(bf16[256,1024]{1,0:T(8,128)(2,1)S(1)} %pad_maximum_fusion.11), channel_id=1, source_target_pairs={{0,1},{1,0},{2,3},{3,2},{4,5},{5,4},{6,7},{7,6},{8,9},{9,8},{10,11... | collective-permute-start | bytes 1572872 | tf_op jit(solution)/shard_map/ppermute | solution.py:48
  90.6 37.4 %collective-permute-start.12 = (bf16[224,3072]{1,0:T(8,128)(2,1)}, bf16[224,3072]{1,0:T(8,128)(2,1)}, u32[]{:S(2)}, u32[]{:S(2)}) collective-permute-start(bf16[224,3072]{1,0:T(8,128)(2,1)} %all-gather.3.cloned.1.call-done.zw), channel_id=1, source_target_pairs={{0,1},{1,0},{2,3},{3,2},{4,5},{5,4},{6,7},{7,6},{8,9},{9,8},{10,11... | collective-permute-start | bytes 4128776 | tf_op jit(solution)/shard_map/ppermute | solution.py:48
  106.7 46.7 %collective-permute-start.18 = (bf16[224,4224]{1,0:T(8,128)(2,1)}, bf16[224,4224]{1,0:T(8,128)(2,1)}, u32[]{:S(2)}, u32[]{:S(2)}) collective-permute-start(bf16[224,4224]{1,0:T(8,128)(2,1)} %all-gather.5.cloned.1.call-done.zw), channel_id=1, source_target_pairs={{0,4},{4,0},{1,5},{5,1},{2,6},{6,2},{3,7},{7,3},{8,12},{12,8},{9,1... | collective-permute-start | bytes 5677064 | tf_op jit(solution)/shard_map/ppermute | solution.py:48
  106.8 59.9 %collective-permute-start.19 = (bf16[224,4224]{1,0:T(8,128)(2,1)}, bf16[224,4224]{1,0:T(8,128)(2,1)}, u32[]{:S(2)}, u32[]{:S(2)}) collective-permute-start(bf16[224,4224]{1,0:T(8,128)(2,1)} %all-gather.5.cloned.1.call-done.zw), channel_id=1, source_target_pairs={{0,1},{1,0},{2,3},{3,2},{4,5},{5,4},{6,7},{7,6},{8,9},{9,8},{10,11... | collective-permute-start | bytes 5677064 | tf_op jit(solution)/shard_map/ppermute | solution.py:48
  122.7 48.5 %collective-permute-start.15 = (bf16[1024,896]{1,0:T(8,128)(2,1)S(1)}, bf16[1024,896]{1,0:T(8,128)(2,1)}, u32[]{:S(2)}, u32[]{:S(2)}) collective-permute-start(bf16[1024,896]{1,0:T(8,128)(2,1)S(1)} %fusion.12.cm), channel_id=1, source_target_pairs={{0,2},{2,0},{1,3},{3,1},{4,6},{6,4},{5,7},{7,5},{8,10},{10,8},{9,1... | collective-permute-start | bytes 5505032 | tf_op jit(solution)/shard_map/ppermute | solution.py:48
  150.2 31.5 %collective-permute-start.14 = (bf16[1024,896]{1,0:T(8,128)(2,1)S(1)}, bf16[1024,896]{1,0:T(8,128)(2,1)}, u32[]{:S(2)}, u32[]{:S(2)}) collective-permute-start(bf16[1024,896]{1,0:T(8,128)(2,1)S(1)} %multiply_convert_fusion.xm), channel_id=1, source_target_pairs={{0,2},{2,0},{1,3},{3,1},{4,6},{6,4},{5,7},{7,5},{8,10},{10,8},{9,1... | collective-permute-start | bytes 5505032 | tf_op jit(solution)/shard_map/ppermute | solution.py:48
  153.4 17.8 %collective-permute-start.16 = (bf16[112,3072]{1,0:T(8,128)(2,1)S(1)}, bf16[112,3072]{1,0:T(8,128)(2,1)S(1)}, u32[]{:S(2)}, u32[]{:S(2)}) collective-permute-start(bf16[112,3072]{1,0:T(8,128)(2,1)S(1)} %slice.379), channel_id=1, source_target_pairs={{0,4},{4,0},{1,5},{5,1},{2,6},{6,2},{3,7},{7,3},{8,12},{12,8},{9,1... | collective-permute-start | bytes 2064392 | tf_op jit(solution)/shard_map/ppermute | solution.py:48
  153.5 27.5 %collective-permute-start.17 = (bf16[112,3072]{1,0:T(8,128)(2,1)S(1)}, bf16[112,3072]{1,0:T(8,128)(2,1)S(1)}, u32[]{:S(2)}, u32[]{:S(2)}) collective-permute-start(bf16[112,3072]{1,0:T(8,128)(2,1)S(1)} %slice.380), channel_id=1, source_target_pairs={{0,1},{1,0},{2,3},{3,2},{4,5},{5,4},{6,7},{7,6},{8,9},{9,8},{10,11... | collective-permute-start | bytes 2064392 | tf_op jit(solution)/shard_map/ppermute | solution.py:48
  168.9 62.3 %collective-permute-start.20 = (bf16[112,4224]{1,0:T(8,128)(2,1)}, bf16[112,4224]{1,0:T(8,128)(2,1)}, u32[]{:S(2)}, u32[]{:S(2)}) collective-permute-start(bf16[112,4224]{1,0:T(8,128)(2,1)} %slice.381), channel_id=1, source_target_pairs={{0,4},{4,0},{1,5},{5,1},{2,6},{6,2},{3,7},{7,3},{8,12},{12,8},{9,1... | collective-permute-start | bytes 2838536 | tf_op jit(solution)/shard_map/ppermute | solution.py:48
  171.2 60.0 %collective-permute-start.21 = (bf16[112,4224]{1,0:T(8,128)(2,1)}, bf16[112,4224]{1,0:T(8,128)(2,1)}, u32[]{:S(2)}, u32[]{:S(2)}) collective-permute-start(bf16[112,4224]{1,0:T(8,128)(2,1)} %slice.382), channel_id=1, source_target_pairs={{0,1},{1,0},{2,3},{3,2},{4,5},{5,4},{6,7},{7,6},{8,9},{9,8},{10,11... | collective-permute-start | bytes 2838536 | tf_op jit(solution)/shard_map/ppermute | solution.py:48
  228.9 77.8 %collective-permute-start.25 = (bf16[112,3072]{1,0:T(8,128)(2,1)}, bf16[112,3072]{1,0:T(8,128)(2,1)}, u32[]{:S(2)}, u32[]{:S(2)}) collective-permute-start(bf16[112,3072]{1,0:T(8,128)(2,1)} %get-tuple-element.120), channel_id=1, source_target_pairs={{0,4},{4,0},{1,5},{5,1},{2,6},{6,2},{3,7},{7,3},{8,12},{12,8},{9,1... | collective-permute-start | bytes 2064392 | tf_op jit(solution)/shard_map/ppermute | solution.py:48
  229.0 78.2 %collective-permute-start.26 = (bf16[112,3072]{1,0:T(8,128)(2,1)}, bf16[112,3072]{1,0:T(8,128)(2,1)}, u32[]{:S(2)}, u32[]{:S(2)}) collective-permute-start(bf16[112,3072]{1,0:T(8,128)(2,1)} %get-tuple-element.121), channel_id=1, source_target_pairs={{0,1},{1,0},{2,3},{3,2},{4,5},{5,4},{6,7},{7,6},{8,9},{9,8},{10,11... | collective-permute-start | bytes 2064392 | tf_op jit(solution)/shard_map/ppermute | solution.py:48
  302.1 11.7 %collective-permute-start.23 = (bf16[1024,896]{1,0:T(8,128)(2,1)S(1)}, bf16[1024,896]{1,0:T(8,128)(2,1)S(1)}, u32[]{:S(2)}, u32[]{:S(2)}) collective-permute-start(bf16[1024,896]{1,0:T(8,128)(2,1)S(1)} %add_convert_fusion.4), channel_id=1, source_target_pairs={{0,2},{2,0},{1,3},{3,1},{4,6},{6,4},{5,7},{7,5},{8,10},{10,8},{9,1... | collective-permute-start | bytes 5505032 | tf_op jit(solution)/shard_map/ppermute | solution.py:48
  304.2 40.2 %collective-permute-start.29 = (bf16[112,4224]{1,0:T(8,128)(2,1)}, bf16[112,4224]{1,0:T(8,128)(2,1)}, u32[]{:S(2)}, u32[]{:S(2)}) collective-permute-start(bf16[112,4224]{1,0:T(8,128)(2,1)} %get-tuple-element.136), channel_id=1, source_target_pairs={{0,4},{4,0},{1,5},{5,1},{2,6},{6,2},{3,7},{7,3},{8,12},{12,8},{9,1... | collective-permute-start | bytes 2838536 | tf_op jit(solution)/shard_map/ppermute | solution.py:48
  305.0 39.4 %collective-permute-start.30 = (bf16[112,4224]{1,0:T(8,128)(2,1)}, bf16[112,4224]{1,0:T(8,128)(2,1)}, u32[]{:S(2)}, u32[]{:S(2)}) collective-permute-start(bf16[112,4224]{1,0:T(8,128)(2,1)} %get-tuple-element.137), channel_id=1, source_target_pairs={{0,1},{1,0},{2,3},{3,2},{4,5},{5,4},{6,7},{7,6},{8,9},{9,8},{10,11... | collective-permute-start | bytes 2838536 | tf_op jit(solution)/shard_map/ppermute | solution.py:48
  306.7 75.2 %collective-permute-start.22 = (bf16[1024,896]{1,0:T(8,128)(2,1)}, bf16[1024,896]{1,0:T(8,128)(2,1)}, u32[]{:S(2)}, u32[]{:S(2)}) collective-permute-start(bf16[1024,896]{1,0:T(8,128)(2,1)} %add_convert_fusion.6), channel_id=1, source_target_pairs={{0,2},{2,0},{1,3},{3,1},{4,6},{6,4},{5,7},{7,5},{8,10},{10,8},{9,1... | collective-permute-start | bytes 5505032 | tf_op jit(solution)/shard_map/ppermute | solution.py:48
  309.8 77.5 %collective-permute-start.28 = (bf16[224,3072]{1,0:T(8,128)(2,1)}, bf16[224,3072]{1,0:T(8,128)(2,1)}, u32[]{:S(2)}, u32[]{:S(2)}) collective-permute-start(bf16[224,3072]{1,0:T(8,128)(2,1)} %add_convert_fusion.8), channel_id=1, source_target_pairs={{0,1},{1,0},{2,3},{3,2},{4,5},{5,4},{6,7},{7,6},{8,9},{9,8},{10,11... | collective-permute-start | bytes 4128776 | tf_op jit(solution)/shard_map/ppermute | solution.py:48
  313.8 73.5 %collective-permute-start.27 = (bf16[224,3072]{1,0:T(8,128)(2,1)}, bf16[224,3072]{1,0:T(8,128)(2,1)}, u32[]{:S(2)}, u32[]{:S(2)}) collective-permute-start(bf16[224,3072]{1,0:T(8,128)(2,1)} %add_convert_fusion.9), channel_id=1, source_target_pairs={{0,4},{4,0},{1,5},{5,1},{2,6},{6,2},{3,7},{7,3},{8,12},{12,8},{9,1... | collective-permute-start | bytes 4128776 | tf_op jit(solution)/shard_map/ppermute | solution.py:48
  347.3 87.2 %collective-permute-start.32 = (bf16[224,4224]{1,0:T(8,128)(2,1)}, bf16[224,4224]{1,0:T(8,128)(2,1)}, u32[]{:S(2)}, u32[]{:S(2)}) collective-permute-start(bf16[224,4224]{1,0:T(8,128)(2,1)} %add_convert_fusion.1), channel_id=1, source_target_pairs={{0,1},{1,0},{2,3},{3,2},{4,5},{5,4},{6,7},{7,6},{8,9},{9,8},{10,11... | collective-permute-start | bytes 5677064 | tf_op jit(solution)/shard_map/ppermute | solution.py:48
  367.7 66.8 %collective-permute-start.31 = (bf16[224,4224]{1,0:T(8,128)(2,1)}, bf16[224,4224]{1,0:T(8,128)(2,1)}, u32[]{:S(2)}, u32[]{:S(2)}) collective-permute-start(bf16[224,4224]{1,0:T(8,128)(2,1)} %add_convert_fusion.2), channel_id=1, source_target_pairs={{0,4},{4,0},{1,5},{5,1},{2,6},{6,2},{3,7},{7,3},{8,12},{12,8},{9,1... | collective-permute-start | bytes 5677064 | tf_op jit(solution)/shard_map/ppermute | solution.py:48
  382.0 50.1 %collective-permute-start.24 = (bf16[128,1024]{1,0:T(8,128)(2,1)S(1)}, bf16[128,1024]{1,0:T(8,128)(2,1)S(1)}, u32[]{:S(2)}, u32[]{:S(2)}) collective-permute-start(bf16[128,1024]{1,0:T(8,128)(2,1)S(1)} %copy-done.61), channel_id=1, source_target_pairs={{0,1},{1,0},{2,3},{3,2},{4,5},{5,4},{6,7},{7,6},{8,9},{9,8},{10,11... | collective-permute-start | bytes 786440 | tf_op jit(solution)/shard_map/ppermute | solution.py:48
  390.9 127.2 %reduce-scatter.7.cloned.1.call-start = ((), (), s32[]{:S(2)}) async-start(), calls=%async_computation.5 | async-start | bytes 2365440
  413.2 26.9 %collective-permute-start.33 = (bf16[128,1024]{1,0:T(8,128)(2,1)}, bf16[128,1024]{1,0:T(8,128)(2,1)}, u32[]{:S(2)}, u32[]{:S(2)}) collective-permute-start(bf16[128,1024]{1,0:T(8,128)(2,1)} %get-tuple-element.132), channel_id=1, source_target_pairs={{0,1},{1,0},{2,3},{3,2},{4,5},{5,4},{6,7},{7,6},{8,9},{9,8},{10,11... | collective-permute-start | bytes 786440 | tf_op jit(solution)/shard_map/ppermute | solution.py:48
  443.4 13.0 %collective-permute-start.34 = (bf16[896,1024]{0,1:T(8,128)(2,1)S(1)}, bf16[896,1024]{0,1:T(8,128)(2,1)}, u32[]{:S(2)}, u32[]{:S(2)}) collective-permute-start(bf16[896,1024]{0,1:T(8,128)(2,1)S(1)} %pad_maximum_fusion.1), channel_id=1, source_target_pairs={{0,2},{2,0},{1,3},{3,1},{4,6},{6,4},{5,7},{7,5},{8,10},{10,8},{9,1... | collective-permute-start | bytes 5505032 | tf_op jit(solution)/shard_map/ppermute | solution.py:48
  458.9 8.1 %collective-permute-start.35 = (bf16[112,1152]{0,1:T(8,128)(2,1)S(1)}, bf16[112,1152]{0,1:T(8,128)(2,1)S(1)}, u32[]{:S(2)}, u32[]{:S(2)}) collective-permute-start(bf16[112,1152]{0,1:T(8,128)(2,1)S(1)} %get-tuple-element.196), channel_id=1, source_target_pairs={{0,1},{1,0},{2,3},{3,2},{4,5},{5,4},{6,7},{7,6},{8,9},{9,8},{10,11... | collective-permute-start | bytes 774152 | tf_op jit(solution)/shard_map/ppermute | solution.py:48
  459.0 8.1 %collective-permute-start.37 = (bf16[112,1152]{0,1:T(8,128)(2,1)S(1)}, bf16[112,1152]{0,1:T(8,128)(2,1)S(1)}, u32[]{:S(2)}, u32[]{:S(2)}) collective-permute-start(bf16[112,1152]{0,1:T(8,128)(2,1)S(1)} %get-tuple-element.197), channel_id=1, source_target_pairs={{0,4},{4,0},{1,5},{5,1},{2,6},{6,2},{3,7},{7,3},{8,12},{12,8},{9,1... | collective-permute-start | bytes 774152 | tf_op jit(solution)/shard_map/ppermute | solution.py:48
  468.4 12.0 %collective-permute-start.36 = (bf16[224,1152]{1,0:T(8,128)(2,1)S(1)}, bf16[224,1152]{1,0:T(8,128)(2,1)S(1)}, u32[]{:S(2)}, u32[]{:S(2)}) collective-permute-start(bf16[224,1152]{1,0:T(8,128)(2,1)S(1)} %copy.192), channel_id=1, source_target_pairs={{0,4},{4,0},{1,5},{5,1},{2,6},{6,2},{3,7},{7,3},{8,12},{12,8},{9,1... | collective-permute-start | bytes 1548296 | tf_op jit(solution)/shard_map/ppermute | solution.py:48
  469.6 11.8 %collective-permute-start.38 = (bf16[224,1152]{1,0:T(8,128)(2,1)S(1)}, bf16[224,1152]{1,0:T(8,128)(2,1)S(1)}, u32[]{:S(2)}, u32[]{:S(2)}) collective-permute-start(bf16[224,1152]{1,0:T(8,128)(2,1)S(1)} %copy.194), channel_id=1, source_target_pairs={{0,1},{1,0},{2,3},{3,2},{4,5},{5,4},{6,7},{7,6},{8,9},{9,8},{10,11... | collective-permute-start | bytes 1548296 | tf_op jit(solution)/shard_map/ppermute | solution.py:48
  483.5 9.0 %collective-permute-start.39 = (bf16[56,1152]{0,1:T(8,128)(2,1)S(1)}, bf16[56,1152]{0,1:T(8,128)(2,1)S(1)}, u32[]{:S(2)}, u32[]{:S(2)}) collective-permute-start(bf16[56,1152]{0,1:T(8,128)(2,1)S(1)} %get-tuple-element.208), channel_id=1, source_target_pairs={{0,8},{8,0},{16,24},{24,16},{1,9},{9,1},{17,25},{25,17},{2,10},{10... | collective-permute-start | bytes 387080 | tf_op jit(solution)/shard_map/ppermute | solution.py:119
  483.6 22.7 %collective-permute-start.40 = (bf16[56,1152]{0,1:T(8,128)(2,1)S(1)}, bf16[56,1152]{0,1:T(8,128)(2,1)S(1)}, u32[]{:S(2)}, u32[]{:S(2)}) collective-permute-start(bf16[56,1152]{0,1:T(8,128)(2,1)S(1)} %get-tuple-element.210), channel_id=1, source_target_pairs={{0,16},{8,24},{16,0},{24,8},{1,17},{9,25},{17,1},{25,9},{2,18},{10... | collective-permute-start | bytes 387080 | tf_op jit(solution)/shard_map/ppermute | solution.py:119
  488.7 24.0 %collective-permute-start.41 = (bf16[56,1152]{0,1:T(8,128)(2,1)S(1)}, bf16[56,1152]{0,1:T(8,128)(2,1)S(1)}, u32[]{:S(2)}, u32[]{:S(2)}) collective-permute-start(bf16[56,1152]{0,1:T(8,128)(2,1)S(1)} %get-tuple-element.209), channel_id=1, source_target_pairs={{0,24},{8,16},{16,8},{24,0},{1,25},{9,17},{17,9},{25,1},{2,26},{10... | collective-permute-start | bytes 387080 | tf_op jit(solution)/shard_map/ppermute | solution.py:119
  489.5 33.8 %collective-permute-start.43 = (f32[28,3072]{1,0:T(8,128)S(1)}, f32[28,3072]{1,0:T(8,128)S(1)}, u32[]{:S(2)}, u32[]{:S(2)}) collective-permute-start(f32[28,3072]{1,0:T(8,128)S(1)} %get-tuple-element.200), channel_id=1, source_target_pairs={{0,2},{2,0},{1,3},{3,1},{4,6},{6,4},{5,7},{7,5},{8,10},{10,8},{9,1... | collective-permute-start | bytes 1032200 | tf_op jit(solution)/shard_map/ppermute | solution.py:48
  513.4 3.1 collective-permute-start.42
  520.3 3.0 collective-permute-start.44
  (67 other events, 983.2 us)
Sparse Core Ops, SparseCore 0:
  26.0 35.4 all-gather.2
  63.7 40.8 all-gather.4
  391.0 33.5 reduce-scatter.4
  438.7 43.5 reduce-scatter.6

commit v3 on v2

--- a/solution.py
+++ b/solution.py
@@ -160,6 +160,37 @@
         out_shape=shapes,
         name="pack",
     )(core, gate, up, down)
+
+
+def pack_attn_kernel(core_ref, q_ref, k_ref, v_ref, o_ref, vec_ref, mine_ref, theirs_ref):
+    rows = q_ref.shape[0]
+    fh, kh = q_ref.shape[1] // 2, k_ref.shape[1] // 2
+
+    def side(s, out):
+        out[...] = jnp.concatenate(
+            [q_ref[:, s * fh : (s + 1) * fh], k_ref[:, s * kh : (s + 1) * kh], v_ref[:, s * kh : (s + 1) * kh],
+             o_ref[:, s * fh : (s + 1) * fh], vec_ref[...]], axis=1)
+
+    @pl.when(core_ref[0] == 0)
+    def _():
+        side(0, mine_ref)
+        side(1, theirs_ref)
+
+    @pl.when(core_ref[0] != 0)
+    def _():
+        side(1, mine_ref)
+        side(0, theirs_ref)
+
+
+def pack_attn(core, q, k, v, o, vec):
+    shape = jax.ShapeDtypeStruct((q.shape[0], (q.shape[1] + k.shape[1] + v.shape[1] + o.shape[1]) // 2 + vec.shape[1]), q.dtype)
+    return pl.pallas_call(
+        pack_attn_kernel,
+        in_specs=[pl.BlockSpec(memory_space=pltpu.SMEM)] + [whole()] * 5,
+        out_specs=[whole()] * 2,
+        out_shape=[shape] * 2,
+        name="pack_attention",
+    )(core, q, k, v, o, vec)
 
 
 def unpack_kernel(chunks, core_ref, *refs):
@@ -571,12 +602,7 @@
         [column(v, rows) for v in (attn_gain, mlp_gain, query_bias, key_bias, value_bias)]
         + [jnp.zeros((rows, EXTRA - 5), BF16)], axis=1)
     fh, kh = feat // 2, kv_feat // 2
-    sides = [
-        jnp.concatenate([query_weight[:, s * fh : (s + 1) * fh], key_weight[:, s * kh : (s + 1) * kh],
-                         value_weight[:, s * kh : (s + 1) * kh], out_weight[:, s * fh : (s + 1) * fh], extras], axis=1)
-        for s in range(2)
-    ]
-    a_own = pair_rows(jnp.where(own_first, sides[0], sides[1]), jnp.where(own_first, sides[1], sides[0]))
+    a_own = pair_rows(*pack_attn(core_arr, query_weight, key_weight, value_weight, out_weight, extras))
     tokens, cotangent = after((tokens, cotangent), a_own)
     a_zs = along_z(a_own, True)
     gate_weight, up_weight, down_weight = after((gate_weight, up_weight, down_weight), a_own)

time: 542 us -> 538 us (level)
  no operation moved by 1% of the time
where the time goes in v3:
time: 538 us; the launch traced here: 531 us
  Pallas kernels  197 us (37%)
  starting transfers between devices  107 us (20%)
  matrix products  65 us (12%)
  other arithmetic  58.3 us (11%)
  waiting for transfers between devices  53.7 us (10%)
  local copies, waits for them, and re-layouts  35.5 us (7%)
  between operations  15.2 us (3%)
    pallas_call x2, Pallas kernels, mlp(): pl.pallas_call(functools.partial(mlp_kernel, last_t, rows), grid=(steps,)...  116 us
    ppermute x39, starting transfers between devices, swap(): return lax.ppermute(v, axis, SWAP)  98.1 us
    pallas_call x2, Pallas kernels, attn_bwd(): pl.pallas_call(functools.partial(attn_bwd_kernel, bk), grid=(blocks,), in...  44.7 us
    ppermute x39, waiting for transfers between devices, swap(): return lax.ppermute(v, axis, SWAP)  34 us
    convert_element_type x26, other arithmetic, bf(): return v.astype(BF16)  33.6 us
    pallas_call x2, Pallas kernels, attn_fwd(): pl.pallas_call(functools.partial(attn_fwd_kernel, bk), grid=(blocks,), in...  29.4 us
    ppermute x3, waiting for transfers between devices, sum_along_z(): parts.append(lax.ppermute(part, 'zz', [(i, i ^ j) for i in range(count)]))  19.6 us
    dot_general x2, matrix products, nt(): lax.dot_general(a, b, (((1,), (1,)), ((), ())), preferred_element_type=F32)  13.3 us
  transfers between devices with their start and end apart: 49, of which 11 were waited for; matrix products, arithmetic and copies ran while one was open for 28% of the time, Pallas kernels for 36%

profile of v3, /device:TPU:9, one launch (start us, length us, event | category | flops | bytes accessed | tf_op | source)
XLA Modules:
  0.0 530.9 jit_solution(1851130665603383636)
XLA Ops:
  19.9 2.5 collective-permute-start.2
  24.6 4.0 multiply_reduce_fusion.5
  28.5 5.1 copy.105
  42.1 9.7 %collective-permute-done.5 = bf16[224,1152]{1,0:T(8,128)(2,1)S(1)} collective-permute-done((bf16[224,1152]{1,0:T(8,128)(2,1)S(1)}, bf16[224,1152]{1,0:T(8,128)(2,1)S(1)}, u32[]{:S(2)}, u32[]{:S(2)}) %collective-permute-start.5) | collective-permute-done | bytes 516128 | tf_op jit(solution)/shard_map/ppermute | solution.py:48
  55.3 3.3 collective-permute-done.6
  65.7 2.4 multiply_convert_fusion.1
  78.4 2.4 convolution_add_fusion.1
  83.8 5.3 collective-permute-done.10
  91.3 14.8 %attention.2 = (bf16[448,1024]{1,0:T(8,128)(2,1)}, bf16[448,1024]{1,0:T(8,128)(2,1)}, f32[4,1,1792]{2,1,0:T(1,128)}) custom-call(s32[3]{0:T(128)} %pad_add_fusion.info_ref, bf16[448,1024]{1,0:T(8,128)(2,1)} %bitcast.75, bf16[128,1024]{1,0:T(8,128)(2,1)} %pad_maximum_fusion.14.loc_ref, bf16[128,1024]{1,0:T(8,128)(2,1)} %get-tuple-element.216.rem_ref), custom_call_target="tpu_custom_call" | custom-call | flops 7516192768 | bytes 3670016 | tf_op jit(solution)/shard_map/attention/pallas_call | solution.py:416
  106.3 11.0 %collective-permute-start.19 = (bf16[224,4224]{1,0:T(8,128)(2,1)}, bf16[224,4224]{1,0:T(8,128)(2,1)}, u32[]{:S(2)}, u32[]{:S(2)}) collective-permute-start(bf16[224,4224]{1,0:T(8,128)(2,1)} %all-gather.5.cloned.1.call-done.zw), channel_id=1, source_target_pairs={{0,1},{1,0},{2,3},{3,2},{4,5},{5,4},{6,7},{7,6},{8,9},{9,8},{10,11... | collective-permute-start | bytes 5677064 | tf_op jit(solution)/shard_map/ppermute | solution.py:48
  117.2 3.8 fusion.12.cm
  121.0 3.0 collective-permute-start.15
  124.0 3.5 fusion.32
  127.5 14.6 %attention.3 = (bf16[448,1024]{1,0:T(8,128)(2,1)}, bf16[448,1024]{1,0:T(8,128)(2,1)}, f32[4,1,1792]{2,1,0:T(1,128)}) custom-call(s32[3]{0:T(128)} %pad_add_fusion.info_ref, bf16[448,1024]{1,0:T(8,128)(2,1)} %bitcast.73, bf16[128,1024]{1,0:T(8,128)(2,1)} %pad_maximum_fusion.15.loc_ref, bf16[128,1024]{1,0:T(8,128)(2,1)} %get-tuple-element.215.rem_ref), custom_call_target="tpu_custom_call" | custom-call | flops 7516192768 | bytes 3670016 | tf_op jit(solution)/shard_map/attention/pallas_call | solution.py:416
  142.1 5.7 %multiply_reduce_fusion.4 = (f32[1024]{0:T(1024)S(1)}, f32[1024,896]{1,0:T(8,128)S(1)}) fusion(bf16[448,1024]{1,0:T(8,128)(2,1)} %get-tuple-element.103.o_ref, bf16[896,1152]{1,0:T(8,128)(2,1)} %collective-permute-done.8, f32[1024,896]{1,0:T(8,128)} %copy.105, f32[1024,896]{1,0:T(8,128)} %fusion.32), kind=kOutput, calls=%fused_computation.15 | convolution fusion | flops 825752576 | bytes 12849152 | tf_op jit(solution)/shard_map/dot_general | solution.py:680
  152.9 10.2 %collective-permute-start.17 = (bf16[112,3072]{1,0:T(8,128)(2,1)S(1)}, bf16[112,3072]{1,0:T(8,128)(2,1)S(1)}, u32[]{:S(2)}, u32[]{:S(2)}) collective-permute-start(bf16[112,3072]{1,0:T(8,128)(2,1)S(1)} %slice.348), channel_id=1, source_target_pairs={{0,1},{1,0},{2,3},{3,2},{4,5},{5,4},{6,7},{7,6},{8,9},{9,8},{10,11... | collective-permute-start | bytes 2064392 | tf_op jit(solution)/shard_map/ppermute | solution.py:48
  170.8 7.2 %collective-permute-done.17.bw = bf16[112,3072]{1,0:T(8,128)(2,1)S(1)} collective-permute-done((bf16[112,3072]{1,0:T(8,128)(2,1)S(1)}, bf16[112,3072]{1,0:T(8,128)(2,1)S(1)}, u32[]{:S(2)}, u32[]{:S(2)}) %collective-permute-start.17) | collective-permute-done | bytes 688160 | tf_op jit(solution)/shard_map/ppermute | solution.py:48
  178.8 47.1 %feed_forward.2 = (bf16[1024,896]{1,0:T(8,128)(2,1)}, bf16[1024,896]{1,0:T(8,128)(2,1)}, bf16[1024,896]{1,0:T(8,128)(2,1)}, bf16[1024,896]{1,0:T(8,128)(2,1)}, b...) custom-call(bf16[1024,896]{1,0:T(8,128)(2,1)} %copy-done.22, ...), custom_call_target="tpu_custom_call" | custom-call | flops 33822867456 | bytes 11010048 | tf_op jit(solution)/shard_map/feed_forward/pallas_call | solution.py:320
  229.1 68.8 %feed_forward.3 = (bf16[1024,896]{1,0:T(8,128)(2,1)}, bf16[1024,896]{1,0:T(8,128)(2,1)}, bf16[1024,896]{1,0:T(8,128)(2,1)}, bf16[1024,896]{1,0:T(8,128)(2,1)}, b...) custom-call(bf16[1024,896]{1,0:T(8,128)(2,1)} %copy-done.22, ...), custom_call_target="tpu_custom_call" | custom-call | flops 46506442752 | bytes 15138816 | tf_op jit(solution)/shard_map/feed_forward/pallas_call | solution.py:320
  300.0 2.7 collective-permute-start.23
  305.9 2.6 add_convert_fusion.8
  310.0 2.4 add_convert_fusion.9
  314.6 3.1 fusion.87
  317.7 2.7 convolution_convert_fusion.3.do_ref
  320.4 22.4 %attention_back.2 = (bf16[448,1024]{1,0:T(8,128)(2,1)}, f32[128,1024]{1,0:T(8,128)}, bf16[128,1024]{1,0:T(8,128)(2,1)}, f32[128,128]{1,0:T(8,128)}) custom-call(s32[3]{0:T(128)} %pad_add_fusion.info_ref, bf16[448,1024]{1,0:T(8,128)(2,1)} %bitcast.76, bf16[448,1024]{1,0:T(8,128)(2,1)} %convolution_convert_fusion.3.do_ref, ...), custom_call_target="tpu_custom_call" | custom-call | flops 18790481920 | bytes 7340032 | tf_op jit(solution)/shard_map/attention_back/pallas_call | solution.py:518
  342.9 2.8 add_convert_fusion.1
  345.7 17.5 %collective-permute-start.32 = (bf16[224,4224]{1,0:T(8,128)(2,1)}, bf16[224,4224]{1,0:T(8,128)(2,1)}, u32[]{:S(2)}, u32[]{:S(2)}) collective-permute-start(bf16[224,4224]{1,0:T(8,128)(2,1)} %add_convert_fusion.1), channel_id=1, source_target_pairs={{0,1},{1,0},{2,3},{3,2},{4,5},{5,4},{6,7},{7,6},{8,9},{9,8},{10,11... | collective-permute-start | bytes 5677064 | tf_op jit(solution)/shard_map/ppermute | solution.py:48
  363.2 2.9 add_convert_fusion.2
  367.4 3.2 convolution_convert_fusion.5
  371.6 3.2 convolution_convert_fusion.4
  374.8 4.1 convolution_convert_fusion.2.do_ref
  379.0 5.3 fusion.13
  384.4 3.6 add_convert_fusion.7
  388.0 22.2 %attention_back.3 = (bf16[448,1024]{1,0:T(8,128)(2,1)}, f32[128,1024]{1,0:T(8,128)}, bf16[128,1024]{1,0:T(8,128)(2,1)}, f32[128,128]{1,0:T(8,128)}) custom-call(s32[3]{0:T(128)} %pad_add_fusion.info_ref, bf16[448,1024]{1,0:T(8,128)(2,1)} %bitcast.74, bf16[448,1024]{1,0:T(8,128)(2,1)} %convolution_convert_fusion.2.do_ref, ...), custom_call_target="tpu_custom_call" | custom-call | flops 18790481920 | bytes 7340032 | tf_op jit(solution)/shard_map/attention_back/pallas_call | solution.py:518
  410.2 18.9 %collective-permute-start.33 = (bf16[128,1024]{1,0:T(8,128)(2,1)}, bf16[128,1024]{1,0:T(8,128)(2,1)}, u32[]{:S(2)}, u32[]{:S(2)}) collective-permute-start(bf16[128,1024]{1,0:T(8,128)(2,1)} %get-tuple-element.136), channel_id=1, source_target_pairs={{0,1},{1,0},{2,3},{3,2},{4,5},{5,4},{6,7},{7,6},{8,9},{9,8},{10,11... | collective-permute-start | bytes 786440 | tf_op jit(solution)/shard_map/ppermute | solution.py:48
  429.2 2.3 convolution_convert_fusion.1
  431.6 4.0 add_convert_fusion
  440.4 3.2 collective-permute-start.34
  444.9 3.5 fusion.21
  448.5 4.0 multiply_reduce_fusion.1
  457.5 6.5 %collective-permute-done.35 = bf16[112,1152]{0,1:T(8,128)(2,1)S(1)} collective-permute-done((bf16[112,1152]{0,1:T(8,128)(2,1)S(1)}, bf16[112,1152]{0,1:T(8,128)(2,1)S(1)}, u32[]{:S(2)}, u32[]{:S(2)}) %collective-permute-start.35) | collective-permute-done | bytes 258080 | tf_op jit(solution)/shard_map/ppermute | solution.py:48
  468.2 8.0 %fusion.14 = bf16[1024,896]{1,0:T(8,128)(2,1)} fusion(f32[1024,896]{1,0:T(8,128)} %copy.105, f32[1024,896]{1,0:T(8,128)} %get-tuple-element.191, f32[1024,896]{1,0:T(8,128)} %get-tuple-element.258, f32[1024]{0:T(1024)S(1)} %broadcast_multiply_fusion, f32[1024]{0:T(1024)S(1)} %copy-done.53, f32[896]{0:T(1024)S(1)} %copy-done.48, f32[1024]{0:T(1024)S(1)} %copy-done.51, ...), kind=kOutput, calls=%fused_computation.44 | convolution fusion | flops 1652310016 | bytes 12864512 | tf_op jit(solution)/shard_map/dot_general | solution.py:40
  481.5 4.6 collective-permute-start.40
  487.1 3.1 collective-permute-start.43
  490.3 13.2 %collective-permute-done.40 = bf16[56,1152]{0,1:T(8,128)(2,1)S(1)} collective-permute-done((bf16[56,1152]{0,1:T(8,128)(2,1)S(1)}, bf16[56,1152]{0,1:T(8,128)(2,1)S(1)}, u32[]{:S(2)}, u32[]{:S(2)}) %collective-permute-start.40) | collective-permute-done | bytes 129056 | tf_op jit(solution)/shard_map/ppermute | solution.py:119
  503.5 6.3 %collective-permute-done.41 = bf16[56,1152]{0,1:T(8,128)(2,1)S(1)} collective-permute-done((bf16[56,1152]{0,1:T(8,128)(2,1)S(1)}, bf16[56,1152]{0,1:T(8,128)(2,1)S(1)}, u32[]{:S(2)}, u32[]{:S(2)}) %collective-permute-start.41) | collective-permute-done | bytes 129056 | tf_op jit(solution)/shard_map/ppermute | solution.py:119
  510.5 3.5 collective-permute-start.42
  521.3 2.8 unpack.1
  (375 shorter events, 106.5 us)
Async XLA Ops:
  7.2 63.6 %all-gather.3.cloned.1.call-start = ((), (), s32[]{:S(2)}) async-start(), calls=%async_computation.2 | async-start | bytes 1720320 | tf_op jit(solution)/shard_map/all_gather | solution.py:62
  19.2 3.4 collective-permute-start.9
  19.9 15.7 %collective-permute-start.1 = (bf16[56,1152]{1,0:T(8,128)(2,1)S(1)}, bf16[56,1152]{1,0:T(8,128)(2,1)}, u32[]{:S(2)}, u32[]{:S(2)}) collective-permute-start(bf16[56,1152]{1,0:T(8,128)(2,1)S(1)} %get-tuple-element.193), channel_id=1, source_target_pairs={{0,8},{8,0},{16,24},{24,16},{1,9},{9,1},{17,25},{25,17},{2,10},{10... | collective-permute-start | bytes 387080 | tf_op jit(solution)/shard_map/ppermute | solution.py:68
  19.9 16.5 %collective-permute-start.2 = (bf16[56,1152]{1,0:T(8,128)(2,1)S(1)}, bf16[56,1152]{1,0:T(8,128)(2,1)}, u32[]{:S(2)}, u32[]{:S(2)}) collective-permute-start(bf16[56,1152]{1,0:T(8,128)(2,1)S(1)} %get-tuple-element.193), channel_id=1, source_target_pairs={{0,16},{8,24},{16,0},{24,8},{1,17},{9,25},{17,1},{25,9},{2,18},{10... | collective-permute-start | bytes 387080 | tf_op jit(solution)/shard_map/ppermute | solution.py:68
  22.4 15.0 %collective-permute-start.3 = (bf16[56,1152]{1,0:T(8,128)(2,1)S(1)}, bf16[56,1152]{1,0:T(8,128)(2,1)S(1)}, u32[]{:S(2)}, u32[]{:S(2)}) collective-permute-start(bf16[56,1152]{1,0:T(8,128)(2,1)S(1)} %get-tuple-element.193), channel_id=1, source_target_pairs={{0,24},{8,16},{16,8},{24,0},{1,25},{9,17},{17,9},{25,1},{2,26},{10... | collective-permute-start | bytes 387080 | tf_op jit(solution)/shard_map/ppermute | solution.py:68
  24.5 81.6 %all-gather.5.cloned.1.call-start = ((), (), s32[]{:S(2)}) async-start(), calls=%async_computation.3 | async-start | bytes 2365440 | tf_op jit(solution)/shard_map/all_gather | solution.py:62
  33.6 7.2 %collective-permute-start.13 = (bf16[28,4224]{1,0:T(8,128)(2,1)S(1)}, bf16[28,4224]{1,0:T(8,128)(2,1)S(1)}, u32[]{:S(2)}, u32[]{:S(2)}) collective-permute-start(bf16[28,4224]{1,0:T(8,128)(2,1)S(1)} %copy-done.60), channel_id=1, source_target_pairs={{0,2},{2,0},{1,3},{3,1},{4,6},{6,4},{5,7},{7,5},{8,10},{10,8},{9,1... | collective-permute-start | bytes 709640 | tf_op jit(solution)/shard_map/ppermute | solution.py:48
  37.5 14.8 %collective-permute-start.4 = (bf16[224,1152]{1,0:T(8,128)(2,1)S(1)}, bf16[224,1152]{1,0:T(8,128)(2,1)S(1)}, u32[]{:S(2)}, u32[]{:S(2)}) collective-permute-start(bf16[224,1152]{1,0:T(8,128)(2,1)S(1)} %constant_dynamic-update-slice_fusion.5), channel_id=1, source_target_pairs={{0,4},{4,0},{1,5},{5,1},{2,6},{6,2},{3,7},{7,3},{8,12},{12,8},{9,1... | collective-permute-start | bytes 1548296 | tf_op jit(solution)/shard_map/ppermute | solution.py:48
  38.7 13.1 %collective-permute-start.5 = (bf16[224,1152]{1,0:T(8,128)(2,1)S(1)}, bf16[224,1152]{1,0:T(8,128)(2,1)S(1)}, u32[]{:S(2)}, u32[]{:S(2)}) collective-permute-start(bf16[224,1152]{1,0:T(8,128)(2,1)S(1)} %constant_dynamic-update-slice_fusion.5), channel_id=1, source_target_pairs={{0,1},{1,0},{2,3},{3,2},{4,5},{5,4},{6,7},{7,6},{8,9},{9,8},{10,11... | collective-permute-start | bytes 1548296 | tf_op jit(solution)/shard_map/ppermute | solution.py:48
  41.8 434.4 %reduce-scatter.5.cloned.1.call-start = ((), (), s32[]{:S(2)}) async-start(), calls=%async_computation.4 | async-start | bytes 1720320 | tf_op jit(solution)/shard_map/reduce_scatter | solution.py:114
  51.8 6.8 %collective-permute-start.6 = (bf16[112,1152]{1,0:T(8,128)(2,1)S(1)}, bf16[112,1152]{1,0:T(8,128)(2,1)S(1)}, u32[]{:S(2)}, u32[]{:S(2)}) collective-permute-start(bf16[112,1152]{1,0:T(8,128)(2,1)S(1)} %slice.396), channel_id=1, source_target_pairs={{0,4},{4,0},{1,5},{5,1},{2,6},{6,2},{3,7},{7,3},{8,12},{12,8},{9,1... | collective-permute-start | bytes 774152 | tf_op jit(solution)/shard_map/ppermute | solution.py:48
  52.3 7.1 %collective-permute-start.7 = (bf16[112,1152]{1,0:T(8,128)(2,1)S(1)}, bf16[112,1152]{1,0:T(8,128)(2,1)S(1)}, u32[]{:S(2)}, u32[]{:S(2)}) collective-permute-start(bf16[112,1152]{1,0:T(8,128)(2,1)S(1)} %slice.397), channel_id=1, source_target_pairs={{0,1},{1,0},{2,3},{3,2},{4,5},{5,4},{6,7},{7,6},{8,9},{9,8},{10,11... | collective-permute-start | bytes 774152 | tf_op jit(solution)/shard_map/ppermute | solution.py:48
  60.0 11.6 %collective-permute-start.8 = (bf16[896,1152]{1,0:T(8,128)(2,1)}, bf16[896,1152]{1,0:T(8,128)(2,1)}, u32[]{:S(2)}, u32[]{:S(2)}) collective-permute-start(bf16[896,1152]{1,0:T(8,128)(2,1)} %constant_dynamic-update-slice_fusion), channel_id=1, source_target_pairs={{0,2},{2,0},{1,3},{3,1},{4,6},{6,4},{5,7},{7,5},{8,10},{10,8},{9,1... | collective-permute-start | bytes 6193160 | tf_op jit(solution)/shard_map/ppermute | solution.py:48
  70.8 56.8 %collective-permute-start.11 = (bf16[224,3072]{1,0:T(8,128)(2,1)}, bf16[224,3072]{1,0:T(8,128)(2,1)}, u32[]{:S(2)}, u32[]{:S(2)}) collective-permute-start(bf16[224,3072]{1,0:T(8,128)(2,1)} %all-gather.3.cloned.1.call-done.zw), channel_id=1, source_target_pairs={{0,4},{4,0},{1,5},{5,1},{2,6},{6,2},{3,7},{7,3},{8,12},{12,8},{9,1... | collective-permute-start | bytes 4128776 | tf_op jit(solution)/shard_map/ppermute | solution.py:48
  75.7 13.4 %collective-permute-start.10 = (bf16[256,1024]{1,0:T(8,128)(2,1)S(1)}, bf16[256,1024]{1,0:T(8,128)(2,1)S(1)}, u32[]{:S(2)}, u32[]{:S(2)}) collective-permute-start(bf16[256,1024]{1,0:T(8,128)(2,1)S(1)} %pad_maximum_fusion.11), channel_id=1, source_target_pairs={{0,1},{1,0},{2,3},{3,2},{4,5},{5,4},{6,7},{7,6},{8,9},{9,8},{10,11... | collective-permute-start | bytes 1572872 | tf_op jit(solution)/shard_map/ppermute | solution.py:48
  90.0 37.6 %collective-permute-start.12 = (bf16[224,3072]{1,0:T(8,128)(2,1)}, bf16[224,3072]{1,0:T(8,128)(2,1)}, u32[]{:S(2)}, u32[]{:S(2)}) collective-permute-start(bf16[224,3072]{1,0:T(8,128)(2,1)} %all-gather.3.cloned.1.call-done.zw), channel_id=1, source_target_pairs={{0,1},{1,0},{2,3},{3,2},{4,5},{5,4},{6,7},{7,6},{8,9},{9,8},{10,11... | collective-permute-start | bytes 4128776 | tf_op jit(solution)/shard_map/ppermute | solution.py:48
  106.2 46.7 %collective-permute-start.18 = (bf16[224,4224]{1,0:T(8,128)(2,1)}, bf16[224,4224]{1,0:T(8,128)(2,1)}, u32[]{:S(2)}, u32[]{:S(2)}) collective-permute-start(bf16[224,4224]{1,0:T(8,128)(2,1)} %all-gather.5.cloned.1.call-done.zw), channel_id=1, source_target_pairs={{0,4},{4,0},{1,5},{5,1},{2,6},{6,2},{3,7},{7,3},{8,12},{12,8},{9,1... | collective-permute-start | bytes 5677064 | tf_op jit(solution)/shard_map/ppermute | solution.py:48
  106.3 58.9 %collective-permute-start.19 = (bf16[224,4224]{1,0:T(8,128)(2,1)}, bf16[224,4224]{1,0:T(8,128)(2,1)}, u32[]{:S(2)}, u32[]{:S(2)}) collective-permute-start(bf16[224,4224]{1,0:T(8,128)(2,1)} %all-gather.5.cloned.1.call-done.zw), channel_id=1, source_target_pairs={{0,1},{1,0},{2,3},{3,2},{4,5},{5,4},{6,7},{7,6},{8,9},{9,8},{10,11... | collective-permute-start | bytes 5677064 | tf_op jit(solution)/shard_map/ppermute | solution.py:48
  121.0 49.7 %collective-permute-start.15 = (bf16[1024,896]{1,0:T(8,128)(2,1)S(1)}, bf16[1024,896]{1,0:T(8,128)(2,1)}, u32[]{:S(2)}, u32[]{:S(2)}) collective-permute-start(bf16[1024,896]{1,0:T(8,128)(2,1)S(1)} %fusion.12.cm), channel_id=1, source_target_pairs={{0,2},{2,0},{1,3},{3,1},{4,6},{6,4},{5,7},{7,5},{8,10},{10,8},{9,1... | collective-permute-start | bytes 5505032 | tf_op jit(solution)/shard_map/ppermute | solution.py:48
  149.7 29.1 %collective-permute-start.14 = (bf16[1024,896]{1,0:T(8,128)(2,1)S(1)}, bf16[1024,896]{1,0:T(8,128)(2,1)}, u32[]{:S(2)}, u32[]{:S(2)}) collective-permute-start(bf16[1024,896]{1,0:T(8,128)(2,1)S(1)} %multiply_convert_fusion.xm), channel_id=1, source_target_pairs={{0,2},{2,0},{1,3},{3,1},{4,6},{6,4},{5,7},{7,5},{8,10},{10,8},{9,1... | collective-permute-start | bytes 5505032 | tf_op jit(solution)/shard_map/ppermute | solution.py:48
  152.8 17.9 %collective-permute-start.16 = (bf16[112,3072]{1,0:T(8,128)(2,1)S(1)}, bf16[112,3072]{1,0:T(8,128)(2,1)S(1)}, u32[]{:S(2)}, u32[]{:S(2)}) collective-permute-start(bf16[112,3072]{1,0:T(8,128)(2,1)S(1)} %slice.347), channel_id=1, source_target_pairs={{0,4},{4,0},{1,5},{5,1},{2,6},{6,2},{3,7},{7,3},{8,12},{12,8},{9,1... | collective-permute-start | bytes 2064392 | tf_op jit(solution)/shard_map/ppermute | solution.py:48
  152.9 25.0 %collective-permute-start.17 = (bf16[112,3072]{1,0:T(8,128)(2,1)S(1)}, bf16[112,3072]{1,0:T(8,128)(2,1)S(1)}, u32[]{:S(2)}, u32[]{:S(2)}) collective-permute-start(bf16[112,3072]{1,0:T(8,128)(2,1)S(1)} %slice.348), channel_id=1, source_target_pairs={{0,1},{1,0},{2,3},{3,2},{4,5},{5,4},{6,7},{7,6},{8,9},{9,8},{10,11... | collective-permute-start | bytes 2064392 | tf_op jit(solution)/shard_map/ppermute | solution.py:48
  167.4 61.7 %collective-permute-start.20 = (bf16[112,4224]{1,0:T(8,128)(2,1)}, bf16[112,4224]{1,0:T(8,128)(2,1)}, u32[]{:S(2)}, u32[]{:S(2)}) collective-permute-start(bf16[112,4224]{1,0:T(8,128)(2,1)} %slice.349), channel_id=1, source_target_pairs={{0,4},{4,0},{1,5},{5,1},{2,6},{6,2},{3,7},{7,3},{8,12},{12,8},{9,1... | collective-permute-start | bytes 2838536 | tf_op jit(solution)/shard_map/ppermute | solution.py:48
  170.7 58.3 %collective-permute-start.21 = (bf16[112,4224]{1,0:T(8,128)(2,1)}, bf16[112,4224]{1,0:T(8,128)(2,1)}, u32[]{:S(2)}, u32[]{:S(2)}) collective-permute-start(bf16[112,4224]{1,0:T(8,128)(2,1)} %slice.350), channel_id=1, source_target_pairs={{0,1},{1,0},{2,3},{3,2},{4,5},{5,4},{6,7},{7,6},{8,9},{9,8},{10,11... | collective-permute-start | bytes 2838536 | tf_op jit(solution)/shard_map/ppermute | solution.py:48
  225.9 79.5 %collective-permute-start.25 = (bf16[112,3072]{1,0:T(8,128)(2,1)}, bf16[112,3072]{1,0:T(8,128)(2,1)}, u32[]{:S(2)}, u32[]{:S(2)}) collective-permute-start(bf16[112,3072]{1,0:T(8,128)(2,1)} %get-tuple-element.124), channel_id=1, source_target_pairs={{0,4},{4,0},{1,5},{5,1},{2,6},{6,2},{3,7},{7,3},{8,12},{12,8},{9,1... | collective-permute-start | bytes 2064392 | tf_op jit(solution)/shard_map/ppermute | solution.py:48
  228.0 77.8 %collective-permute-start.26 = (bf16[112,3072]{1,0:T(8,128)(2,1)}, bf16[112,3072]{1,0:T(8,128)(2,1)}, u32[]{:S(2)}, u32[]{:S(2)}) collective-permute-start(bf16[112,3072]{1,0:T(8,128)(2,1)} %get-tuple-element.125), channel_id=1, source_target_pairs={{0,1},{1,0},{2,3},{3,2},{4,5},{5,4},{6,7},{7,6},{8,9},{9,8},{10,11... | collective-permute-start | bytes 2064392 | tf_op jit(solution)/shard_map/ppermute | solution.py:48
  300.0 12.5 %collective-permute-start.23 = (bf16[1024,896]{1,0:T(8,128)(2,1)S(1)}, bf16[1024,896]{1,0:T(8,128)(2,1)S(1)}, u32[]{:S(2)}, u32[]{:S(2)}) collective-permute-start(bf16[1024,896]{1,0:T(8,128)(2,1)S(1)} %add_convert_fusion.4), channel_id=1, source_target_pairs={{0,2},{2,0},{1,3},{3,1},{4,6},{6,4},{5,7},{7,5},{8,10},{10,8},{9,1... | collective-permute-start | bytes 5505032 | tf_op jit(solution)/shard_map/ppermute | solution.py:48
  302.7 40.2 %collective-permute-start.29 = (bf16[112,4224]{1,0:T(8,128)(2,1)}, bf16[112,4224]{1,0:T(8,128)(2,1)}, u32[]{:S(2)}, u32[]{:S(2)}) collective-permute-start(bf16[112,4224]{1,0:T(8,128)(2,1)} %get-tuple-element.140), channel_id=1, source_target_pairs={{0,4},{4,0},{1,5},{5,1},{2,6},{6,2},{3,7},{7,3},{8,12},{12,8},{9,1... | collective-permute-start | bytes 2838536 | tf_op jit(solution)/shard_map/ppermute | solution.py:48
  303.6 39.2 %collective-permute-start.30 = (bf16[112,4224]{1,0:T(8,128)(2,1)}, bf16[112,4224]{1,0:T(8,128)(2,1)}, u32[]{:S(2)}, u32[]{:S(2)}) collective-permute-start(bf16[112,4224]{1,0:T(8,128)(2,1)} %get-tuple-element.141), channel_id=1, source_target_pairs={{0,1},{1,0},{2,3},{3,2},{4,5},{5,4},{6,7},{7,6},{8,9},{9,8},{10,11... | collective-permute-start | bytes 2838536 | tf_op jit(solution)/shard_map/ppermute | solution.py:48
  305.4 73.6 %collective-permute-start.22 = (bf16[1024,896]{1,0:T(8,128)(2,1)}, bf16[1024,896]{1,0:T(8,128)(2,1)}, u32[]{:S(2)}, u32[]{:S(2)}) collective-permute-start(bf16[1024,896]{1,0:T(8,128)(2,1)} %add_convert_fusion.6), channel_id=1, source_target_pairs={{0,2},{2,0},{1,3},{3,1},{4,6},{6,4},{5,7},{7,5},{8,10},{10,8},{9,1... | collective-permute-start | bytes 5505032 | tf_op jit(solution)/shard_map/ppermute | solution.py:48
  308.4 75.9 %collective-permute-start.28 = (bf16[224,3072]{1,0:T(8,128)(2,1)}, bf16[224,3072]{1,0:T(8,128)(2,1)}, u32[]{:S(2)}, u32[]{:S(2)}) collective-permute-start(bf16[224,3072]{1,0:T(8,128)(2,1)} %add_convert_fusion.8), channel_id=1, source_target_pairs={{0,1},{1,0},{2,3},{3,2},{4,5},{5,4},{6,7},{7,6},{8,9},{9,8},{10,11... | collective-permute-start | bytes 4128776 | tf_op jit(solution)/shard_map/ppermute | solution.py:48
  312.5 71.9 %collective-permute-start.27 = (bf16[224,3072]{1,0:T(8,128)(2,1)}, bf16[224,3072]{1,0:T(8,128)(2,1)}, u32[]{:S(2)}, u32[]{:S(2)}) collective-permute-start(bf16[224,3072]{1,0:T(8,128)(2,1)} %add_convert_fusion.9), channel_id=1, source_target_pairs={{0,4},{4,0},{1,5},{5,1},{2,6},{6,2},{3,7},{7,3},{8,12},{12,8},{9,1... | collective-permute-start | bytes 4128776 | tf_op jit(solution)/shard_map/ppermute | solution.py:48
  345.7 85.8 %collective-permute-start.32 = (bf16[224,4224]{1,0:T(8,128)(2,1)}, bf16[224,4224]{1,0:T(8,128)(2,1)}, u32[]{:S(2)}, u32[]{:S(2)}) collective-permute-start(bf16[224,4224]{1,0:T(8,128)(2,1)} %add_convert_fusion.1), channel_id=1, source_target_pairs={{0,1},{1,0},{2,3},{3,2},{4,5},{5,4},{6,7},{7,6},{8,9},{9,8},{10,11... | collective-permute-start | bytes 5677064 | tf_op jit(solution)/shard_map/ppermute | solution.py:48
  366.2 65.4 %collective-permute-start.31 = (bf16[224,4224]{1,0:T(8,128)(2,1)}, bf16[224,4224]{1,0:T(8,128)(2,1)}, u32[]{:S(2)}, u32[]{:S(2)}) collective-permute-start(bf16[224,4224]{1,0:T(8,128)(2,1)} %add_convert_fusion.2), channel_id=1, source_target_pairs={{0,4},{4,0},{1,5},{5,1},{2,6},{6,2},{3,7},{7,3},{8,12},{12,8},{9,1... | collective-permute-start | bytes 5677064 | tf_op jit(solution)/shard_map/ppermute | solution.py:48
  379.0 50.1 %collective-permute-start.24 = (bf16[128,1024]{1,0:T(8,128)(2,1)S(1)}, bf16[128,1024]{1,0:T(8,128)(2,1)S(1)}, u32[]{:S(2)}, u32[]{:S(2)}) collective-permute-start(bf16[128,1024]{1,0:T(8,128)(2,1)S(1)} %copy-done.61), channel_id=1, source_target_pairs={{0,1},{1,0},{2,3},{3,2},{4,5},{5,4},{6,7},{7,6},{8,9},{9,8},{10,11... | collective-permute-start | bytes 786440 | tf_op jit(solution)/shard_map/ppermute | solution.py:48
  387.9 127.4 %reduce-scatter.7.cloned.1.call-start = ((), (), s32[]{:S(2)}) async-start(), calls=%async_computation.5 | async-start | bytes 2365440
  410.2 26.9 %collective-permute-start.33 = (bf16[128,1024]{1,0:T(8,128)(2,1)}, bf16[128,1024]{1,0:T(8,128)(2,1)}, u32[]{:S(2)}, u32[]{:S(2)}) collective-permute-start(bf16[128,1024]{1,0:T(8,128)(2,1)} %get-tuple-element.136), channel_id=1, source_target_pairs={{0,1},{1,0},{2,3},{3,2},{4,5},{5,4},{6,7},{7,6},{8,9},{9,8},{10,11... | collective-permute-start | bytes 786440 | tf_op jit(solution)/shard_map/ppermute | solution.py:48
  440.4 13.0 %collective-permute-start.34 = (bf16[896,1024]{0,1:T(8,128)(2,1)S(1)}, bf16[896,1024]{0,1:T(8,128)(2,1)}, u32[]{:S(2)}, u32[]{:S(2)}) collective-permute-start(bf16[896,1024]{0,1:T(8,128)(2,1)S(1)} %pad_maximum_fusion.1), channel_id=1, source_target_pairs={{0,2},{2,0},{1,3},{3,1},{4,6},{6,4},{5,7},{7,5},{8,10},{10,8},{9,1... | collective-permute-start | bytes 5505032 | tf_op jit(solution)/shard_map/ppermute | solution.py:48
  455.9 8.1 %collective-permute-start.35 = (bf16[112,1152]{0,1:T(8,128)(2,1)S(1)}, bf16[112,1152]{0,1:T(8,128)(2,1)S(1)}, u32[]{:S(2)}, u32[]{:S(2)}) collective-permute-start(bf16[112,1152]{0,1:T(8,128)(2,1)S(1)} %get-tuple-element.200), channel_id=1, source_target_pairs={{0,1},{1,0},{2,3},{3,2},{4,5},{5,4},{6,7},{7,6},{8,9},{9,8},{10,11... | collective-permute-start | bytes 774152 | tf_op jit(solution)/shard_map/ppermute | solution.py:48
  456.0 8.1 %collective-permute-start.37 = (bf16[112,1152]{0,1:T(8,128)(2,1)S(1)}, bf16[112,1152]{0,1:T(8,128)(2,1)S(1)}, u32[]{:S(2)}, u32[]{:S(2)}) collective-permute-start(bf16[112,1152]{0,1:T(8,128)(2,1)S(1)} %get-tuple-element.201), channel_id=1, source_target_pairs={{0,4},{4,0},{1,5},{5,1},{2,6},{6,2},{3,7},{7,3},{8,12},{12,8},{9,1... | collective-permute-start | bytes 774152 | tf_op jit(solution)/shard_map/ppermute | solution.py:48
  465.4 12.0 %collective-permute-start.36 = (bf16[224,1152]{1,0:T(8,128)(2,1)S(1)}, bf16[224,1152]{1,0:T(8,128)(2,1)S(1)}, u32[]{:S(2)}, u32[]{:S(2)}) collective-permute-start(bf16[224,1152]{1,0:T(8,128)(2,1)S(1)} %copy.121), channel_id=1, source_target_pairs={{0,4},{4,0},{1,5},{5,1},{2,6},{6,2},{3,7},{7,3},{8,12},{12,8},{9,1... | collective-permute-start | bytes 1548296 | tf_op jit(solution)/shard_map/ppermute | solution.py:48
  467.1 11.7 %collective-permute-start.38 = (bf16[224,1152]{1,0:T(8,128)(2,1)S(1)}, bf16[224,1152]{1,0:T(8,128)(2,1)S(1)}, u32[]{:S(2)}, u32[]{:S(2)}) collective-permute-start(bf16[224,1152]{1,0:T(8,128)(2,1)S(1)} %copy.123), channel_id=1, source_target_pairs={{0,1},{1,0},{2,3},{3,2},{4,5},{5,4},{6,7},{7,6},{8,9},{9,8},{10,11... | collective-permute-start | bytes 1548296 | tf_op jit(solution)/shard_map/ppermute | solution.py:48
  480.9 9.4 %collective-permute-start.39 = (bf16[56,1152]{0,1:T(8,128)(2,1)S(1)}, bf16[56,1152]{0,1:T(8,128)(2,1)S(1)}, u32[]{:S(2)}, u32[]{:S(2)}) collective-permute-start(bf16[56,1152]{0,1:T(8,128)(2,1)S(1)} %get-tuple-element.212), channel_id=1, source_target_pairs={{0,8},{8,0},{16,24},{24,16},{1,9},{9,1},{17,25},{25,17},{2,10},{10... | collective-permute-start | bytes 387080 | tf_op jit(solution)/shard_map/ppermute | solution.py:119
  481.5 22.0 %collective-permute-start.40 = (bf16[56,1152]{0,1:T(8,128)(2,1)S(1)}, bf16[56,1152]{0,1:T(8,128)(2,1)S(1)}, u32[]{:S(2)}, u32[]{:S(2)}) collective-permute-start(bf16[56,1152]{0,1:T(8,128)(2,1)S(1)} %get-tuple-element.214), channel_id=1, source_target_pairs={{0,16},{8,24},{16,0},{24,8},{1,17},{9,25},{17,1},{25,9},{2,18},{10... | collective-permute-start | bytes 387080 | tf_op jit(solution)/shard_map/ppermute | solution.py:119
  486.1 23.7 %collective-permute-start.41 = (bf16[56,1152]{0,1:T(8,128)(2,1)S(1)}, bf16[56,1152]{0,1:T(8,128)(2,1)S(1)}, u32[]{:S(2)}, u32[]{:S(2)}) collective-permute-start(bf16[56,1152]{0,1:T(8,128)(2,1)S(1)} %get-tuple-element.213), channel_id=1, source_target_pairs={{0,24},{8,16},{16,8},{24,0},{1,25},{9,17},{17,9},{25,1},{2,26},{10... | collective-permute-start | bytes 387080 | tf_op jit(solution)/shard_map/ppermute | solution.py:119
  487.1 33.2 %collective-permute-start.43 = (f32[28,3072]{1,0:T(8,128)S(1)}, f32[28,3072]{1,0:T(8,128)S(1)}, u32[]{:S(2)}, u32[]{:S(2)}) collective-permute-start(f32[28,3072]{1,0:T(8,128)S(1)} %get-tuple-element.204), channel_id=1, source_target_pairs={{0,2},{2,0},{1,3},{3,1},{4,6},{6,4},{5,7},{7,5},{8,10},{10,8},{9,1... | collective-permute-start | bytes 1032200 | tf_op jit(solution)/shard_map/ppermute | solution.py:48
  510.5 4.5 collective-permute-start.42
  517.4 2.9 collective-permute-start.44
  (67 other events, 979.6 us)
Sparse Core Ops, SparseCore 0:
  24.6 35.4 all-gather.2
  62.3 40.8 all-gather.4
  388.1 34.9 reduce-scatter.4
  435.7 44.8 reduce-scatter.6
